TPU v7x, 256 devices: a whole 4x4x8 slice. The times are simulated.
256 devices in a mesh: edge: 64 (over y, z, core), rep: 4 (over x).
Axes of the slice: x: 4, y: 4, z: 8, core: 2. Of those that a mesh axis runs over, the one named last changes fastest.
Arguments:
- entities: float32 [4, 65536, 400], P('rep', 'edge'), may hold values from -3 to 3
- ent_accum: float32 [4, 65536], P('rep', 'edge'), may hold values from 0.01 to 0.1
- relations: float32 [1000, 400], replicated, may hold values from -3 to 3
- rel_accum: float32 [1000], replicated, may hold values from 1 to 10
- heads: int32 [4, 2, 8192], P('rep', None, 'edge'), may hold values from 0 to 65535, as said below
- tails: int32 [4, 2, 8192], P('rep', None, 'edge'), may hold values from 0 to 65535, as said below
- negatives: int32 [4, 2, 65536], P('rep', None, 'edge'), may hold values from 0 to 65535, as said below
- rel_ids: int32 [4, 2, 8192], P('rep', None, 'edge'), may hold values from 0 to 999
Outputs:
- new_entities: float32 [4, 65536, 400], P('rep', 'edge')
- new_ent_accum: float32 [4, 65536], P('rep', 'edge')
- new_relations: float32 [1000, 400], replicated
- new_rel_accum: float32 [1000], replicated
Inputs may be any that keep to these rules, and one draw needn't show every extreme that they name: Row i of a bucket belongs to owner i // 1024. In each bucket, step and block, at most 40 of the block's 1280 requests (heads, tails, negatives together) name rows of one owner, and in every bucket and step one owner is named exactly 40 times by every block. `tails`: drawn together with heads under the same bound. `negatives`: drawn together with heads under the same bound.
All inputs are finite; a program needn't handle non-finite values.
Results may differ from a plain program's by a relative error of at most 0.0042.
Values may be sent and summed in bfloat16 or wider, within the bound.
No kernel may reach another device: no remote copies, remote signals or barrier semaphores. Data moves between devices by JAX's collectives and lax.ppermute only.
A program may use at most 64 MiB of HBM per device.

v0:
```python
import jax
import jax.numpy as jnp
from jax import lax
from jax.sharding import PartitionSpec as P

entity_rate = 0.1
relation_rate = 0.1


def complex_parts(rows):
    half = rows.shape[-1] // 2
    return (rows[:, :half], rows[:, half:])


def span_grads(head_entity_rows, tail_rows, negative_rows, relation_rows):
    negative_count = negative_rows.shape[0]
    head_full = head_entity_rows.astype(jnp.float32)
    tail_full = tail_rows.astype(jnp.float32)
    head_re, head_im = complex_parts(head_full)
    tail_re, tail_im = complex_parts(tail_full)
    rel_re, rel_im = complex_parts(relation_rows)
    query_tail = jnp.concatenate(
        [head_re * rel_re - head_im * rel_im, head_re * rel_im + head_im * rel_re], axis=1
    )
    query_head = jnp.concatenate(
        [rel_re * tail_re + rel_im * tail_im, rel_re * tail_im - rel_im * tail_re], axis=1
    )
    positive_score = jnp.sum(query_tail * tail_full, axis=1)
    tail_query16 = query_tail.astype(jnp.bfloat16)
    head_query16 = query_head.astype(jnp.bfloat16)
    contract_last = (((1,), (1,)), ((), ()))
    scores_tail = lax.dot_general(
        tail_query16, negative_rows, contract_last, preferred_element_type=jnp.float32
    )
    scores_head = lax.dot_general(
        head_query16, negative_rows, contract_last, preferred_element_type=jnp.float32
    )
    weight_tail = (jax.nn.sigmoid(scores_tail) / negative_count).astype(jnp.bfloat16)
    weight_head = (jax.nn.sigmoid(scores_head) / negative_count).astype(jnp.bfloat16)
    positive_weight = -jax.nn.sigmoid(-positive_score)[:, None]
    grad_tail_query = positive_weight * tail_full + jnp.dot(
        weight_tail, negative_rows, preferred_element_type=jnp.float32
    )
    grad_head_query = jnp.dot(weight_head, negative_rows, preferred_element_type=jnp.float32)
    contract_first = (((0,), (0,)), ((), ()))
    grad_negative = lax.dot_general(
        weight_tail, tail_query16, contract_first, preferred_element_type=jnp.float32
    )
    grad_negative = grad_negative + lax.dot_general(
        weight_head, head_query16, contract_first, preferred_element_type=jnp.float32
    )
    pull_re, pull_im = complex_parts(grad_tail_query)
    push_re, push_im = complex_parts(grad_head_query)
    grad_head = jnp.concatenate(
        [pull_re * rel_re + pull_im * rel_im, pull_im * rel_re - pull_re * rel_im], axis=1
    )
    grad_tail = positive_weight * query_tail + jnp.concatenate(
        [push_re * rel_re - push_im * rel_im, push_re * rel_im + push_im * rel_re], axis=1
    )
    grad_relation = jnp.concatenate(
        [
            pull_re * head_re + pull_im * head_im + push_re * tail_re + push_im * tail_im,
            pull_im * head_re - pull_re * head_im + push_re * tail_im - push_im * tail_re,
        ],
        axis=1,
    )
    return (jnp.concatenate([grad_head, grad_tail, grad_negative], axis=0), grad_relation)


def shards(entities, ent_accum, relations, rel_accum, heads, tails, negatives, rel_ids):
    owners_count = lax.axis_size("edge")
    rows_dev = entities.shape[1]
    width = entities.shape[2]
    span_size = heads.shape[2]
    request_count = 2 * span_size + negatives.shape[2]
    capacity = 2 * request_count // owners_count
    table = entities[0]
    accum = ent_accum[0]
    rel_table = relations
    rel_state = rel_accum
    for step_index in range(heads.shape[1]):
        requests = jnp.concatenate(
            [heads[0, step_index], tails[0, step_index], negatives[0, step_index]]
        )
        owner_ids = requests // rows_dev
        local_rows = requests % rows_dev
        order = jnp.argsort(owner_ids, stable=True)
        sorted_owner = owner_ids[order]
        counts = jnp.sum(
            (owner_ids[:, None] == jnp.arange(owners_count, dtype=jnp.int32)[None, :]).astype(
                jnp.int32
            ),
            axis=0,
        )
        starts = jnp.cumsum(counts) - counts
        ranks = jnp.arange(request_count, dtype=jnp.int32) - starts[sorted_owner]
        slot_of = jnp.zeros((request_count,), jnp.int32).at[order].set(ranks)
        flat_slot = owner_ids * capacity + slot_of
        send_rows = jnp.zeros((owners_count * capacity,), jnp.int32).at[flat_slot].set(local_rows)
        send_rows = send_rows.reshape(owners_count, capacity)
        received = lax.all_to_all(send_rows, "edge", split_axis=0, concat_axis=0, tiled=True)
        replies = lax.all_to_all(
            table[received].astype(jnp.bfloat16), "edge", split_axis=0, concat_axis=0, tiled=True
        )
        fetched = replies.reshape(owners_count * capacity, width)[flat_slot]
        relation_ids = rel_ids[0, step_index]
        request_grads, relation_grads = span_grads(
            fetched[:span_size],
            fetched[span_size : 2 * span_size],
            fetched[2 * span_size :],
            rel_table[relation_ids],
        )
        send_grads = (
            jnp.zeros((owners_count * capacity, width), jnp.bfloat16)
            .at[flat_slot]
            .set(request_grads.astype(jnp.bfloat16))
        )
        send_grads = send_grads.reshape(owners_count, capacity, width)
        returned = lax.all_to_all(send_grads, "edge", split_axis=0, concat_axis=0, tiled=True)
        entity_grad = jax.ops.segment_sum(
            returned.reshape(owners_count * capacity, width).astype(jnp.float32),
            received.reshape(owners_count * capacity),
            num_segments=rows_dev,
        )
        relation_local = jax.ops.segment_sum(
            relation_grads, relation_ids, num_segments=rel_table.shape[0]
        )
        relation_total = lax.psum(relation_local, ("edge", "rep"))
        accum = accum + jnp.mean(entity_grad * entity_grad, axis=1)
        table = table - entity_rate * entity_grad / jnp.sqrt(accum)[:, None]
        rel_state = rel_state + jnp.mean(relation_total * relation_total, axis=1)
        rel_table = rel_table - relation_rate * relation_total / jnp.sqrt(rel_state)[:, None]
    return (table[None], accum[None], rel_table, rel_state)


def solution(mesh):
    in_specs = (
        P("rep", "edge", None),
        P("rep", "edge"),
        P(),
        P(),
        P("rep", None, "edge"),
        P("rep", None, "edge"),
        P("rep", None, "edge"),
        P("rep", None, "edge"),
    )
    out_specs = (P("rep", "edge", None), P("rep", "edge"), P(), P())
    return jax.shard_map(shards, mesh=mesh, in_specs=in_specs, out_specs=out_specs, check_vma=False)
```

profile of v0, /device:TPU:1, one launch (start us, length us, event | category | flops | bytes accessed | tf_op | source)
XLA Modules:
  0.0 972.3 jit_solution(9696131635299519426)
XLA Ops:
  12.8 5.0 sort.31
  17.9 7.1 gather_fusion
  25.0 4.5 fusion.62
  30.4 35.7 %select_subtract_fusion.1 = s32[1280]{0:T(1024)S(1)} fusion(pred[1280]{0:T(1024)(128)(4,1)S(1)} %get-tuple-element.137, pred[1280]{0:T(1024)(128)(4,1)S(1)} %get-tuple-element.136, pred[1280]{0:T(1024)(128)(4,1)S(1)} %get-tuple-element.135, pred[1280]{0:T(1024)(128)(4,1)S(1)} %get-tuple-element.134, pred[1280]{0:T(1024)(128)(4,1)S(1)} %get-tuple-element.133, ...), kind=kLoop, calls=%fused_computation.273 | loop fusion | flops 74240 | bytes 83428 | tf_op jit(solution)/shard_map/sub | solution.py:96
  66.1 5.2 scatter_custom_fusion
  71.4 5.3 scatter_custom_fusion.1
  77.3 13.2 %all-to-all-start = ((s32[64,1,40]{2,1,0:T(1,128)}), s32[64,1,40]{2,1,0:T(1,128)S(1)}, u32[]{:S(2)}, u32[]{:S(2)}) async-start(s32[64,1,40]{2,1,0:T(1,128)} %bitcast.69), calls=%async_computation | async-start | bytes 65536 | tf_op jit(solution)/shard_map/all_to_all | solution.py:101
  92.4 7.3 all-to-all-done
  99.8 7.1 gather_fusion.1
  106.9 5.5 all-to-all-start.1
  112.4 5.0 sort.32
  117.4 7.1 gather_fusion.4
  126.4 4.3 fusion.63
  133.1 35.9 %select_subtract_fusion = s32[1280]{0:T(1024)S(1)} fusion(pred[1280]{0:T(1024)(128)(4,1)S(1)} %get-tuple-element.80, pred[1280]{0:T(1024)(128)(4,1)S(1)} %get-tuple-element.79, pred[1280]{0:T(1024)(128)(4,1)S(1)} %get-tuple-element.78, pred[1280]{0:T(1024)(128)(4,1)S(1)} %get-tuple-element.77, pred[1280]{0:T(1024)(128)(4,1)S(1)} %get-tuple-element.76, ...), kind=kLoop, calls=%fused_computation.272 | loop fusion | flops 74240 | bytes 83428 | tf_op jit(solution)/shard_map/sub | solution.py:96
  169.0 5.2 scatter_custom_fusion.4
  174.2 5.3 scatter_custom_fusion.5
  186.4 11.0 %all-to-all-start.3 = ((s32[64,1,40]{2,1,0:T(1,128)}), s32[64,1,40]{2,1,0:T(1,128)}, u32[]{:S(2)}, u32[]{:S(2)}) async-start(s32[64,1,40]{2,1,0:T(1,128)} %bitcast.146), calls=%async_computation.3 | async-start | bytes 65536 | tf_op jit(solution)/shard_map/all_to_all | solution.py:101
  197.4 4.7 gather_fusion.2
  207.3 10.0 %scatter_custom_fusion.2 = bf16[2560,400]{1,0:T(8,128)(2,1)} fusion(s32[1280]{0:T(1024)} %copy-done.14, bf16[1280,400]{1,0:T(8,128)(2,1)S(1)} %copy.75, bf16[]{:T(256)} %constant.79.clone.1), kind=kCustom, calls=%fused_computation.34 | custom fusion | bytes 2048512 | tf_op jit(solution)/shard_map/scatter | solution.py:116
  217.3 10.5 %all-to-all-start.2 = ((bf16[64,40,400]{2,1,0:T(8,128)(2,1)}), bf16[64,40,400]{2,1,0:T(8,128)(2,1)S(1)}, u32[]{:S(2)}, u32[]{:S(2)}) async-start(bf16[64,40,400]{2,1,0:T(8,128)(2,1)} %bitcast.75), calls=%async_computation.2 | async-start | bytes 5242880 | tf_op jit(solution)/shard_map/all_to_all | solution.py:119
  230.0 60.1 %all-to-all-done.2 = bf16[64,40,400]{2,1,0:T(8,128)(2,1)S(1)} async-done(((bf16[64,40,400]{2,1,0:T(8,128)(2,1)}), bf16[64,40,400]{2,1,0:T(8,128)(2,1)S(1)}, u32[]{:S(2)}, u32[]{:S(2)}) %all-to-all-start.2) | async-done | bytes 2048032 | tf_op jit(solution)/shard_map/all_to_all | solution.py:119
  291.5 17.1 %scatter_custom_fusion.3 = f32[1024,400]{1,0:T(8,128)S(1)} fusion(s32[2560]{0:T(1024)S(1)} %reshape.707, bf16[2560,400]{1,0:T(8,128)(2,1)} %bitcast.194, f32[]{:T(128)} %constant.68.clone.1), kind=kCustom, calls=%fused_computation.20 | custom fusion | flops 2048000 | bytes 3686404 | tf_op jit(solution)/shard_map/scatter-add | solution.py:120
  313.0 7.1 gather_fusion.5
  320.1 7.0 all-to-all-start.4
  330.2 277.2 %all-reduce.3.cloned.1.call-done = f32[1000,400]{1,0:T(8,128)} async-done(((f32[1000,400]{1,0:T(8,128)}), f32[1000,400]{1,0:T(8,128)}) %all-reduce.3.cloned.1.call-update) | async-done | bytes 1600016 | tf_op jit(solution)/shard_map/psum | solution.py:128
  609.5 3.3 divide_subtract_fusion.2
  615.6 6.9 gather_fusion.6
  631.6 10.6 %scatter_custom_fusion.7 = bf16[2560,400]{1,0:T(8,128)(2,1)} fusion(s32[1280]{0:T(1024)S(1)} %copy-done.16, bf16[1280,400]{1,0:T(8,128)(2,1)} %copy.84, bf16[]{:T(256)} %constant.79.clone.1), kind=kCustom, calls=%fused_computation.32 | custom fusion | bytes 2048512 | tf_op jit(solution)/shard_map/scatter | solution.py:116
  642.1 10.7 %all-to-all-start.5 = ((bf16[64,40,400]{2,1,0:T(8,128)(2,1)}), bf16[64,40,400]{2,1,0:T(8,128)(2,1)}, u32[]{:S(2)}, u32[]{:S(2)}) async-start(bf16[64,40,400]{2,1,0:T(8,128)(2,1)} %bitcast.193), calls=%async_computation.5 | async-start | bytes 5242880 | tf_op jit(solution)/shard_map/all_to_all | solution.py:119
  657.5 273.8 %all-reduce.5.cloned.1.call-done = f32[1000,400]{1,0:T(8,128)} async-done(((f32[1000,400]{1,0:T(8,128)}), f32[1000,400]{1,0:T(8,128)}) %all-reduce.5.cloned.1.call-update) | async-done | bytes 1600016 | tf_op jit(solution)/shard_map/psum | solution.py:128
  933.8 3.3 divide_subtract_fusion.1
  939.9 17.8 %scatter_custom_fusion.8 = f32[1024,400]{1,0:T(8,128)} fusion(s32[2560]{0:T(1024)S(1)} %reshape.747, bf16[2560,400]{1,0:T(8,128)(2,1)} %bitcast.160, f32[]{:T(128)} %constant.68.clone.1), kind=kCustom, calls=%fused_computation.18 | custom fusion | flops 2048000 | bytes 3686404 | tf_op jit(solution)/shard_map/scatter-add | solution.py:120
  (166 shorter events, 67.5 us)
Async XLA Ops:
  71.4 115.0 %copy-start.14 = (s32[1280]{0:T(1024)}, s32[1280]{0:T(1024)S(1)}, u32[]{:S(2)}) copy-start(s32[1280]{0:T(1024)S(1)} %compare_select_fusion.6) | copy-start | bytes 15364
  77.3 22.4 %all-to-all-start = ((s32[64,1,40]{2,1,0:T(1,128)}), s32[64,1,40]{2,1,0:T(1,128)S(1)}, u32[]{:S(2)}, u32[]{:S(2)}) async-start(s32[64,1,40]{2,1,0:T(1,128)} %bitcast.69), calls=%async_computation | async-start | bytes 65536 | tf_op jit(solution)/shard_map/all_to_all | solution.py:101
  92.3 14.5 %copy-start = (f32[1,1024,400]{2,1,0:T(8,128)}, f32[1,1024,400]{2,1,0:T(8,128)S(1)}, u32[]{:S(2)}) copy-start(f32[1,1024,400]{2,1,0:T(8,128)S(1)} %copy.67) | copy-start | bytes 4915204
  99.7 7.2 copy-start.11
  106.9 79.5 %all-to-all-start.1 = ((bf16[64,40,400]{2,1,0:T(8,128)(2,1)}), bf16[64,40,400]{2,1,0:T(8,128)(2,1)S(1)}, u32[]{:S(2)}, u32[]{:S(2)}) async-start(bf16[64,40,400]{2,1,0:T(8,128)(2,1)} %bitcast.195), calls=%async_computation.1 | async-start | bytes 5242880 | tf_op jit(solution)/shard_map/all_to_all | solution.py:102
  133.1 50.0 %copy-start.18 = (s32[1,2,128]{2,1,0:T(2,128)S(1)}, s32[1,2,128]{2,1,0:T(2,128)}, u32[]{:S(2)}) copy-start(s32[1,2,128]{2,1,0:T(2,128)} %param.15) | copy-start | bytes 3076
  174.2 9.3 copy-start.15
  186.3 17.2 %copy-start.9 = (f32[128,200]{0,1:T(8,128)}, f32[128,200]{0,1:T(8,128)S(1)}, u32[]{:S(2)}) copy-start(f32[128,200]{0,1:T(8,128)S(1)} %copy.89) | copy-start | bytes 307204
  186.4 30.9 %all-to-all-start.3 = ((s32[64,1,40]{2,1,0:T(1,128)}), s32[64,1,40]{2,1,0:T(1,128)}, u32[]{:S(2)}, u32[]{:S(2)}) async-start(s32[64,1,40]{2,1,0:T(1,128)} %bitcast.146), calls=%async_computation.3 | async-start | bytes 65536 | tf_op jit(solution)/shard_map/all_to_all | solution.py:101
  202.1 1.6 copy-start.7
  205.6 0.9 copy-start.10
  217.3 11.8 %copy-start.12 = (s32[64,1,40]{2,1,0:T(1,128)S(1)}, s32[64,1,40]{2,1,0:T(1,128)}, u32[]{:S(2)}) copy-start(s32[64,1,40]{2,1,0:T(1,128)} %copy-done.11) | copy-start | bytes 30724
  217.3 72.7 %all-to-all-start.2 = ((bf16[64,40,400]{2,1,0:T(8,128)(2,1)}), bf16[64,40,400]{2,1,0:T(8,128)(2,1)S(1)}, u32[]{:S(2)}, u32[]{:S(2)}) async-start(bf16[64,40,400]{2,1,0:T(8,128)(2,1)} %bitcast.75), calls=%async_computation.2 | async-start | bytes 5242880 | tf_op jit(solution)/shard_map/all_to_all | solution.py:119
  290.0 1.5 copy-start.6
  308.6 1.4 copy-start.3
  308.6 1.3 copy-start.13
  308.6 2.4 copy-start.1
  320.1 295.5 %all-to-all-start.4 = ((bf16[64,40,400]{2,1,0:T(8,128)(2,1)}), bf16[64,40,400]{2,1,0:T(8,128)(2,1)}, u32[]{:S(2)}, u32[]{:S(2)}) async-start(bf16[64,40,400]{2,1,0:T(8,128)(2,1)} %bitcast.196), calls=%async_computation.4 | async-start | bytes 5242880 | tf_op jit(solution)/shard_map/all_to_all | solution.py:102
  327.1 280.3 %all-reduce.3.cloned.1.call-start = ((), (), s32[]{:S(2)}) async-start(), calls=%async_computation.6 | async-start | bytes 4096000 | tf_op jit(solution)/shard_map/psum | solution.py:128
  327.4 2.8 copy-start.19
  327.4 2.8 copy-start.16
  330.1 279.2 %copy-start.17 = (f32[1000]{0:T(1024)S(1)}, f32[1000]{0:T(1024)}, u32[]{:S(2)}) copy-start(f32[1000]{0:T(1024)} %param.11) | copy-start | bytes 12004
  607.3 2.2 copy-start.4
  623.8 2.0 copy-start.8
  642.1 297.8 %all-to-all-start.5 = ((bf16[64,40,400]{2,1,0:T(8,128)(2,1)}), bf16[64,40,400]{2,1,0:T(8,128)(2,1)}, u32[]{:S(2)}, u32[]{:S(2)}) async-start(bf16[64,40,400]{2,1,0:T(8,128)(2,1)} %bitcast.193), calls=%async_computation.5 | async-start | bytes 5242880 | tf_op jit(solution)/shard_map/all_to_all | solution.py:119
  652.9 278.4 %all-reduce.5.cloned.1.call-start = ((), (), s32[]{:S(2)}) async-start(), calls=%async_computation.7 | async-start | bytes 4096000 | tf_op jit(solution)/shard_map/psum | solution.py:128
  931.3 2.5 copy-start.5
  957.7 2.2 copy-start.2
Sparse Core Ops, SparseCore 0:
  333.3 273.9 all-reduce.2
  659.1 272.1 all-reduce.4
where the time goes:
time: 983 us; the launch traced here: 972 us
  waiting for transfers between devices  618 us (63%)
  other arithmetic  156 us (16%)
  local copies, waits for them, and re-layouts  117 us (12%)
  starting transfers between devices  57.8 us (6%)
  between operations  15.3 us (2%)
    psum x2, waiting for transfers between devices, shards(): relation_total = lax.psum(relation_local, ('edge', 'rep'))  551 us
    sub x2, other arithmetic, shards(): ranks = jnp.arange(request_count, dtype=jnp.int32) - starts[sorted_owner]  71.6 us
    all_to_all x2, waiting for transfers between devices, shards(): lax.all_to_all(send_grads, 'edge', split_axis=0, concat_axis=0, tiled=True)  60.1 us
    scatter-add x2, other arithmetic, shards(): jax.ops.segment_sum(returned.reshape(owners_count * capacity, width).asty...  34.9 us
    all_to_all x2, starting transfers between devices, shards(): lax.all_to_all(send_rows, 'edge', split_axis=0, concat_axis=0, tiled=True)  24.1 us
    all_to_all x2, starting transfers between devices, shards(): lax.all_to_all(send_grads, 'edge', split_axis=0, concat_axis=0, tiled=True)  21.2 us
    scatter x2, local copies, waits for them, and re-layouts, shards(): send_grads = jnp.zeros((owners_count * capacity, width), jnp.bfloat16).at...  20.5 us
  transfers between devices with their start and end apart: 8, of which 4 were waited for; matrix products, arithmetic and copies ran while one was open for 12% of the time, Pallas kernels for 0%

commit v1 on v0

v1 whole, which is shorter than its diff:
```python
import jax
import jax.numpy as jnp
from jax import lax
from jax.experimental import pallas as pl
from jax.experimental.pallas import tpu as pltpu
from jax.sharding import PartitionSpec as P

F32, BF16, I32 = jnp.float32, jnp.bfloat16, jnp.int32
RATE = 0.1
OWN = 64
CAP = 40
SLOTS = OWN * CAP
WIDTH = 400
HALF = 200
BODY = 384
REL = 1024


def iota(shape, dim):
    return lax.broadcasted_iota(I32, shape, dim)


def one_hot(hit):
    return jnp.where(hit, 1.0, 0.0).astype(BF16)


def dot(a, b, dims=((1,), (0,))):
    return lax.dot_general(a, b, (dims, ((), ())), preferred_element_type=F32)


def fold_tail(x):
    x = x + pltpu.roll(x, 64, 1)
    x = x + pltpu.roll(x, 32, 1)
    return x + pltpu.roll(x, 16, 1)


def spread_tail(x16):
    rows = x16.shape[0]
    return fold_tail(jnp.concatenate([x16, jnp.zeros((rows, 112), F32)], axis=1))


def to_wide(x):
    return jnp.concatenate([x[:, :BODY], spread_tail(x[:, BODY:])], axis=1)


def to_narrow(x):
    return jnp.concatenate([x[:, :BODY], fold_tail(x[:, BODY:])[:, :16]], axis=1)


def pack(rows):
    group = iota((8, 128), 1) // 16
    tail = jnp.zeros((8, 128), F32)
    for i in range(5):
        tail = jnp.where(group == i, rows[8 * i : 8 * i + 8, BODY:], tail)
    return jnp.concatenate([rows[:, :128], rows[:, 128:256], rows[:, 256:384], tail], axis=0)


def unpack(block):
    group = iota((8, 128), 1) // 16
    tail = jnp.concatenate([jnp.where(group == i, block[120:], 0.0) for i in range(5)], axis=0)
    return jnp.concatenate([block[:40], block[40:80], block[80:120], tail], axis=1)


def unpack_all(wire_ref, rows_ref):
    def pair(e, _):
        two = [unpack(wire_ref[2 * e + k].astype(F32)) for k in range(2)]
        at = pl.multiple_of(e * 2 * CAP, 2 * CAP)
        rows_ref[pl.ds(at, 2 * CAP), :] = jnp.concatenate(two, axis=0).astype(BF16)
        return 0

    lax.fori_loop(0, OWN // 2, pair, 0)


def lane_to_column(row):
    return jnp.transpose(jnp.broadcast_to(row, (128, 128)))


def prepare(heads_ref, tails_ref, negatives_ref, send_ref, negative_ref, slots_ref):
    count = 2 * heads_ref.shape[2] + negatives_ref.shape[2]
    steps = heads_ref.shape[1]
    before = one_hot(iota((128, 128), 0) < iota((128, 128), 1))
    send = jnp.zeros((OWN, 128), F32)
    negative = jnp.zeros((OWN, 128), F32)
    for s in range(steps):
        requests = jnp.concatenate(
            [heads_ref[0, s : s + 1, :], tails_ref[0, s : s + 1, :], negatives_ref[0, s : s + 1, :]], axis=1
        )
        owner = lax.shift_right_logical(requests, 10)
        local = requests & 1023
        at_owner = jnp.where(iota((OWN, count), 0) == owner, 1.0, 0.0)
        seen = jnp.zeros((OWN, 1), F32)
        ranks = []
        for j in range(count // 128):
            part = at_owner[:, 128 * j : 128 * j + 128]
            earlier = dot(part.astype(BF16), before) + seen
            ranks.append(jnp.sum(part * earlier, axis=0, keepdims=True))
            seen = seen + jnp.sum(part, axis=1, keepdims=True)
        rank = jnp.concatenate(ranks, axis=1).astype(I32)
        at_rank = one_hot(iota((128, count), 0) == rank + CAP * s)
        high = (at_owner * lax.shift_right_logical(local, 5).astype(F32)).astype(BF16)
        low = (at_owner * (local & 31).astype(F32)).astype(BF16)
        last = ((1,), (1,))
        send = send + dot(high, at_rank, last) * 32.0 + dot(low, at_rank, last)
        chosen = jnp.where(iota((OWN, count), 1) >= 256, at_owner, 0.0).astype(BF16)
        negative = negative + dot(chosen, at_rank, last)
        slots_ref[s : s + 1, :] = (owner * CAP + rank)[:, :256]
    send_ref[...] = send.astype(I32)
    negative_ref[...] = negative


def gather_rows(named_ref, step, wide_ref, wire_ref):
    named = named_ref[...].astype(F32)
    named = jnp.transpose(jnp.concatenate([named, named], axis=0))
    named = named[CAP * step : CAP * step + CAP, :OWN].astype(I32)
    for g in range(OWN // 8):
        columns = jnp.concatenate([named[:, 8 * g + j : 8 * g + j + 1] for j in range(8)], axis=0)
        hit = one_hot(columns == iota((8 * CAP, 1024), 1))
        rows = dot(hit, wide_ref[...])
        for j in range(8):
            wire_ref[8 * g + j] = pack(rows[CAP * j : CAP * j + CAP]).astype(BF16)


def first_rows(table_ref, named_ref, wire_ref, wide_ref):
    wide_ref[...] = to_wide(table_ref[0]).astype(BF16)
    gather_rows(named_ref, 0, wide_ref, wire_ref)


def update(step, last, wire_in_ref, flat_ref, table_ref, accum_ref, named_ref, *rest):
    if last:
        new_table_ref, new_accum_ref, grads_ref = rest
    else:
        new_table_ref, new_accum_ref, wire_ref, grads_ref, wide_ref = rest
    unpack_all(wire_in_ref, grads_ref)
    for b in range(8):
        rows = slice(128 * b, 128 * b + 128)
        hit = one_hot(iota((128, SLOTS), 0) + 128 * b == flat_ref[step : step + 1, :])
        total = dot(hit, grads_ref[...])
        total = to_narrow(total)
        accum = lane_to_column(accum_ref[b : b + 1, :])
        accum = accum + jnp.sum(total * total, axis=1, keepdims=True) / WIDTH
        new_accum_ref[b : b + 1, :] = jnp.transpose(accum)[:1]
        new = table_ref[0, rows, :] - total * (RATE * lax.rsqrt(accum[:, :1]))
        new_table_ref[0, rows, :] = new
        if not last:
            wide_ref[rows, :] = to_wide(new).astype(BF16)
    if not last:
        gather_rows(named_ref, step + 1, wide_ref, wire_ref)


def complex_parts(x):
    return x[:, :HALF], x[:, HALF:]


def join(re, im):
    return jnp.concatenate([re, im], axis=1)


def split3(x):
    a = x.astype(BF16)
    x = x - a.astype(F32)
    b = x.astype(BF16)
    return a, b, (x - b.astype(F32)).astype(BF16)


def block(
    step, wire_in_ref, slots_ref, negative_ref, relations_ref, rel_ids_ref,
    wire_ref, relation_grad_ref, rows_ref, weights_ref,
):
    edges, parts = 128, 4
    part = SLOTS // parts
    per = OWN // parts
    unpack_all(wire_in_ref, rows_ref)
    slots = slots_ref[step : step + 1, :]
    slots_column = jnp.concatenate(
        [lane_to_column(slots[:, 128 * k : 128 * k + 128].astype(F32))[:, :1] for k in range(2)], axis=0
    ).astype(I32)
    fetched = jnp.zeros((2 * edges, 512), F32)
    for g in range(parts):
        hit = one_hot(slots_column == iota((2 * edges, part), 1) + part * g)
        fetched = fetched + dot(hit, rows_ref[part * g : part * g + part, :])
    fetched = to_narrow(fetched)
    head, tail = fetched[:edges], fetched[edges:]
    rel_ids = rel_ids_ref[0, step : step + 1, :]
    rel_column = lane_to_column(rel_ids.astype(F32))[:, :1].astype(I32)
    rel_hit = one_hot(rel_column == iota((edges, REL), 1))
    relation = jnp.zeros((edges, WIDTH), F32)
    for piece in reversed(split3(relations_ref[...])):
        relation = relation + dot(rel_hit, piece)

    head_re, head_im = complex_parts(head)
    tail_re, tail_im = complex_parts(tail)
    rel_re, rel_im = complex_parts(relation)
    query_tail = join(head_re * rel_re - head_im * rel_im, head_re * rel_im + head_im * rel_re)
    query_head = join(rel_re * tail_re + rel_im * tail_im, rel_re * tail_im - rel_im * tail_re)
    positive = jnp.sum(query_tail * tail, axis=1, keepdims=True)
    queries = to_wide(jnp.concatenate([query_tail, query_head], axis=0)).astype(BF16)
    pull = jnp.zeros((2 * edges, 512), F32)
    for g in range(parts):
        here = slice(part * g, part * g + part)
        scores = dot(queries, rows_ref[here, :], ((1,), (1,)))
        weights = jax.nn.sigmoid(scores) * (negative_ref[step : step + 1, here] / 1024)
        weights = weights.astype(BF16)
        weights_ref[:, here] = weights
        pull = pull + dot(weights, rows_ref[here, :])
    pull = to_narrow(pull)
    positive_weight = -jax.nn.sigmoid(-positive)
    pull_re, pull_im = complex_parts(positive_weight * tail + pull[:edges])
    push_re, push_im = complex_parts(pull[edges:])
    grad_head = join(pull_re * rel_re + pull_im * rel_im, pull_im * rel_re - pull_re * rel_im)
    grad_tail = positive_weight * query_tail + join(
        push_re * rel_re - push_im * rel_im, push_re * rel_im + push_im * rel_re
    )
    grad_relation = join(
        pull_re * head_re + pull_im * head_im + push_re * tail_re + push_im * tail_im,
        pull_im * head_re - pull_re * head_im + push_re * tail_im - push_im * tail_re,
    )
    rel_spread = one_hot(iota((REL, edges), 0) == rel_ids)
    relation_grad = jnp.zeros((REL, WIDTH), F32)
    for piece in reversed(split3(grad_relation)):
        relation_grad = relation_grad + dot(rel_spread, piece)
    relation_grad_ref[...] = relation_grad
    edge_grads = to_wide(jnp.concatenate([grad_head, grad_tail], axis=0)).astype(BF16)
    for g in range(parts):
        here = slice(part * g, part * g + part)
        grads = dot(weights_ref[:, here], queries, ((0,), (0,)))
        hit = one_hot(iota((part, 2 * edges), 0) + part * g == slots)
        grads = grads + dot(hit, edge_grads)
        for j in range(per):
            wire_ref[per * g + j] = pack(grads[CAP * j : CAP * j + CAP]).astype(BF16)


def relation_update(grad_ref, table_ref, state_ref, new_table_ref, new_state_ref):
    for b in range(REL // 128):
        rows = slice(128 * b, 128 * b + 128)
        total = grad_ref[rows, :]
        state = lane_to_column(state_ref[b : b + 1, :])
        state = state + jnp.sum(total * total, axis=1, keepdims=True) / WIDTH
        new_state_ref[b : b + 1, :] = jnp.transpose(state)[:1]
        new_table_ref[rows, :] = table_ref[rows, :] - total * (RATE * lax.rsqrt(state[:, :1]))


def kernel(body, outs, scratch=(), flops=0, nbytes=4 << 20):
    return pl.pallas_call(
        body,
        out_shape=outs,
        scratch_shapes=scratch,
        compiler_params=pltpu.CompilerParams(vmem_limit_bytes=40 << 20),
        cost_estimate=pl.CostEstimate(flops=flops, bytes_accessed=nbytes, transcendentals=0),
    )


def exchange(x):
    return lax.all_to_all(x, "edge", split_axis=0, concat_axis=0, tiled=True)


def relation_sum(grad):
    part = lax.psum_scatter(grad, "rep", scatter_dimension=0, tiled=True)
    rows = part.shape[0] // OWN
    mine = jnp.sum(exchange(part.reshape(OWN, rows, WIDTH)), axis=0)
    part = exchange(jnp.broadcast_to(mine[None], (OWN, rows, WIDTH))).reshape(OWN * rows, WIDTH)
    return lax.all_gather(part, "rep", axis=0, tiled=True)


def shards(entities, ent_accum, relations, rel_accum, heads, tails, negatives, rel_ids):
    steps = heads.shape[1]
    shape = jax.ShapeDtypeStruct
    wire = shape((OWN, 128, 128), BF16)
    table, accum = entities, ent_accum.reshape(8, 128)
    rel_count = relations.shape[0]
    rel_table = jnp.pad(relations, ((0, REL - rel_count), (0, 0)))
    rel_state = jnp.pad(rel_accum, (0, REL - rel_count), constant_values=1.0).reshape(8, 128)
    send, negative, slots = kernel(
        prepare, (shape((OWN, 128), I32), shape((OWN, 128), F32), shape((steps, 256), I32))
    )(heads, tails, negatives)
    named = exchange(send.reshape(OWN, 1, 128)).reshape(OWN, 128)
    flat = jnp.stack([named[:, CAP * s : CAP * s + CAP].reshape(SLOTS) for s in range(steps)])
    negative = jnp.stack([negative[:, CAP * s : CAP * s + CAP].reshape(SLOTS) for s in range(steps)])
    rows = kernel(first_rows, wire, [pltpu.VMEM((1024, 512), BF16)], 3 << 30)(table, named)
    for s in range(steps):
        last = s == steps - 1
        rows = exchange(rows)
        grads, relation_grad = kernel(
            lambda *refs, s=s: block(s, *refs),
            (wire, shape((REL, WIDTH), F32)),
            [pltpu.VMEM((SLOTS, 512), BF16), pltpu.VMEM((256, SLOTS), BF16)],
            4 << 30,
        )(rows, slots, negative, rel_table, rel_ids)
        grads = exchange(grads)
        relation_total = relation_sum(relation_grad)
        outs = (shape(table.shape, F32), shape((8, 128), F32)) + (() if last else (wire,))
        scratch = [pltpu.VMEM((SLOTS, 512), BF16)] + ([] if last else [pltpu.VMEM((1024, 512), BF16)])
        table, accum, *rows = kernel(
            lambda *refs, s=s, last=last: update(s, last, *refs), outs, scratch, 5 << 30
        )(grads, flat, table, accum, named)
        rows = None if last else rows[0]
        rel_table, rel_state = kernel(
            relation_update, (shape((REL, WIDTH), F32), shape((8, 128), F32))
        )(relation_total, rel_table, rel_state)
    return table, accum.reshape(1, 1024), rel_table[:rel_count], rel_state.reshape(REL)[:rel_count]


def solution(mesh):
    in_specs = (
        P("rep", "edge", None),
        P("rep", "edge"),
        P(),
        P(),
        P("rep", None, "edge"),
        P("rep", None, "edge"),
        P("rep", None, "edge"),
        P("rep", None, "edge"),
    )
    out_specs = (P("rep", "edge", None), P("rep", "edge"), P(), P())
    return jax.shard_map(shards, mesh=mesh, in_specs=in_specs, out_specs=out_specs, check_vma=False)
```

time: 983 us -> 482 us (0.49)
  waiting for transfers between devices: 618 us -> 261 us
  other arithmetic: 156 us -> 0.29 us
  local copies, waits for them, and re-layouts: 117 us -> 36.7 us
  blocking collectives: 0 us -> 78.9 us
  Pallas kernels: 0 us -> 39 us
  starting transfers between devices: 57.8 us -> 45.4 us
    psum x2 -> x0, waiting for transfers between devices: 551 us -> none  [shards(): relation_total = lax.psum(relation_local, ('edge', 'rep'))]
    all_to_all x6, waiting for transfers between devices: 67.4 us -> 170 us  [exchange(): return lax.all_to_all(x, 'edge', split_axis=0, concat_axis=0, tiled=True)]
    sub x7 -> x0, other arithmetic: 80.2 us -> none  [the longest x2 71.6 us: shards(): ranks = jnp.arange(request_count, dtype=jnp.int32) - starts[sorted_owner]]
    all_to_all x0 -> x3, blocking collectives: none -> 78.9 us  [exchange(): return lax.all_to_all(x, 'edge', split_axis=0, concat_axis=0, tiled=True)]
    reduce_scatter x0 -> x2, waiting for transfers between devices: none -> 56.2 us  [relation_sum(): part = lax.psum_scatter(grad, 'rep', scatter_dimension=0, tiled=True)]
    gather x16 -> x0, local copies, waits for them, and re-layouts: 50.5 us -> none  [the longest x2 14.2 us: shards(): table[received].astype(jnp.bfloat16)]
    scatter x6 -> x0, local copies, waits for them, and re-layouts: 41.6 us -> none  [the longest x2 20.5 us: shards(): send_grads = jnp.zeros((owners_count * capacity, width), jnp.bfloat16).at...]
    scatter-add x4 -> x0, other arithmetic: 40.3 us -> none  [the longest x2 34.9 us: shards(): jax.ops.segment_sum(returned.reshape(owners_count * capacity, width).asty...]
  transfers between devices with their start and end apart: 8 -> 10, of which waited for: 4 -> 9; matrix products, arithmetic and copies ran while one was open for 12% -> 3% of each run, Pallas kernels for 0% -> 3%
where the time goes in v1:
time: 482 us; the launch traced here: 475 us
  waiting for transfers between devices  261 us (54%)
  blocking collectives  78.9 us (16%)
  starting transfers between devices  45.4 us (9%)
  Pallas kernels  39 us (8%)
  local copies, waits for them, and re-layouts  36.7 us (8%)
  between operations  14.3 us (3%)
    all_to_all x6, waiting for transfers between devices, exchange(): return lax.all_to_all(x, 'edge', split_axis=0, concat_axis=0, tiled=True)  170 us
    all_to_all x3, blocking collectives, exchange(): return lax.all_to_all(x, 'edge', split_axis=0, concat_axis=0, tiled=True)  78.9 us
    reduce_scatter x2, waiting for transfers between devices, relation_sum(): part = lax.psum_scatter(grad, 'rep', scatter_dimension=0, tiled=True)  56.2 us
    all_to_all x6, starting transfers between devices, exchange(): return lax.all_to_all(x, 'edge', split_axis=0, concat_axis=0, tiled=True)  44.2 us
    all_gather x2, waiting for transfers between devices, relation_sum(): return lax.all_gather(part, 'rep', axis=0, tiled=True)  34.9 us
    unnamed x44, local copies, waits for them, and re-layouts  28.9 us
    pallas_call x2, Pallas kernels, shards(): kernel(lambda *refs, s=s: block(s, *refs), (wire, shape((REL, WIDTH), F32...  19.3 us
    pallas_call x2, Pallas kernels, shards(): kernel(lambda *refs, s=s, last=last: update(s, last, *refs), outs, scratc...  12.5 us
  transfers between devices with their start and end apart: 10, of which 9 were waited for; matrix products, arithmetic and copies ran while one was open for 3% of the time, Pallas kernels for 3%

profile of v1, /device:TPU:1, one launch (start us, length us, event | category | flops | bytes accessed | tf_op | source)
XLA Modules:
  0.0 475.3 jit_solution(161351989014258765)
XLA Ops:
  9.2 1.7 shard_map.111
  10.9 13.2 %all-to-all-start = ((s32[64,1,128]{2,1,0:T(1,128)}), s32[64,1,128]{2,1,0:T(1,128)S(1)}, u32[]{:S(2)}, u32[]{:S(2)}) async-start(s32[64,1,128]{2,1,0:T(1,128)} %bitcast.1), calls=%async_computation | async-start | bytes 65536 | tf_op jit(solution)/shard_map/all_to_all | solution.py:253
  24.1 1.8 copy.23.table_ref.refs_2_
  25.9 7.3 %all-to-all-done = s32[64,1,128]{2,1,0:T(1,128)S(1)} async-done(((s32[64,1,128]{2,1,0:T(1,128)}), s32[64,1,128]{2,1,0:T(1,128)S(1)}, u32[]{:S(2)}, u32[]{:S(2)}) %all-to-all-start) | async-done | bytes 32800 | tf_op jit(solution)/shard_map/all_to_all | solution.py:253
  33.3 3.5 shard_map.112
  38.2 5.6 %all-to-all-start.1 = ((bf16[64,128,128]{2,1,0:T(8,128)(2,1)}), bf16[64,128,128]{2,1,0:T(8,128)(2,1)}, u32[]{:S(2)}, u32[]{:S(2)}) async-start(bf16[64,128,128]{2,1,0:T(8,128)(2,1)} %copy-done.10), calls=%async_computation.1 | async-start | bytes 4194304 | tf_op jit(solution)/shard_map/all_to_all | solution.py:253
  44.6 2.9 copy.24
  47.5 1.8 pad.8.refs_3_.table_ref
  49.3 45.7 %all-to-all-done.1.refs_0_ = bf16[64,128,128]{2,1,0:T(8,128)(2,1)} async-done(((bf16[64,128,128]{2,1,0:T(8,128)(2,1)}), bf16[64,128,128]{2,1,0:T(8,128)(2,1)}, u32[]{:S(2)}, u32[]{:S(2)}) %all-to-all-start.1) | async-done | bytes 2097184 | tf_op jit(solution)/shard_map/all_to_all | solution.py:253
  95.0 8.8 %shard_map.113 = (bf16[64,128,128]{2,1,0:T(8,128)(2,1)S(1)}, f32[1024,400]{1,0:T(8,128)S(1)}) custom-call(bf16[64,128,128]{2,1,0:T(8,128)(2,1)} %all-to-all-done.1.refs_0_, s32[2,256]{1,0:T(2,128)S(1)} %get-tuple-element.21.refs_1_, f32[2,2560]{1,0:T(2,128)S(1)} %pad_maximum_fusion.refs_2_, f32[1024,400]{1,0:T(8,128)S(1)} %pad.8.refs_3_.table_ref, ...), custom_call_target="tpu_custom_call" | custom-call | flops 4294967296 | bytes 4194304 | tf_op jit(solution)/shard_map/pallas_call | solution.py:282
  106.6 28.9 %reduce-scatter.3.cloned.1.call-done = f32[256,400]{1,0:T(8,128)} async-done(((f32[1024,400]{1,0:T(8,128)}), f32[256,400]{1,0:T(8,128)}) %reduce-scatter.3.cloned.1.call-update) | async-done | bytes 409616 | tf_op jit(solution)/shard_map/reduce_scatter | solution.py:257
  136.7 27.7 %all_to_all.45 = f32[64,4,400]{2,1,0:T(4,128)S(1)} all-to-all(f32[64,4,400]{2,1,0:T(4,128)S(1)} %reshape.43), channel_id=1, replica_groups=mesh['edge'=64,'rep'=4] {'edge'}, dimensions={0} | all-to-all | bytes 819200 | tf_op jit(solution)/shard_map/all_to_all | solution.py:253
  164.4 6.5 %all-to-all-start.2 = ((bf16[64,128,128]{2,1,0:T(8,128)(2,1)}), bf16[64,128,128]{2,1,0:T(8,128)(2,1)}, u32[]{:S(2)}, u32[]{:S(2)}) async-start(bf16[64,128,128]{2,1,0:T(8,128)(2,1)} %copy-done.9), calls=%async_computation.2 | async-start | bytes 4194304 | tf_op jit(solution)/shard_map/all_to_all | solution.py:253
  171.3 50.7 %all-to-all-done.2.refs_0_ = bf16[64,128,128]{2,1,0:T(8,128)(2,1)} async-done(((bf16[64,128,128]{2,1,0:T(8,128)(2,1)}), bf16[64,128,128]{2,1,0:T(8,128)(2,1)}, u32[]{:S(2)}, u32[]{:S(2)}) %all-to-all-start.2) | async-done | bytes 2097184 | tf_op jit(solution)/shard_map/all_to_all | solution.py:253
  222.9 6.1 %all-to-all-start.5 = ((f32[64,4,400]{2,1,0:T(4,128)}), f32[64,4,400]{2,1,0:T(4,128)S(1)}, u32[]{:S(2)}, u32[]{:S(2)}) async-start(f32[64,4,400]{2,1,0:T(4,128)} %broadcast_in_dim.4), calls=%async_computation.6 | async-start | bytes 1048576 | tf_op jit(solution)/shard_map/all_to_all | solution.py:253
  230.6 8.2 %shard_map.114 = (f32[1,1024,400]{2,1,0:T(8,128)S(1)}, f32[8,128]{1,0:T(8,128)S(1)}, bf16[64,128,128]{2,1,0:T(8,128)(2,1)S(1)}) custom-call(bf16[64,128,128]{2,1,0:T(8,128)(2,1)} %all-to-all-done.2.refs_0_, s32[2,2560]{1,0:T(2,128)S(1)} %pad_add_fusion.refs_1_, f32[1,1024,400]{2,1,0:T(8,128)S(1)} %copy-done.1, f32[8,128]{1,0:T(8,128)S(1)} %bitcast.14, ...), custom_call_target="tpu_custom_call" | custom-call | flops 5368709120 | bytes 4194304 | tf_op jit(solution)/shard_map/pallas_call | solution.py:292
  241.6 4.6 all-to-all-done.5
  246.2 6.6 %all-to-all-start.3 = ((bf16[64,128,128]{2,1,0:T(8,128)(2,1)}), bf16[64,128,128]{2,1,0:T(8,128)(2,1)}, u32[]{:S(2)}, u32[]{:S(2)}) async-start(bf16[64,128,128]{2,1,0:T(8,128)(2,1)} %copy-done.8), calls=%async_computation.3 | async-start | bytes 4194304 | tf_op jit(solution)/shard_map/all_to_all | solution.py:253
  254.1 34.9 %all-gather.3.cloned.1.call-done.grad_ref = f32[1024,400]{1,0:T(8,128)} async-done(((f32[256,400]{1,0:T(8,128)}), f32[1024,400]{1,0:T(8,128)}) %all-gather.3.cloned.1.call-update) | async-done | bytes 1638416 | tf_op jit(solution)/shard_map/all_gather | solution.py:261
  289.0 1.6 copy-done.6
  292.7 11.3 %all-to-all-done.3.refs_0_ = bf16[64,128,128]{2,1,0:T(8,128)(2,1)} async-done(((bf16[64,128,128]{2,1,0:T(8,128)(2,1)}), bf16[64,128,128]{2,1,0:T(8,128)(2,1)}, u32[]{:S(2)}, u32[]{:S(2)}) %all-to-all-start.3) | async-done | bytes 2097184 | tf_op jit(solution)/shard_map/all_to_all | solution.py:253
  304.0 1.6 copy-done.3
  305.6 10.5 %shard_map.116 = (bf16[64,128,128]{2,1,0:T(8,128)(2,1)}, f32[1024,400]{1,0:T(8,128)}) custom-call(bf16[64,128,128]{2,1,0:T(8,128)(2,1)} %all-to-all-done.3.refs_0_, s32[2,256]{1,0:T(2,128)S(1)} %get-tuple-element.21.refs_1_, f32[2,2560]{1,0:T(2,128)S(1)} %pad_maximum_fusion.refs_2_, f32[1024,400]{1,0:T(8,128)S(1)} %copy-done.3, s32[1,2,128]{2,1,0:T(2,128)S(1)} %copy-done.16), custom_call_target="tpu_custom_call" | custom-call | flops 4294967296 | bytes 4194304 | tf_op jit(solution)/shard_map/pallas_call | solution.py:282
  316.1 27.3 %reduce-scatter.5.cloned.1.call-done = f32[256,400]{1,0:T(8,128)} async-done(((f32[1024,400]{1,0:T(8,128)}), f32[256,400]{1,0:T(8,128)}) %reduce-scatter.5.cloned.1.call-update) | async-done | bytes 409616 | tf_op jit(solution)/shard_map/reduce_scatter | solution.py:257
  344.6 27.8 %all_to_all.46 = f32[64,4,400]{2,1,0:T(4,128)S(1)} all-to-all(f32[64,4,400]{2,1,0:T(4,128)S(1)} %reshape.47), channel_id=1, replica_groups=mesh['edge'=64,'rep'=4] {'edge'}, dimensions={0} | all-to-all | bytes 819200 | tf_op jit(solution)/shard_map/all_to_all | solution.py:253
  372.6 23.4 %all_to_all.47 = f32[64,4,400]{2,1,0:T(4,128)S(1)} all-to-all(f32[64,4,400]{2,1,0:T(4,128)S(1)} %broadcast_in_dim.5), channel_id=1, replica_groups=mesh['edge'=64,'rep'=4] {'edge'}, dimensions={0} | all-to-all | bytes 819200 | tf_op jit(solution)/shard_map/all_to_all | solution.py:253
  396.0 6.3 %all-to-all-start.6 = ((bf16[64,128,128]{2,1,0:T(8,128)(2,1)}), bf16[64,128,128]{2,1,0:T(8,128)(2,1)S(1)}, u32[]{:S(2)}, u32[]{:S(2)}) async-start(bf16[64,128,128]{2,1,0:T(8,128)(2,1)} %get-tuple-element.27), calls=%async_computation.7 | async-start | bytes 4194304 | tf_op jit(solution)/shard_map/all_to_all | solution.py:253
  403.6 49.9 %all-to-all-done.6.refs_0_ = bf16[64,128,128]{2,1,0:T(8,128)(2,1)S(1)} async-done(((bf16[64,128,128]{2,1,0:T(8,128)(2,1)}), bf16[64,128,128]{2,1,0:T(8,128)(2,1)S(1)}, u32[]{:S(2)}, u32[]{:S(2)}) %all-to-all-start.6) | async-done | bytes 2097184 | tf_op jit(solution)/shard_map/all_to_all | solution.py:253
  453.5 1.6 copy-done.18
  455.1 4.3 shard_map.117
  460.8 2.9 copy.26
  466.8 1.7 copy.27
  (66 shorter events, 24.4 us)
Async XLA Ops:
  7.2 0.7 copy-start.12
  7.9 0.7 copy-start.13
  8.5 0.7 copy-start.14
  10.9 22.4 %all-to-all-start = ((s32[64,1,128]{2,1,0:T(1,128)}), s32[64,1,128]{2,1,0:T(1,128)S(1)}, u32[]{:S(2)}, u32[]{:S(2)}) async-start(s32[64,1,128]{2,1,0:T(1,128)} %bitcast.1), calls=%async_computation | async-start | bytes 65536 | tf_op jit(solution)/shard_map/all_to_all | solution.py:253
  25.9 10.8 %copy-start = (f32[1,1024,400]{2,1,0:T(8,128)}, f32[1,1024,400]{2,1,0:T(8,128)S(1)}, u32[]{:S(2)}) copy-start(f32[1,1024,400]{2,1,0:T(8,128)S(1)} %copy.23.table_ref.refs_2_) | copy-start | bytes 4915204
  36.8 1.4 copy-start.10
  38.2 56.9 %all-to-all-start.1 = ((bf16[64,128,128]{2,1,0:T(8,128)(2,1)}), bf16[64,128,128]{2,1,0:T(8,128)(2,1)}, u32[]{:S(2)}, u32[]{:S(2)}) async-start(bf16[64,128,128]{2,1,0:T(8,128)(2,1)} %copy-done.10), calls=%async_computation.1 | async-start | bytes 4194304 | tf_op jit(solution)/shard_map/all_to_all | solution.py:253
  43.8 91.7 %reduce-scatter.3.cloned.1.call-start = ((), (), s32[]{:S(2)}) async-start(), calls=%async_computation.11 | async-start | bytes 2621440 | tf_op jit(solution)/shard_map/reduce_scatter | solution.py:257
  47.5 47.5 %copy-start.16 = (s32[1,2,128]{2,1,0:T(2,128)S(1)}, s32[1,2,128]{2,1,0:T(2,128)}, u32[]{:S(2)}) copy-start(s32[1,2,128]{2,1,0:T(2,128)} %refs_4_.3) | copy-start | bytes 3076
  103.8 1.3 copy-start.9
  105.2 1.4 copy-start.11
  164.4 57.6 %all-to-all-start.2 = ((bf16[64,128,128]{2,1,0:T(8,128)(2,1)}), bf16[64,128,128]{2,1,0:T(8,128)(2,1)}, u32[]{:S(2)}, u32[]{:S(2)}) async-start(bf16[64,128,128]{2,1,0:T(8,128)(2,1)} %copy-done.9), calls=%async_computation.2 | async-start | bytes 4194304 | tf_op jit(solution)/shard_map/all_to_all | solution.py:253
  170.9 58.2 %copy-start.15 = (f32[1,1024]{1,0:T(1,128)S(1)}, f32[1,1024]{1,0:T(1,128)}, u32[]{:S(2)}) copy-start(f32[1,1024]{1,0:T(1,128)} %param.9) | copy-start | bytes 12292
  222.9 23.3 %all-to-all-start.5 = ((f32[64,4,400]{2,1,0:T(4,128)}), f32[64,4,400]{2,1,0:T(4,128)S(1)}, u32[]{:S(2)}, u32[]{:S(2)}) async-start(f32[64,4,400]{2,1,0:T(4,128)} %broadcast_in_dim.4), calls=%async_computation.6 | async-start | bytes 1048576 | tf_op jit(solution)/shard_map/all_to_all | solution.py:253
  229.0 1.6 copy-start.1
  238.8 1.4 copy-start.8
  240.3 1.4 copy-start.17
  246.2 7.9 %copy-start.19 = (f32[1000]{0:T(1024)S(1)}, f32[1000]{0:T(1024)}, u32[]{:S(2)}) copy-start(f32[1000]{0:T(1024)} %param.11) | copy-start | bytes 12004
  246.2 57.8 %all-to-all-start.3 = ((bf16[64,128,128]{2,1,0:T(8,128)(2,1)}), bf16[64,128,128]{2,1,0:T(8,128)(2,1)}, u32[]{:S(2)}, u32[]{:S(2)}) async-start(bf16[64,128,128]{2,1,0:T(8,128)(2,1)} %copy-done.8), calls=%async_computation.3 | async-start | bytes 4194304 | tf_op jit(solution)/shard_map/all_to_all | solution.py:253
  252.8 36.2 %all-gather.3.cloned.1.call-start = ((), (), s32[]{:S(2)}) async-start(), calls=%async_computation.12 | async-start | bytes 2621440 | tf_op jit(solution)/shard_map/all_gather | solution.py:261
  253.9 89.5 %reduce-scatter.5.cloned.1.call-start = ((), (), s32[]{:S(2)}) async-start(), calls=%async_computation.13 | async-start | bytes 2621440 | tf_op jit(solution)/shard_map/reduce_scatter | solution.py:257
  289.0 1.6 copy-start.6
  291.3 1.3 copy-start.2
  304.0 1.6 copy-start.3
  396.0 57.5 %all-to-all-start.6 = ((bf16[64,128,128]{2,1,0:T(8,128)(2,1)}), bf16[64,128,128]{2,1,0:T(8,128)(2,1)S(1)}, u32[]{:S(2)}, u32[]{:S(2)}) async-start(bf16[64,128,128]{2,1,0:T(8,128)(2,1)} %get-tuple-element.27), calls=%async_computation.7 | async-start | bytes 4194304 | tf_op jit(solution)/shard_map/all_to_all | solution.py:253
  402.3 61.4 %all-gather.5.cloned.1.call-start = ((), (), s32[]{:S(2)}) async-start(), calls=%async_computation.14 | async-start | bytes 2621440 | tf_op jit(solution)/shard_map/all_gather | solution.py:261
  453.5 1.6 copy-start.18
  459.4 1.4 copy-start.7
  460.8 2.9 copy-start.4
  463.7 1.6 copy-start.5
Sparse Core Ops, SparseCore 0:
  106.7 28.6 reduce-scatter.2
  256.2 32.7 all-gather.2
  316.2 27.1 reduce-scatter.4
  405.2 32.7 all-gather.4

commit v2 on v1

--- a/solution.py
+++ b/solution.py
@@ -163,8 +163,8 @@
 
 
 def block(
-    step, wire_in_ref, slots_ref, negative_ref, relations_ref, rel_ids_ref,
-    wire_ref, relation_grad_ref, rows_ref, weights_ref,
+    step, at_ref, wire_in_ref, slots_ref, negative_ref, relations_ref, rel_ids_ref,
+    wire_ref, keep_ref, give_ref, rows_ref, weights_ref,
 ):
     edges, parts = 128, 4
     part = SLOTS // parts
@@ -183,13 +183,13 @@
     rel_ids = rel_ids_ref[0, step : step + 1, :]
     rel_column = lane_to_column(rel_ids.astype(F32))[:, :1].astype(I32)
     rel_hit = one_hot(rel_column == iota((edges, REL), 1))
-    relation = jnp.zeros((edges, WIDTH), F32)
-    for piece in reversed(split3(relations_ref[...])):
-        relation = relation + dot(rel_hit, piece)
+    relation = [
+        sum(dot(rel_hit, piece) for piece in reversed(split3(relations_ref[k]))) for k in range(2)
+    ]
 
     head_re, head_im = complex_parts(head)
     tail_re, tail_im = complex_parts(tail)
-    rel_re, rel_im = complex_parts(relation)
+    rel_re, rel_im = relation
     query_tail = join(head_re * rel_re - head_im * rel_im, head_re * rel_im + head_im * rel_re)
     query_head = join(rel_re * tail_re + rel_im * tail_im, rel_re * tail_im - rel_im * tail_re)
     positive = jnp.sum(query_tail * tail, axis=1, keepdims=True)
@@ -210,15 +210,14 @@
     grad_tail = positive_weight * query_tail + join(
         push_re * rel_re - push_im * rel_im, push_re * rel_im + push_im * rel_re
     )
-    grad_relation = join(
+    grad_relation = (
         pull_re * head_re + pull_im * head_im + push_re * tail_re + push_im * tail_im,
         pull_im * head_re - pull_re * head_im + push_re * tail_im - push_im * tail_re,
     )
     rel_spread = one_hot(iota((REL, edges), 0) == rel_ids)
-    relation_grad = jnp.zeros((REL, WIDTH), F32)
-    for piece in reversed(split3(grad_relation)):
-        relation_grad = relation_grad + dot(rel_spread, piece)
-    relation_grad_ref[...] = relation_grad
+    relation_grad = [sum(dot(rel_spread, piece) for piece in reversed(split3(g))) for g in grad_relation]
+    keep_ref[...] = jnp.where(at_ref[3] == 0, relation_grad[0], relation_grad[1])
+    give_ref[...] = jnp.where(at_ref[3] == 0, relation_grad[1], relation_grad[0])
     edge_grads = to_wide(jnp.concatenate([grad_head, grad_tail], axis=0)).astype(BF16)
     for g in range(parts):
         here = slice(part * g, part * g + part)
@@ -229,20 +228,51 @@
             wire_ref[per * g + j] = pack(grads[CAP * j : CAP * j + CAP]).astype(BF16)
 
 
-def relation_update(grad_ref, table_ref, state_ref, new_table_ref, new_state_ref):
+def scatter_stage(axis, count, own_ref, *refs):
+    at_ref, *rest = refs
+    arrived, outs = rest[: len(rest) - count], rest[len(rest) - count :]
+    total = own_ref[...]
+    for ref in arrived:
+        total = total + ref[...]
+    if count == 1:
+        outs[0][...] = total
+        return
+    *outs, sum_ref = outs
+    sum_ref[...] = total
+    n = count - 1
+    rows = total.shape[0] // n
+    for d in range(n):
+        start = pl.multiple_of(lax.rem(at_ref[axis] + d, n) * rows, 8)
+        outs[d][...] = sum_ref[pl.ds(start, rows), :]
+
+
+def gather_stage(axis, at_ref, *refs):
+    *parts, out_ref = refs
+    n, rows = len(parts), parts[0].shape[0]
+    for d in range(n):
+        start = pl.multiple_of(lax.rem(at_ref[axis] + n - d, n) * rows, 8)
+        out_ref[pl.ds(start, rows), :] = parts[d][...]
+
+
+def relation_update(at_ref, mine_ref, other_ref, table_ref, state_ref, new_table_ref, new_state_ref):
     for b in range(REL // 128):
         rows = slice(128 * b, 128 * b + 128)
-        total = grad_ref[rows, :]
+        mine, other = mine_ref[rows, :], other_ref[rows, :]
+        total = [jnp.where(at_ref[3] == k, mine, other) for k in range(2)]
         state = lane_to_column(state_ref[b : b + 1, :])
-        state = state + jnp.sum(total * total, axis=1, keepdims=True) / WIDTH
+        square = sum(jnp.sum(t * t, axis=1, keepdims=True) for t in total)
+        state = state + square / WIDTH
         new_state_ref[b : b + 1, :] = jnp.transpose(state)[:1]
-        new_table_ref[rows, :] = table_ref[rows, :] - total * (RATE * lax.rsqrt(state[:, :1]))
-
-
-def kernel(body, outs, scratch=(), flops=0, nbytes=4 << 20):
+        for k in range(2):
+            new_table_ref[k, rows, :] = table_ref[k, rows, :] - total[k] * (RATE * lax.rsqrt(state[:, :1]))
+
+
+def kernel(body, outs, scratch=(), flops=0, nbytes=4 << 20, in_specs=None):
+    more = {} if in_specs is None else {"in_specs": in_specs}
     return pl.pallas_call(
         body,
         out_shape=outs,
+        **more,
         scratch_shapes=scratch,
         compiler_params=pltpu.CompilerParams(vmem_limit_bytes=40 << 20),
         cost_estimate=pl.CostEstimate(flops=flops, bytes_accessed=nbytes, transcendentals=0),
@@ -253,12 +283,51 @@
     return lax.all_to_all(x, "edge", split_axis=0, concat_axis=0, tiled=True)
 
 
-def relation_sum(grad):
-    part = lax.psum_scatter(grad, "rep", scatter_dimension=0, tiled=True)
-    rows = part.shape[0] // OWN
-    mine = jnp.sum(exchange(part.reshape(OWN, rows, WIDTH)), axis=0)
-    part = exchange(jnp.broadcast_to(mine[None], (OWN, rows, WIDTH))).reshape(OWN * rows, WIDTH)
-    return lax.all_gather(part, "rep", axis=0, tiled=True)
+def edge_of(y, z, core):
+    return (y * 8 + z) * 2 + core
+
+
+def edge_pairs(dy, dz, flip=0):
+    return [
+        (edge_of(y, z, core), edge_of((y + dy) % 4, (z + dz) % 8, core ^ flip))
+        for y in range(4)
+        for z in range(8)
+        for core in range(2)
+    ]
+
+
+def move(x, axis, d):
+    if axis == 0:
+        return lax.ppermute(x, "rep", [(k, (k + d) % 4) for k in range(4)])
+    return lax.ppermute(x, "edge", edge_pairs(d if axis == 1 else 0, d if axis == 2 else 0))
+
+
+def relation_sum(at, keep, give):
+    shape = jax.ShapeDtypeStruct
+    smem, vmem = pl.BlockSpec(memory_space=pltpu.SMEM), pl.BlockSpec(memory_space=pltpu.VMEM)
+    sizes = (4, 4, 8)
+    arrived = [lax.ppermute(give, "edge", edge_pairs(0, 0, 1))]
+    own, rows = keep, REL
+    for axis, n in enumerate(sizes):
+        outs = [shape((rows // n, HALF), F32)] * n + [shape((rows, HALF), F32)]
+        own, *parts, _ = kernel(
+            lambda *refs, axis=axis, n=n: scatter_stage(axis, n + 1, *refs), outs,
+            in_specs=[vmem, smem] + [vmem] * len(arrived),
+        )(own, at, *arrived)
+        arrived = [move(part, axis, d + 1) for d, part in enumerate(parts)]
+        rows //= n
+    own = kernel(
+        lambda *refs: scatter_stage(0, 1, *refs), [shape((rows, HALF), F32)],
+        in_specs=[vmem, smem] + [vmem] * len(arrived),
+    )(own, at, *arrived)[0]
+    for axis, n in reversed(list(enumerate(sizes))):
+        arrived = [move(own, axis, d) for d in range(1, n)]
+        rows *= n
+        own = kernel(
+            lambda *refs, axis=axis: gather_stage(axis, *refs), shape((rows, HALF), F32),
+            in_specs=[smem] + [vmem] * n,
+        )(at, own, *arrived)
+    return own, lax.ppermute(own, "edge", edge_pairs(0, 0, 1))
 
 
 def shards(entities, ent_accum, relations, rel_accum, heads, tails, negatives, rel_ids):
@@ -268,6 +337,10 @@
     table, accum = entities, ent_accum.reshape(8, 128)
     rel_count = relations.shape[0]
     rel_table = jnp.pad(relations, ((0, REL - rel_count), (0, 0)))
+    rel_table = jnp.stack(complex_parts(rel_table))
+    edge = lax.axis_index("edge")
+    at = jnp.stack([lax.axis_index("rep"), edge // 16, edge // 2 % 8, edge % 2]).astype(I32)
+    smem, vmem = pl.BlockSpec(memory_space=pltpu.SMEM), pl.BlockSpec(memory_space=pltpu.VMEM)
     rel_state = jnp.pad(rel_accum, (0, REL - rel_count), constant_values=1.0).reshape(8, 128)
     send, negative, slots = kernel(
         prepare, (shape((OWN, 128), I32), shape((OWN, 128), F32), shape((steps, 256), I32))
@@ -279,14 +352,15 @@
     for s in range(steps):
         last = s == steps - 1
         rows = exchange(rows)
-        grads, relation_grad = kernel(
+        grads, keep, give = kernel(
             lambda *refs, s=s: block(s, *refs),
-            (wire, shape((REL, WIDTH), F32)),
+            (wire, shape((REL, HALF), F32), shape((REL, HALF), F32)),
             [pltpu.VMEM((SLOTS, 512), BF16), pltpu.VMEM((256, SLOTS), BF16)],
             4 << 30,
-        )(rows, slots, negative, rel_table, rel_ids)
+            in_specs=[smem] + [vmem] * 5,
+        )(at, rows, slots, negative, rel_table, rel_ids)
         grads = exchange(grads)
-        relation_total = relation_sum(relation_grad)
+        mine, other = relation_sum(at, keep, give)
         outs = (shape(table.shape, F32), shape((8, 128), F32)) + (() if last else (wire,))
         scratch = [pltpu.VMEM((SLOTS, 512), BF16)] + ([] if last else [pltpu.VMEM((1024, 512), BF16)])
         table, accum, *rows = kernel(
@@ -294,9 +368,11 @@
         )(grads, flat, table, accum, named)
         rows = None if last else rows[0]
         rel_table, rel_state = kernel(
-            relation_update, (shape((REL, WIDTH), F32), shape((8, 128), F32))
-        )(relation_total, rel_table, rel_state)
-    return table, accum.reshape(1, 1024), rel_table[:rel_count], rel_state.reshape(REL)[:rel_count]
+            relation_update, (shape((2, REL, HALF), F32), shape((8, 128), F32)),
+            in_specs=[smem] + [vmem] * 4,
+        )(at, mine, other, rel_table, rel_state)
+    rel_table = jnp.concatenate([rel_table[0], rel_table[1]], axis=1)[:rel_count]
+    return table, accum.reshape(1, 1024), rel_table, rel_state.reshape(REL)[:rel_count]
 
 
 def solution(mesh):

time: 482 us -> 423 us (0.88)
  starting transfers between devices: 45.4 us -> 146 us
  waiting for transfers between devices: 261 us -> 180 us
  blocking collectives: 78.9 us -> 0 us
  Pallas kernels: 39 us -> 55.1 us
  between operations: 14.3 us -> 1.38 us
    ppermute x0 -> x56, starting transfers between devices: none -> 105 us  [the longest x40 68.3 us: move(): lax.ppermute(x, 'edge', edge_pairs(d if axis == 1 else 0, d if axis == 2...]
    all_to_all x3 -> x0, blocking collectives: 78.9 us -> none  [exchange(): return lax.all_to_all(x, 'edge', split_axis=0, concat_axis=0, tiled=True)]
    ppermute x0 -> x56, waiting for transfers between devices: none -> 74.1 us  [the longest x40 33.8 us: move(): lax.ppermute(x, 'edge', edge_pairs(d if axis == 1 else 0, d if axis == 2...]
    all_to_all x6 -> x5, waiting for transfers between devices: 170 us -> 106 us  [exchange(): return lax.all_to_all(x, 'edge', split_axis=0, concat_axis=0, tiled=True)]
    reduce_scatter x2 -> x0, waiting for transfers between devices: 56.2 us -> none  [relation_sum(): part = lax.psum_scatter(grad, 'rep', scatter_dimension=0, tiled=True)]
    all_gather x2 -> x0, waiting for transfers between devices: 34.9 us -> none  [relation_sum(): return lax.all_gather(part, 'rep', axis=0, tiled=True)]
    pallas_call x4 -> x18, Pallas kernels: 21.4 us -> 35.8 us  [the longest x2 19 us: shards(): kernel(lambda *refs, s=s: block(s, *refs), (wire, shape((REL, HALF), F32)...]
    all_to_all x6 -> x5, starting transfers between devices: 44.2 us -> 40.2 us  [exchange(): return lax.all_to_all(x, 'edge', split_axis=0, concat_axis=0, tiled=True)]
  transfers between devices with their start and end apart: 10 -> 61, of which waited for: 9 -> 35; matrix products, arithmetic and copies ran while one was open for 3% -> 4% of each run, Pallas kernels for 3% -> 4%
where the time goes in v2:
time: 423 us; the launch traced here: 417 us
  waiting for transfers between devices  180 us (43%)
  starting transfers between devices  146 us (35%)
  Pallas kernels  55.1 us (13%)
  local copies, waits for them, and re-layouts  34.4 us (8%)
    all_to_all x5, waiting for transfers between devices, exchange(): return lax.all_to_all(x, 'edge', split_axis=0, concat_axis=0, tiled=True)  106 us
    ppermute x40, starting transfers between devices, move(): lax.ppermute(x, 'edge', edge_pairs(d if axis == 1 else 0, d if axis == 2...  68.3 us
    all_to_all x5, starting transfers between devices, exchange(): return lax.all_to_all(x, 'edge', split_axis=0, concat_axis=0, tiled=True)  40.2 us
    ppermute x40, waiting for transfers between devices, move(): lax.ppermute(x, 'edge', edge_pairs(d if axis == 1 else 0, d if axis == 2...  33.8 us
    ppermute x12, waiting for transfers between devices, move(): return lax.ppermute(x, 'rep', [(k, (k + d) % 4) for k in range(4)])  31.8 us
    unnamed x42, local copies, waits for them, and re-layouts  25.8 us
    ppermute x12, starting transfers between devices, move(): return lax.ppermute(x, 'rep', [(k, (k + d) % 4) for k in range(4)])  19.5 us
    pallas_call x2, Pallas kernels, shards(): kernel(lambda *refs, s=s: block(s, *refs), (wire, shape((REL, HALF), F32)...  19 us
  transfers between devices with their start and end apart: 61, of which 35 were waited for; matrix products, arithmetic and copies ran while one was open for 4% of the time, Pallas kernels for 4%

profile of v2, /device:TPU:1, one launch (start us, length us, event | category | flops | bytes accessed | tf_op | source)
XLA Modules:
  0.0 417.4 jit_solution(7854784919834706820)
XLA Ops:
  4.4 13.2 %all-to-all-start = ((s32[64,1,128]{2,1,0:T(1,128)}), s32[64,1,128]{2,1,0:T(1,128)S(1)}, u32[]{:S(2)}, u32[]{:S(2)}) async-start(s32[64,1,128]{2,1,0:T(1,128)} %bitcast.5), calls=%async_computation | async-start | bytes 65536 | tf_op jit(solution)/shard_map/all_to_all | solution.py:283
  19.4 7.3 %all-to-all-done = s32[64,1,128]{2,1,0:T(1,128)S(1)} async-done(((s32[64,1,128]{2,1,0:T(1,128)}), s32[64,1,128]{2,1,0:T(1,128)S(1)}, u32[]{:S(2)}, u32[]{:S(2)}) %all-to-all-start) | async-done | bytes 32800 | tf_op jit(solution)/shard_map/all_to_all | solution.py:283
  26.8 3.5 shard_map.112
  31.6 6.1 %all-to-all-start.1 = ((bf16[64,128,128]{2,1,0:T(8,128)(2,1)}), bf16[64,128,128]{2,1,0:T(8,128)(2,1)}, u32[]{:S(2)}, u32[]{:S(2)}) async-start(bf16[64,128,128]{2,1,0:T(8,128)(2,1)} %copy-done.7), calls=%async_computation.1 | async-start | bytes 4194304 | tf_op jit(solution)/shard_map/all_to_all | solution.py:283
  40.7 48.1 %all-to-all-done.1.refs_1_ = bf16[64,128,128]{2,1,0:T(8,128)(2,1)} async-done(((bf16[64,128,128]{2,1,0:T(8,128)(2,1)}), bf16[64,128,128]{2,1,0:T(8,128)(2,1)}, u32[]{:S(2)}, u32[]{:S(2)}) %all-to-all-start.1) | async-done | bytes 2097184 | tf_op jit(solution)/shard_map/all_to_all | solution.py:283
  88.7 8.8 %shard_map.113 = (bf16[64,128,128]{2,1,0:T(8,128)(2,1)S(1)}, f32[1024,200]{1,0:T(8,128)S(1)}, f32[1024,200]{1,0:T(8,128)S(1)}) custom-call(s32[4]{0:T(128)S(1)} %pad_add_fusion.1.refs_0_.refs_1_.at_ref, bf16[64,128,128]{2,1,0:T(8,128)(2,1)} %all-to-all-done.1.refs_1_, s32[2,256]{1,0:T(2,128)S(1)} %get-tuple-element.55.refs_2_, ...), custom_call_target="tpu_custom_call" | custom-call | flops 4294967296 | bytes 4194304 | tf_op jit(solution)/shard_map/pallas_call | solution.py:355
  99.8 6.8 %all-to-all-start.2 = ((bf16[64,128,128]{2,1,0:T(8,128)(2,1)}), bf16[64,128,128]{2,1,0:T(8,128)(2,1)}, u32[]{:S(2)}, u32[]{:S(2)}) async-start(bf16[64,128,128]{2,1,0:T(8,128)(2,1)} %copy-done.8), calls=%async_computation.2 | async-start | bytes 4194304 | tf_op jit(solution)/shard_map/all_to_all | solution.py:283
  107.0 50.7 %all-to-all-done.2.refs_0_ = bf16[64,128,128]{2,1,0:T(8,128)(2,1)} async-done(((bf16[64,128,128]{2,1,0:T(8,128)(2,1)}), bf16[64,128,128]{2,1,0:T(8,128)(2,1)}, u32[]{:S(2)}, u32[]{:S(2)}) %all-to-all-start.2) | async-done | bytes 2097184 | tf_op jit(solution)/shard_map/all_to_all | solution.py:283
  159.3 8.2 %shard_map.114 = (f32[1,1024,400]{2,1,0:T(8,128)S(1)}, f32[8,128]{1,0:T(8,128)S(1)}, bf16[64,128,128]{2,1,0:T(8,128)(2,1)S(1)}) custom-call(bf16[64,128,128]{2,1,0:T(8,128)(2,1)} %all-to-all-done.2.refs_0_, s32[2,2560]{1,0:T(2,128)S(1)} %pad_add_fusion.refs_1_, f32[1,1024,400]{2,1,0:T(8,128)S(1)} %copy-done.5, f32[8,128]{1,0:T(8,128)S(1)} %bitcast.26, ...), custom_call_target="tpu_custom_call" | custom-call | flops 5368709120 | bytes 4194304 | tf_op jit(solution)/shard_map/pallas_call | solution.py:366
  170.2 6.0 %all-to-all-start.3 = ((bf16[64,128,128]{2,1,0:T(8,128)(2,1)}), bf16[64,128,128]{2,1,0:T(8,128)(2,1)}, u32[]{:S(2)}, u32[]{:S(2)}) async-start(bf16[64,128,128]{2,1,0:T(8,128)(2,1)} %copy-done.6), calls=%async_computation.3 | async-start | bytes 4194304 | tf_op jit(solution)/shard_map/all_to_all | solution.py:283
  189.4 4.0 collective-permute-done.1.refs_2_
  193.4 6.6 %collective-permute-done.2.refs_3_ = f32[256,200]{1,0:T(8,128)S(1)} collective-permute-done((f32[256,200]{1,0:T(8,128)S(1)}, f32[256,200]{1,0:T(8,128)S(1)}, u32[]{:S(2)}, u32[]{:S(2)}) %collective-permute-start.2) | collective-permute-done | bytes 204832 | tf_op jit(solution)/shard_map/ppermute | solution.py:301
  206.8 4.6 %collective-permute-done.5.refs_3_ = f32[64,200]{1,0:T(8,128)S(1)} collective-permute-done((f32[64,200]{1,0:T(8,128)S(1)}, f32[64,200]{1,0:T(8,128)S(1)}, u32[]{:S(2)}, u32[]{:S(2)}) %collective-permute-start.5) | collective-permute-done | bytes 51232 | tf_op jit(solution)/shard_map/ppermute | solution.py:302
  212.5 5.8 %collective-permute-start.10 = (f32[8,200]{1,0:T(8,128)S(1)}, f32[8,200]{1,0:T(8,128)S(1)}, u32[]{:S(2)}, u32[]{:S(2)}) collective-permute-start(f32[8,200]{1,0:T(8,128)S(1)} %get-tuple-element.73), channel_id=1, source_target_pairs={{0,32},{4,36},{8,40},{12,44},{16,48},{20,52},{24,56},{28,60},{32,0... | collective-permute-start | bytes 19208 | tf_op jit(solution)/shard_map/ppermute | solution.py:302
  222.1 5.2 %collective-permute-done.10.refs_5_ = f32[8,200]{1,0:T(8,128)S(1)} collective-permute-done((f32[8,200]{1,0:T(8,128)S(1)}, f32[8,200]{1,0:T(8,128)S(1)}, u32[]{:S(2)}, u32[]{:S(2)}) %collective-permute-start.10) | collective-permute-done | bytes 6432 | tf_op jit(solution)/shard_map/ppermute | solution.py:302
  228.2 3.7 collective-permute-done.8.refs_3_
  234.7 4.7 %collective-permute-start.16 = (f32[8,200]{1,0:T(8,128)S(1)}, f32[8,200]{1,0:T(8,128)S(1)}, u32[]{:S(2)}, u32[]{:S(2)}) collective-permute-start(f32[8,200]{1,0:T(8,128)S(1)} %shard_map.118.refs_1_), channel_id=1, source_target_pairs={{0,24},{4,28},{8,32},{12,36},{16,40},{20,44},{24,48},{28,52},{32,5... | collective-permute-start | bytes 19208 | tf_op jit(solution)/shard_map/ppermute | solution.py:302
  240.0 3.7 collective-permute-start.18
  261.6 3.8 collective-permute-done.25.refs_3_
  267.2 8.3 %collective-permute-start.27 = (f32[1024,200]{0,1:T(8,128)}, f32[1024,200]{0,1:T(8,128)}, u32[]{:S(2)}, u32[]{:S(2)}) collective-permute-start(f32[1024,200]{0,1:T(8,128)} %copy.28), channel_id=1, source_target_pairs={{0,4},{4,0},{8,12},{12,8},{16,20},{20,16},{24,28},{28,24},{32,36},... | collective-permute-start | bytes 2457608 | tf_op jit(solution)/shard_map/ppermute | solution.py:330
  286.2 10.1 %shard_map.123 = (bf16[64,128,128]{2,1,0:T(8,128)(2,1)}, f32[1024,200]{1,0:T(8,128)S(1)}, f32[1024,200]{1,0:T(8,128)S(1)}) custom-call(s32[4]{0:T(128)S(1)} %pad_add_fusion.1.refs_0_.refs_1_.at_ref, bf16[64,128,128]{2,1,0:T(8,128)(2,1)} %all-to-all-done.3.refs_1_, s32[2,256]{1,0:T(2,128)S(1)} %get-tuple-element.55.refs_2_, ...), custom_call_target="tpu_custom_call" | custom-call | flops 4294967296 | bytes 4194304 | tf_op jit(solution)/shard_map/pallas_call | solution.py:355
  296.3 8.2 %all-to-all-start.4 = ((bf16[64,128,128]{2,1,0:T(8,128)(2,1)}), bf16[64,128,128]{2,1,0:T(8,128)(2,1)}, u32[]{:S(2)}, u32[]{:S(2)}) async-start(bf16[64,128,128]{2,1,0:T(8,128)(2,1)} %get-tuple-element.78), calls=%async_computation.4 | async-start | bytes 4194304 | tf_op jit(solution)/shard_map/all_to_all | solution.py:283
  314.5 4.0 collective-permute-done.29.refs_2_
  318.4 6.5 %collective-permute-done.30.refs_3_ = f32[256,200]{1,0:T(8,128)S(1)} collective-permute-done((f32[256,200]{1,0:T(8,128)S(1)}, f32[256,200]{1,0:T(8,128)S(1)}, u32[]{:S(2)}, u32[]{:S(2)}) %collective-permute-start.30) | collective-permute-done | bytes 204832 | tf_op jit(solution)/shard_map/ppermute | solution.py:301
  331.9 6.1 %collective-permute-done.33.refs_3_ = f32[64,200]{1,0:T(8,128)S(1)} collective-permute-done((f32[64,200]{1,0:T(8,128)S(1)}, f32[64,200]{1,0:T(8,128)S(1)}, u32[]{:S(2)}, u32[]{:S(2)}) %collective-permute-start.33) | collective-permute-done | bytes 51232 | tf_op jit(solution)/shard_map/ppermute | solution.py:302
  340.2 3.7 collective-permute-start.37
  344.9 3.4 collective-permute-start.39
  350.2 3.0 collective-permute-start.40
  364.4 4.3 %collective-permute-start.46 = (f32[8,200]{1,0:T(8,128)S(1)}, f32[8,200]{1,0:T(8,128)S(1)}, u32[]{:S(2)}, u32[]{:S(2)}) collective-permute-start(f32[8,200]{1,0:T(8,128)S(1)} %shard_map.128.refs_1_), channel_id=1, source_target_pairs={{0,40},{4,44},{8,48},{12,52},{16,56},{20,60},{24,0},{28,4},{32,8},... | collective-permute-start | bytes 19208 | tf_op jit(solution)/shard_map/ppermute | solution.py:302
  387.1 3.7 collective-permute-done.53.refs_3_
  391.7 7.9 %collective-permute-start.55 = (f32[1024,200]{0,1:T(8,128)S(1)}, f32[1024,200]{0,1:T(8,128)S(1)}, u32[]{:S(2)}, u32[]{:S(2)}) collective-permute-start(f32[1024,200]{0,1:T(8,128)S(1)} %copy.32), channel_id=1, source_target_pairs={{0,4},{4,0},{8,12},{12,8},{16,20},{20,16},{24,28},{28,24},{32,36},... | collective-permute-start | bytes 2457608 | tf_op jit(solution)/shard_map/ppermute | solution.py:330
  409.6 5.9 %shard_map.124 = (f32[1,1024,400]{2,1,0:T(8,128)S(1)}, f32[8,128]{1,0:T(8,128)}) custom-call(bf16[64,128,128]{2,1,0:T(8,128)(2,1)} %all-to-all-done.4.refs_0_, s32[2,2560]{1,0:T(2,128)S(1)} %pad_add_fusion.refs_1_, f32[1,1024,400]{2,1,0:T(8,128)S(1)} %copy-done.17, f32[8,128]{1,0:T(8,128)S(1)} %get-tuple-element.80.refs_3_, s32[64,128]{1,0:T(8,128)S(1)} %bitcast.25), custom_call_target="tpu_custom_call" | custom-call | flops 5368709120 | bytes 4194304 | tf_op jit(solution)/shard_map/pallas_call | solution.py:366
  (176 shorter events, 140.0 us)
Async XLA Ops:
  4.4 22.4 %all-to-all-start = ((s32[64,1,128]{2,1,0:T(1,128)}), s32[64,1,128]{2,1,0:T(1,128)S(1)}, u32[]{:S(2)}, u32[]{:S(2)}) async-start(s32[64,1,128]{2,1,0:T(1,128)} %bitcast.5), calls=%async_computation | async-start | bytes 65536 | tf_op jit(solution)/shard_map/all_to_all | solution.py:283
  31.6 57.1 %all-to-all-start.1 = ((bf16[64,128,128]{2,1,0:T(8,128)(2,1)}), bf16[64,128,128]{2,1,0:T(8,128)(2,1)}, u32[]{:S(2)}, u32[]{:S(2)}) async-start(bf16[64,128,128]{2,1,0:T(8,128)(2,1)} %copy-done.7), calls=%async_computation.1 | async-start | bytes 4194304 | tf_op jit(solution)/shard_map/all_to_all | solution.py:283
  99.8 57.9 %all-to-all-start.2 = ((bf16[64,128,128]{2,1,0:T(8,128)(2,1)}), bf16[64,128,128]{2,1,0:T(8,128)(2,1)}, u32[]{:S(2)}, u32[]{:S(2)}) async-start(bf16[64,128,128]{2,1,0:T(8,128)(2,1)} %copy-done.8), calls=%async_computation.2 | async-start | bytes 4194304 | tf_op jit(solution)/shard_map/all_to_all | solution.py:283
  170.2 114.4 %all-to-all-start.3 = ((bf16[64,128,128]{2,1,0:T(8,128)(2,1)}), bf16[64,128,128]{2,1,0:T(8,128)(2,1)}, u32[]{:S(2)}, u32[]{:S(2)}) async-start(bf16[64,128,128]{2,1,0:T(8,128)(2,1)} %copy-done.6), calls=%async_computation.3 | async-start | bytes 4194304 | tf_op jit(solution)/shard_map/all_to_all | solution.py:283
  184.6 8.8 %collective-permute-start.1 = (f32[256,200]{1,0:T(8,128)S(1)}, f32[256,200]{1,0:T(8,128)S(1)}, u32[]{:S(2)}, u32[]{:S(2)}) collective-permute-start(f32[256,200]{1,0:T(8,128)S(1)} %get-tuple-element.62), channel_id=1, source_target_pairs={{0,1},{1,2},{2,3},{3,0},{4,5},{5,6},{6,7},{7,4},{8,9},{9,10},{10,1... | collective-permute-start | bytes 614408 | tf_op jit(solution)/shard_map/ppermute | solution.py:301
  185.8 14.2 %collective-permute-start.2 = (f32[256,200]{1,0:T(8,128)S(1)}, f32[256,200]{1,0:T(8,128)S(1)}, u32[]{:S(2)}, u32[]{:S(2)}) collective-permute-start(f32[256,200]{1,0:T(8,128)S(1)} %get-tuple-element.63), channel_id=1, source_target_pairs={{0,2},{1,3},{2,0},{3,1},{4,6},{5,7},{6,4},{7,5},{8,10},{9,11},{10,... | collective-permute-start | bytes 614408 | tf_op jit(solution)/shard_map/ppermute | solution.py:301
  188.3 11.8 %collective-permute-start.3 = (f32[256,200]{1,0:T(8,128)S(1)}, f32[256,200]{1,0:T(8,128)S(1)}, u32[]{:S(2)}, u32[]{:S(2)}) collective-permute-start(f32[256,200]{1,0:T(8,128)S(1)} %get-tuple-element.64), channel_id=1, source_target_pairs={{0,3},{1,0},{2,1},{3,2},{4,7},{5,4},{6,5},{7,6},{8,11},{9,8},{10,9... | collective-permute-start | bytes 614408 | tf_op jit(solution)/shard_map/ppermute | solution.py:301
  202.6 8.8 %collective-permute-start.5 = (f32[64,200]{1,0:T(8,128)S(1)}, f32[64,200]{1,0:T(8,128)S(1)}, u32[]{:S(2)}, u32[]{:S(2)}) collective-permute-start(f32[64,200]{1,0:T(8,128)S(1)} %get-tuple-element.67), channel_id=1, source_target_pairs={{0,128},{4,132},{8,136},{12,140},{16,144},{20,148},{24,152},{28,15... | collective-permute-start | bytes 153608 | tf_op jit(solution)/shard_map/ppermute | solution.py:302
  212.5 14.7 %collective-permute-start.10 = (f32[8,200]{1,0:T(8,128)S(1)}, f32[8,200]{1,0:T(8,128)S(1)}, u32[]{:S(2)}, u32[]{:S(2)}) collective-permute-start(f32[8,200]{1,0:T(8,128)S(1)} %get-tuple-element.73), channel_id=1, source_target_pairs={{0,32},{4,36},{8,40},{12,44},{16,48},{20,52},{24,56},{28,60},{32,0... | collective-permute-start | bytes 19208 | tf_op jit(solution)/shard_map/ppermute | solution.py:302
  218.4 8.9 %collective-permute-start.11 = (f32[8,200]{1,0:T(8,128)S(1)}, f32[8,200]{1,0:T(8,128)S(1)}, u32[]{:S(2)}, u32[]{:S(2)}) collective-permute-start(f32[8,200]{1,0:T(8,128)S(1)} %get-tuple-element.74), channel_id=1, source_target_pairs={{0,40},{4,44},{8,48},{12,52},{16,56},{20,60},{24,0},{28,4},{32,8},... | collective-permute-start | bytes 19208 | tf_op jit(solution)/shard_map/ppermute | solution.py:302
  218.6 9.6 %collective-permute-start.12 = (f32[8,200]{1,0:T(8,128)S(1)}, f32[8,200]{1,0:T(8,128)S(1)}, u32[]{:S(2)}, u32[]{:S(2)}) collective-permute-start(f32[8,200]{1,0:T(8,128)S(1)} %get-tuple-element.75), channel_id=1, source_target_pairs={{0,48},{4,52},{8,56},{12,60},{16,0},{20,4},{24,8},{28,12},{32,16},... | collective-permute-start | bytes 19208 | tf_op jit(solution)/shard_map/ppermute | solution.py:302
  219.6 8.6 %collective-permute-start.13 = (f32[8,200]{1,0:T(8,128)S(1)}, f32[8,200]{1,0:T(8,128)S(1)}, u32[]{:S(2)}, u32[]{:S(2)}) collective-permute-start(f32[8,200]{1,0:T(8,128)S(1)} %get-tuple-element.76), channel_id=1, source_target_pairs={{0,56},{4,60},{8,0},{12,4},{16,8},{20,12},{24,16},{28,20},{32,24},... | collective-permute-start | bytes 19208 | tf_op jit(solution)/shard_map/ppermute | solution.py:302
  233.4 10.3 %collective-permute-start.14 = (f32[8,200]{1,0:T(8,128)S(1)}, f32[8,200]{1,0:T(8,128)S(1)}, u32[]{:S(2)}, u32[]{:S(2)}) collective-permute-start(f32[8,200]{1,0:T(8,128)S(1)} %shard_map.118.refs_1_), channel_id=1, source_target_pairs={{0,8},{4,12},{8,16},{12,20},{16,24},{20,28},{24,32},{28,36},{32,40... | collective-permute-start | bytes 19208 | tf_op jit(solution)/shard_map/ppermute | solution.py:302
  233.8 9.9 %collective-permute-start.15 = (f32[8,200]{1,0:T(8,128)S(1)}, f32[8,200]{1,0:T(8,128)S(1)}, u32[]{:S(2)}, u32[]{:S(2)}) collective-permute-start(f32[8,200]{1,0:T(8,128)S(1)} %shard_map.118.refs_1_), channel_id=1, source_target_pairs={{0,16},{4,20},{8,24},{12,28},{16,32},{20,36},{24,40},{28,44},{32,4... | collective-permute-start | bytes 19208 | tf_op jit(solution)/shard_map/ppermute | solution.py:302
  234.7 10.5 %collective-permute-start.16 = (f32[8,200]{1,0:T(8,128)S(1)}, f32[8,200]{1,0:T(8,128)S(1)}, u32[]{:S(2)}, u32[]{:S(2)}) collective-permute-start(f32[8,200]{1,0:T(8,128)S(1)} %shard_map.118.refs_1_), channel_id=1, source_target_pairs={{0,24},{4,28},{8,32},{12,36},{16,40},{20,44},{24,48},{28,52},{32,5... | collective-permute-start | bytes 19208 | tf_op jit(solution)/shard_map/ppermute | solution.py:302
  256.3 9.0 %collective-permute-start.25 = (f32[256,200]{1,0:T(8,128)S(1)}, f32[256,200]{1,0:T(8,128)S(1)}, u32[]{:S(2)}, u32[]{:S(2)}) collective-permute-start(f32[256,200]{1,0:T(8,128)S(1)} %shard_map.120.refs_1_), channel_id=1, source_target_pairs={{0,2},{1,3},{2,0},{3,1},{4,6},{5,7},{6,4},{7,5},{8,10},{9,11},{10,... | collective-permute-start | bytes 614408 | tf_op jit(solution)/shard_map/ppermute | solution.py:301
  267.2 10.6 %collective-permute-start.27 = (f32[1024,200]{0,1:T(8,128)}, f32[1024,200]{0,1:T(8,128)}, u32[]{:S(2)}, u32[]{:S(2)}) collective-permute-start(f32[1024,200]{0,1:T(8,128)} %copy.28), channel_id=1, source_target_pairs={{0,4},{4,0},{8,12},{12,8},{16,20},{20,16},{24,28},{28,24},{32,36},... | collective-permute-start | bytes 2457608 | tf_op jit(solution)/shard_map/ppermute | solution.py:330
  296.3 111.7 %all-to-all-start.4 = ((bf16[64,128,128]{2,1,0:T(8,128)(2,1)}), bf16[64,128,128]{2,1,0:T(8,128)(2,1)}, u32[]{:S(2)}, u32[]{:S(2)}) async-start(bf16[64,128,128]{2,1,0:T(8,128)(2,1)} %get-tuple-element.78), calls=%async_computation.4 | async-start | bytes 4194304 | tf_op jit(solution)/shard_map/all_to_all | solution.py:283
  309.6 8.8 %collective-permute-start.29 = (f32[256,200]{1,0:T(8,128)S(1)}, f32[256,200]{1,0:T(8,128)S(1)}, u32[]{:S(2)}, u32[]{:S(2)}) collective-permute-start(f32[256,200]{1,0:T(8,128)S(1)} %get-tuple-element.86), channel_id=1, source_target_pairs={{0,1},{1,2},{2,3},{3,0},{4,5},{5,6},{6,7},{7,4},{8,9},{9,10},{10,1... | collective-permute-start | bytes 614408 | tf_op jit(solution)/shard_map/ppermute | solution.py:301
  311.4 13.6 %collective-permute-start.30 = (f32[256,200]{1,0:T(8,128)S(1)}, f32[256,200]{1,0:T(8,128)S(1)}, u32[]{:S(2)}, u32[]{:S(2)}) collective-permute-start(f32[256,200]{1,0:T(8,128)S(1)} %get-tuple-element.87), channel_id=1, source_target_pairs={{0,2},{1,3},{2,0},{3,1},{4,6},{5,7},{6,4},{7,5},{8,10},{9,11},{10,... | collective-permute-start | bytes 614408 | tf_op jit(solution)/shard_map/ppermute | solution.py:301
  313.2 11.8 %collective-permute-start.31 = (f32[256,200]{1,0:T(8,128)S(1)}, f32[256,200]{1,0:T(8,128)S(1)}, u32[]{:S(2)}, u32[]{:S(2)}) collective-permute-start(f32[256,200]{1,0:T(8,128)S(1)} %get-tuple-element.88), channel_id=1, source_target_pairs={{0,3},{1,0},{2,1},{3,2},{4,7},{5,4},{6,5},{7,6},{8,11},{9,8},{10,9... | collective-permute-start | bytes 614408 | tf_op jit(solution)/shard_map/ppermute | solution.py:301
  327.5 10.6 %collective-permute-start.33 = (f32[64,200]{1,0:T(8,128)S(1)}, f32[64,200]{1,0:T(8,128)S(1)}, u32[]{:S(2)}, u32[]{:S(2)}) collective-permute-start(f32[64,200]{1,0:T(8,128)S(1)} %get-tuple-element.91), channel_id=1, source_target_pairs={{0,128},{4,132},{8,136},{12,140},{16,144},{20,148},{24,152},{28,15... | collective-permute-start | bytes 153608 | tf_op jit(solution)/shard_map/ppermute | solution.py:302
  339.3 10.9 %collective-permute-start.35 = (f32[8,200]{1,0:T(8,128)S(1)}, f32[8,200]{1,0:T(8,128)S(1)}, u32[]{:S(2)}, u32[]{:S(2)}) collective-permute-start(f32[8,200]{1,0:T(8,128)S(1)} %get-tuple-element.94), channel_id=1, source_target_pairs={{0,8},{4,12},{8,16},{12,20},{16,24},{20,28},{24,32},{28,36},{32,40... | collective-permute-start | bytes 19208 | tf_op jit(solution)/shard_map/ppermute | solution.py:302
  339.3 14.0 %collective-permute-start.36 = (f32[8,200]{1,0:T(8,128)S(1)}, f32[8,200]{1,0:T(8,128)S(1)}, u32[]{:S(2)}, u32[]{:S(2)}) collective-permute-start(f32[8,200]{1,0:T(8,128)S(1)} %get-tuple-element.95), channel_id=1, source_target_pairs={{0,16},{4,20},{8,24},{12,28},{16,32},{20,36},{24,40},{28,44},{32,4... | collective-permute-start | bytes 19208 | tf_op jit(solution)/shard_map/ppermute | solution.py:302
  340.2 16.0 %collective-permute-start.37 = (f32[8,200]{1,0:T(8,128)S(1)}, f32[8,200]{1,0:T(8,128)S(1)}, u32[]{:S(2)}, u32[]{:S(2)}) collective-permute-start(f32[8,200]{1,0:T(8,128)S(1)} %get-tuple-element.96), channel_id=1, source_target_pairs={{0,24},{4,28},{8,32},{12,36},{16,40},{20,44},{24,48},{28,52},{32,5... | collective-permute-start | bytes 19208 | tf_op jit(solution)/shard_map/ppermute | solution.py:302
  343.9 12.7 %collective-permute-start.38 = (f32[8,200]{1,0:T(8,128)S(1)}, f32[8,200]{1,0:T(8,128)S(1)}, u32[]{:S(2)}, u32[]{:S(2)}) collective-permute-start(f32[8,200]{1,0:T(8,128)S(1)} %get-tuple-element.97), channel_id=1, source_target_pairs={{0,32},{4,36},{8,40},{12,44},{16,48},{20,52},{24,56},{28,60},{32,0... | collective-permute-start | bytes 19208 | tf_op jit(solution)/shard_map/ppermute | solution.py:302
  344.9 11.6 %collective-permute-start.39 = (f32[8,200]{1,0:T(8,128)S(1)}, f32[8,200]{1,0:T(8,128)S(1)}, u32[]{:S(2)}, u32[]{:S(2)}) collective-permute-start(f32[8,200]{1,0:T(8,128)S(1)} %get-tuple-element.98), channel_id=1, source_target_pairs={{0,40},{4,44},{8,48},{12,52},{16,56},{20,60},{24,0},{28,4},{32,8},... | collective-permute-start | bytes 19208 | tf_op jit(solution)/shard_map/ppermute | solution.py:302
  357.5 11.2 %collective-permute-start.42 = (f32[8,200]{1,0:T(8,128)S(1)}, f32[8,200]{1,0:T(8,128)S(1)}, u32[]{:S(2)}, u32[]{:S(2)}) collective-permute-start(f32[8,200]{1,0:T(8,128)S(1)} %shard_map.128.refs_1_), channel_id=1, source_target_pairs={{0,8},{4,12},{8,16},{12,20},{16,24},{20,28},{24,32},{28,36},{32,40... | collective-permute-start | bytes 19208 | tf_op jit(solution)/shard_map/ppermute | solution.py:302
  357.6 11.8 %collective-permute-start.43 = (f32[8,200]{1,0:T(8,128)S(1)}, f32[8,200]{1,0:T(8,128)S(1)}, u32[]{:S(2)}, u32[]{:S(2)}) collective-permute-start(f32[8,200]{1,0:T(8,128)S(1)} %shard_map.128.refs_1_), channel_id=1, source_target_pairs={{0,16},{4,20},{8,24},{12,28},{16,32},{20,36},{24,40},{28,44},{32,4... | collective-permute-start | bytes 19208 | tf_op jit(solution)/shard_map/ppermute | solution.py:302
  359.5 9.9 %collective-permute-start.44 = (f32[8,200]{1,0:T(8,128)S(1)}, f32[8,200]{1,0:T(8,128)S(1)}, u32[]{:S(2)}, u32[]{:S(2)}) collective-permute-start(f32[8,200]{1,0:T(8,128)S(1)} %shard_map.128.refs_1_), channel_id=1, source_target_pairs={{0,24},{4,28},{8,32},{12,36},{16,40},{20,44},{24,48},{28,52},{32,5... | collective-permute-start | bytes 19208 | tf_op jit(solution)/shard_map/ppermute | solution.py:302
  382.4 8.4 %collective-permute-start.53 = (f32[256,200]{1,0:T(8,128)S(1)}, f32[256,200]{1,0:T(8,128)S(1)}, u32[]{:S(2)}, u32[]{:S(2)}) collective-permute-start(f32[256,200]{1,0:T(8,128)S(1)} %shard_map.130.refs_1_), channel_id=1, source_target_pairs={{0,2},{1,3},{2,0},{3,1},{4,6},{5,7},{6,4},{7,5},{8,10},{9,11},{10,... | collective-permute-start | bytes 614408 | tf_op jit(solution)/shard_map/ppermute | solution.py:301
  391.7 9.8 %collective-permute-start.55 = (f32[1024,200]{0,1:T(8,128)S(1)}, f32[1024,200]{0,1:T(8,128)S(1)}, u32[]{:S(2)}, u32[]{:S(2)}) collective-permute-start(f32[1024,200]{0,1:T(8,128)S(1)} %copy.32), channel_id=1, source_target_pairs={{0,4},{4,0},{8,12},{12,8},{16,20},{20,16},{24,28},{28,24},{32,36},... | collective-permute-start | bytes 2457608 | tf_op jit(solution)/shard_map/ppermute | solution.py:330
  (48 other events, 303.8 us)

commit v3 on v1

--- a/solution.py
+++ b/solution.py
@@ -14,6 +14,8 @@
 HALF = 200
 BODY = 384
 REL = 1024
+DENSE = REL // 64 * 200
+WIRE_PARTS = 4
 
 
 def iota(shape, dim):
@@ -61,14 +63,40 @@
     return jnp.concatenate([block[:40], block[40:80], block[80:120], tail], axis=1)
 
 
-def unpack_all(wire_ref, rows_ref):
-    def pair(e, _):
-        two = [unpack(wire_ref[2 * e + k].astype(F32)) for k in range(2)]
-        at = pl.multiple_of(e * 2 * CAP, 2 * CAP)
-        rows_ref[pl.ds(at, 2 * CAP), :] = jnp.concatenate(two, axis=0).astype(BF16)
-        return 0
-
-    lax.fori_loop(0, OWN // 2, pair, 0)
+def pack_relations(rows):
+    group = iota((8, 128), 1) // 16
+    tail = jnp.zeros((8, 128), F32)
+    for i in range(8):
+        tail = jnp.where(group == i, rows[8 * i : 8 * i + 8, BODY:], tail)
+    return jnp.concatenate([rows[:, :128], rows[:, 128:256], rows[:, 256:384], tail], axis=0)
+
+
+def unpack_relations(dense):
+    group = iota((8, 128), 1) // 16
+    tail = jnp.concatenate([jnp.where(group == i, dense[192:], 0.0) for i in range(8)], axis=0)
+    return to_narrow(jnp.concatenate([dense[:64], dense[64:128], dense[128:192], tail], axis=1))
+
+
+def wire_copies(wire_ref, held_ref, sems):
+    per = OWN // WIRE_PARTS
+    return [
+        pltpu.make_async_copy(wire_ref.at[pl.ds(per * g, per)], held_ref.at[pl.ds(per * g, per)], sems.at[g])
+        for g in range(WIRE_PARTS)
+    ]
+
+
+def unpack_all(copies, held_ref, rows_ref):
+    per = OWN // WIRE_PARTS // 2
+    for g, copy in enumerate(copies):
+        copy.wait()
+
+        def pair(e, _):
+            two = [unpack(held_ref[2 * e + k].astype(F32)) for k in range(2)]
+            at = pl.multiple_of(e * 2 * CAP, 2 * CAP)
+            rows_ref[pl.ds(at, 2 * CAP), :] = jnp.concatenate(two, axis=0).astype(BF16)
+            return 0
+
+        lax.fori_loop(per * g, per * g + per, pair, 0)
 
 
 def lane_to_column(row):
@@ -108,29 +136,47 @@
     negative_ref[...] = negative
 
 
-def gather_rows(named_ref, step, wide_ref, wire_ref):
+def gather_rows(named_ref, step, wide_ref, wire_ref, held_ref, sems):
     named = named_ref[...].astype(F32)
     named = jnp.transpose(jnp.concatenate([named, named], axis=0))
     named = named[CAP * step : CAP * step + CAP, :OWN].astype(I32)
-    for g in range(OWN // 8):
-        columns = jnp.concatenate([named[:, 8 * g + j : 8 * g + j + 1] for j in range(8)], axis=0)
-        hit = one_hot(columns == iota((8 * CAP, 1024), 1))
+    per = OWN // 8
+    copies = []
+    for g in range(8):
+        columns = jnp.concatenate([named[:, per * g + j : per * g + j + 1] for j in range(per)], axis=0)
+        hit = one_hot(columns == iota((per * CAP, 1024), 1))
         rows = dot(hit, wide_ref[...])
-        for j in range(8):
-            wire_ref[8 * g + j] = pack(rows[CAP * j : CAP * j + CAP]).astype(BF16)
-
-
-def first_rows(table_ref, named_ref, wire_ref, wide_ref):
+        for j in range(per):
+            held_ref[per * g + j] = pack(rows[CAP * j : CAP * j + CAP]).astype(BF16)
+        here = pl.ds(per * g, per)
+        copies.append(pltpu.make_async_copy(held_ref.at[here], wire_ref.at[here], sems.at[g]))
+        copies[-1].start()
+    for copy in copies:
+        copy.wait()
+
+
+def widen(table_ref, wide_ref):
     wide_ref[...] = to_wide(table_ref[0]).astype(BF16)
-    gather_rows(named_ref, 0, wide_ref, wire_ref)
-
-
-def update(step, last, wire_in_ref, flat_ref, table_ref, accum_ref, named_ref, *rest):
+
+
+def first_rows(wide_ref, named_ref, wire_ref, held_ref, sems):
+    gather_rows(named_ref, 0, wide_ref, wire_ref, held_ref, sems)
+
+
+def update(step, last, wire_in_ref, flat_ref, table_ref, accum_ref, named_ref, _, *rest):
     if last:
-        new_table_ref, new_accum_ref, grads_ref = rest
+        new_table_ref, new_accum_ref, in_sems, table_sem, out_sems, held_ref, rows_ref, grads_ref = rest
     else:
-        new_table_ref, new_accum_ref, wire_ref, grads_ref, wide_ref = rest
-    unpack_all(wire_in_ref, grads_ref)
+        new_table_ref, new_accum_ref, wire_ref, in_sems, table_sem, out_sems, held_ref, rows_ref, grads_ref, *rest = rest
+        wide_ref, sent_ref, sent_sems = rest
+    copies = wire_copies(wire_in_ref, held_ref, in_sems)
+    for copy in copies:
+        copy.start()
+    table_copy = pltpu.make_async_copy(table_ref.at[0], rows_ref, table_sem)
+    table_copy.start()
+    unpack_all(copies, held_ref, grads_ref)
+    table_copy.wait()
+    outs = []
     for b in range(8):
         rows = slice(128 * b, 128 * b + 128)
         hit = one_hot(iota((128, SLOTS), 0) + 128 * b == flat_ref[step : step + 1, :])
@@ -139,12 +185,17 @@
         accum = lane_to_column(accum_ref[b : b + 1, :])
         accum = accum + jnp.sum(total * total, axis=1, keepdims=True) / WIDTH
         new_accum_ref[b : b + 1, :] = jnp.transpose(accum)[:1]
-        new = table_ref[0, rows, :] - total * (RATE * lax.rsqrt(accum[:, :1]))
-        new_table_ref[0, rows, :] = new
+        new = rows_ref[rows, :] - total * (RATE * lax.rsqrt(accum[:, :1]))
+        rows_ref[rows, :] = new
+        here = pl.ds(128 * b, 128)
+        outs.append(pltpu.make_async_copy(rows_ref.at[here], new_table_ref.at[0, here], out_sems.at[b]))
+        outs[-1].start()
         if not last:
             wide_ref[rows, :] = to_wide(new).astype(BF16)
     if not last:
-        gather_rows(named_ref, step + 1, wide_ref, wire_ref)
+        gather_rows(named_ref, step + 1, wide_ref, wire_ref, sent_ref, sent_sems)
+    for copy in outs:
+        copy.wait()
 
 
 def complex_parts(x):
@@ -162,14 +213,24 @@
     return a, b, (x - b.astype(F32)).astype(BF16)
 
 
+def relation_rows(step, table_ref, rel_ids_ref, out_ref):
+    rel_ids = rel_ids_ref[0, step : step + 1, :]
+    column = lane_to_column(rel_ids.astype(F32))[:, :1].astype(I32)
+    hit = one_hot(column == iota((rel_ids.shape[1], REL), 1))
+    out_ref[...] = sum(dot(hit, piece) for piece in reversed(split3(table_ref[...])))
+
+
 def block(
-    step, wire_in_ref, slots_ref, negative_ref, relations_ref, rel_ids_ref,
-    wire_ref, relation_grad_ref, rows_ref, weights_ref,
+    step, at_ref, wire_in_ref, slots_ref, negative_ref, relation_ref, rel_ids_ref,
+    wire_ref, keep_ref, give_ref, rows_ref, weights_ref, held_ref, in_sems, sent_ref, out_sems,
 ):
     edges, parts = 128, 4
     part = SLOTS // parts
     per = OWN // parts
-    unpack_all(wire_in_ref, rows_ref)
+    copies = wire_copies(wire_in_ref, held_ref, in_sems)
+    for copy in copies:
+        copy.start()
+    unpack_all(copies, held_ref, rows_ref)
     slots = slots_ref[step : step + 1, :]
     slots_column = jnp.concatenate(
         [lane_to_column(slots[:, 128 * k : 128 * k + 128].astype(F32))[:, :1] for k in range(2)], axis=0
@@ -180,16 +241,9 @@
         fetched = fetched + dot(hit, rows_ref[part * g : part * g + part, :])
     fetched = to_narrow(fetched)
     head, tail = fetched[:edges], fetched[edges:]
-    rel_ids = rel_ids_ref[0, step : step + 1, :]
-    rel_column = lane_to_column(rel_ids.astype(F32))[:, :1].astype(I32)
-    rel_hit = one_hot(rel_column == iota((edges, REL), 1))
-    relation = jnp.zeros((edges, WIDTH), F32)
-    for piece in reversed(split3(relations_ref[...])):
-        relation = relation + dot(rel_hit, piece)
-
     head_re, head_im = complex_parts(head)
     tail_re, tail_im = complex_parts(tail)
-    rel_re, rel_im = complex_parts(relation)
+    rel_re, rel_im = complex_parts(relation_ref[...])
     query_tail = join(head_re * rel_re - head_im * rel_im, head_re * rel_im + head_im * rel_re)
     query_head = join(rel_re * tail_re + rel_im * tail_im, rel_re * tail_im - rel_im * tail_re)
     positive = jnp.sum(query_tail * tail, axis=1, keepdims=True)
@@ -210,92 +264,240 @@
     grad_tail = positive_weight * query_tail + join(
         push_re * rel_re - push_im * rel_im, push_re * rel_im + push_im * rel_re
     )
-    grad_relation = join(
-        pull_re * head_re + pull_im * head_im + push_re * tail_re + push_im * tail_im,
-        pull_im * head_re - pull_re * head_im + push_re * tail_im - push_im * tail_re,
-    )
-    rel_spread = one_hot(iota((REL, edges), 0) == rel_ids)
-    relation_grad = jnp.zeros((REL, WIDTH), F32)
-    for piece in reversed(split3(grad_relation)):
-        relation_grad = relation_grad + dot(rel_spread, piece)
-    relation_grad_ref[...] = relation_grad
     edge_grads = to_wide(jnp.concatenate([grad_head, grad_tail], axis=0)).astype(BF16)
+    outs = []
     for g in range(parts):
         here = slice(part * g, part * g + part)
         grads = dot(weights_ref[:, here], queries, ((0,), (0,)))
         hit = one_hot(iota((part, 2 * edges), 0) + part * g == slots)
         grads = grads + dot(hit, edge_grads)
         for j in range(per):
-            wire_ref[per * g + j] = pack(grads[CAP * j : CAP * j + CAP]).astype(BF16)
-
-
-def relation_update(grad_ref, table_ref, state_ref, new_table_ref, new_state_ref):
-    for b in range(REL // 128):
+            sent_ref[per * g + j] = pack(grads[CAP * j : CAP * j + CAP]).astype(BF16)
+        blocks = pl.ds(per * g, per)
+        outs.append(pltpu.make_async_copy(sent_ref.at[blocks], wire_ref.at[blocks], out_sems.at[g]))
+        outs[-1].start()
+    grad_relation = to_wide(
+        join(
+            pull_re * head_re + pull_im * head_im + push_re * tail_re + push_im * tail_im,
+            pull_im * head_re - pull_re * head_im + push_re * tail_im - push_im * tail_re,
+        )
+    )
+    high = grad_relation.astype(BF16)
+    low = (grad_relation - high.astype(F32)).astype(BF16)
+    rel_ids = rel_ids_ref[0, step : step + 1, :]
+    half = REL // 128
+    for i in range(half):
+        dense = []
+        for k in range(2):
+            hit = one_hot(iota((64, edges), 0) + 64 * (half * k + i) == rel_ids)
+            dense.append(pack_relations(dot(hit, high) + dot(hit, low)))
+        here = slice(200 * i, 200 * i + 200)
+        keep_ref[here, :] = jnp.where(at_ref[3] == 0, dense[0], dense[1])
+        give_ref[here, :] = jnp.where(at_ref[3] == 0, dense[1], dense[0])
+    for copy in outs:
+        copy.wait()
+
+
+def scatter_stage(axis, at_ref, own_ref, *refs):
+    n = (4, 4)[axis]
+    arrived, outs, sum_ref = refs[: -n - 1], refs[-n - 1 : -1], refs[-1]
+    total = own_ref[...].astype(F32)
+    for ref in arrived:
+        total = total + ref[...].astype(F32)
+    sum_ref[: total.shape[0], :] = total
+    rows = outs[0].shape[0]
+    if total.shape[0] < n * rows:
+        sum_ref[total.shape[0] :, :] = jnp.zeros((n * rows - total.shape[0], 128), F32)
+    for d in range(n):
+        start = pl.multiple_of(lax.rem(at_ref[axis] + d, n) * rows, 8)
+        outs[d][...] = sum_ref[pl.ds(start, rows), :].astype(outs[d].dtype)
+
+
+def sum_stage(*refs):
+    *parts, out_ref = refs
+    total = parts[0][...]
+    for ref in parts[1:]:
+        total = total + ref[...]
+    out_ref[...] = total
+
+
+def gather_y(at_ref, *refs):
+    *parts, out_ref, all_ref = refs
+    rows = parts[0].shape[0]
+    for d in range(4):
+        start = pl.multiple_of(lax.rem(at_ref[1] + 4 - d, 4) * rows, 8)
+        all_ref[pl.ds(start, rows), :] = parts[d][...]
+    out_ref[...] = all_ref[: out_ref.shape[0], :].astype(BF16)
+
+
+def gather_x(at_ref, _, *refs):
+    *parts, out_ref = refs
+    rows = parts[0].shape[0]
+    for d in range(4):
+        start = pl.multiple_of(lax.rem(at_ref[0] + 4 - d, 4) * rows, 16)
+        out_ref[pl.ds(start, rows), :] = parts[d][...]
+
+
+def relation_update(at_ref, mine_ref, other_ref, table_ref, state_ref, new_table_ref, new_state_ref):
+    count = REL // 128
+    for b in range(count):
         rows = slice(128 * b, 128 * b + 128)
-        total = grad_ref[rows, :]
+        here = slice(400 * (b % (count // 2)), 400 * (b % (count // 2)) + 400)
+        mine, other = mine_ref[here, :].astype(F32), other_ref[here, :].astype(F32)
+        dense = jnp.where(at_ref[3] == b // (count // 2), mine, other)
+        total = jnp.concatenate([unpack_relations(dense[:200]), unpack_relations(dense[200:])], axis=0)
         state = lane_to_column(state_ref[b : b + 1, :])
         state = state + jnp.sum(total * total, axis=1, keepdims=True) / WIDTH
         new_state_ref[b : b + 1, :] = jnp.transpose(state)[:1]
         new_table_ref[rows, :] = table_ref[rows, :] - total * (RATE * lax.rsqrt(state[:, :1]))
 
 
-def kernel(body, outs, scratch=(), flops=0, nbytes=4 << 20):
-    return pl.pallas_call(
+SPACES = {
+    "s": pl.BlockSpec(memory_space=pltpu.SMEM),
+    "v": pl.BlockSpec(memory_space=pltpu.VMEM),
+    "h": pl.BlockSpec(memory_space=pltpu.HBM),
+    "a": pl.BlockSpec(memory_space=pl.ANY),
+}
+
+
+def kernel(body, ins, outs, places, scratch=(), flops=0):
+    call = pl.pallas_call(
         body,
-        out_shape=outs,
+        out_shape=[pltpu.HBM(o.shape, o.dtype) if k == "h" else o for o, k in zip(outs, places)],
+        in_specs=[SPACES[k] for k in ins],
+        out_specs=[SPACES[k] for k in places],
         scratch_shapes=scratch,
         compiler_params=pltpu.CompilerParams(vmem_limit_bytes=40 << 20),
-        cost_estimate=pl.CostEstimate(flops=flops, bytes_accessed=nbytes, transcendentals=0),
+        cost_estimate=pl.CostEstimate(flops=flops, bytes_accessed=1 << 20, transcendentals=0),
     )
+    return lambda *args: call(
+        *[pltpu.with_memory_space_constraint(x, pltpu.HBM) if k == "h" else x for x, k in zip(args, ins)]
+    )
+
+
+def copies(n):
+    return pltpu.SemaphoreType.DMA((n,))
 
 
 def exchange(x):
     return lax.all_to_all(x, "edge", split_axis=0, concat_axis=0, tiled=True)
 
 
-def relation_sum(grad):
-    part = lax.psum_scatter(grad, "rep", scatter_dimension=0, tiled=True)
-    rows = part.shape[0] // OWN
-    mine = jnp.sum(exchange(part.reshape(OWN, rows, WIDTH)), axis=0)
-    part = exchange(jnp.broadcast_to(mine[None], (OWN, rows, WIDTH))).reshape(OWN * rows, WIDTH)
-    return lax.all_gather(part, "rep", axis=0, tiled=True)
+def edge_of(y, z, core):
+    return (y * 8 + z) * 2 + core
+
+
+def edge_pairs(dy, dz, flip=0):
+    return [
+        (edge_of(y, z, core), edge_of((y + dy) % 4, (z + dz) % 8, core ^ flip))
+        for y in range(4)
+        for z in range(8)
+        for core in range(2)
+    ]
+
+
+def move(x, axis, d):
+    if axis == 0:
+        return lax.ppermute(x, "rep", [(k, (k + d) % 4) for k in range(4)])
+    return lax.ppermute(x, "edge", edge_pairs(d if axis == 1 else 0, d if axis == 2 else 0))
+
+
+def doubled(x, bit):
+    pairs = [
+        (edge_of(y, z, core), edge_of(y, z ^ bit, core)) for y in range(4) for z in range(8) for core in range(2)
+    ]
+    return kernel(sum_stage, "vv", [jax.ShapeDtypeStruct(x.shape, F32)], "v")(x, lax.ppermute(x, "edge", pairs))[0]
+
+
+def relation_scatter(at, keep, give):
+    shape = jax.ShapeDtypeStruct
+    arrived = [lax.ppermute(give, "edge", edge_pairs(0, 0, 1))]
+    own = keep
+    for axis, (rows, sent) in enumerate(((DENSE // 8, BF16), (104, F32))):
+        own, *parts = kernel(
+            lambda *refs, axis=axis: scatter_stage(axis, *refs),
+            "sv" + "v" * len(arrived),
+            [shape((rows, 128), F32)] + [shape((rows, 128), sent)] * 3,
+            "vvvv",
+            [pltpu.VMEM((4 * rows, 128), F32)],
+        )(at, own, *arrived)
+        arrived = [move(part, axis, d + 1) for d, part in enumerate(parts)]
+    own = kernel(sum_stage, "vvvv", [shape(own.shape, F32)], "v")(own, *arrived)[0]
+    for bit in (1, 2, 4):
+        own = doubled(own, bit)
+    return own
+
+
+def relation_gather_y(at, own):
+    return kernel(
+        gather_y, "svvvv", [jax.ShapeDtypeStruct((DENSE // 8, 128), BF16)], "v", [pltpu.VMEM((416, 128), F32)]
+    )(at, own, *[move(own, 1, d) for d in (1, 2, 3)])[0]
+
+
+def relation_gather_x(at, own, after):
+    own = kernel(gather_x, "savvvv", [jax.ShapeDtypeStruct((DENSE // 2, 128), BF16)], "v")(
+        at, after, own, *[move(own, 0, d) for d in (1, 2, 3)]
+    )[0]
+    return own, lax.ppermute(own, "edge", edge_pairs(0, 0, 1))
 
 
 def shards(entities, ent_accum, relations, rel_accum, heads, tails, negatives, rel_ids):
     steps = heads.shape[1]
     shape = jax.ShapeDtypeStruct
     wire = shape((OWN, 128, 128), BF16)
+    held = pltpu.VMEM((OWN, 128, 128), BF16)
     table, accum = entities, ent_accum.reshape(8, 128)
     rel_count = relations.shape[0]
     rel_table = jnp.pad(relations, ((0, REL - rel_count), (0, 0)))
     rel_state = jnp.pad(rel_accum, (0, REL - rel_count), constant_values=1.0).reshape(8, 128)
+    edge = lax.axis_index("edge")
+    at = jnp.stack([lax.axis_index("rep"), edge // 16, edge // 2 % 8, edge % 2]).astype(I32)
     send, negative, slots = kernel(
-        prepare, (shape((OWN, 128), I32), shape((OWN, 128), F32), shape((steps, 256), I32))
+        prepare, "vvv", [shape((OWN, 128), I32), shape((OWN, 128), F32), shape((steps, 256), I32)], "vvv"
     )(heads, tails, negatives)
     named = exchange(send.reshape(OWN, 1, 128)).reshape(OWN, 128)
+    wide = kernel(widen, "v", [shape((1024, 512), BF16)], "v")(table)[0]
     flat = jnp.stack([named[:, CAP * s : CAP * s + CAP].reshape(SLOTS) for s in range(steps)])
     negative = jnp.stack([negative[:, CAP * s : CAP * s + CAP].reshape(SLOTS) for s in range(steps)])
-    rows = kernel(first_rows, wire, [pltpu.VMEM((1024, 512), BF16)], 3 << 30)(table, named)
+    rows = kernel(first_rows, "vv", [wire], "h", [held, copies(8)], 3 << 30)(wide, named)[0]
     for s in range(steps):
         last = s == steps - 1
+        relation = kernel(
+            lambda *refs, s=s: relation_rows(s, *refs), "vv", [shape((128, WIDTH), F32)], "v"
+        )(rel_table, rel_ids)[0]
         rows = exchange(rows)
-        grads, relation_grad = kernel(
+        dense = shape((DENSE // 2, 128), F32)
+        grads, keep, give = kernel(
             lambda *refs, s=s: block(s, *refs),
-            (wire, shape((REL, WIDTH), F32)),
-            [pltpu.VMEM((SLOTS, 512), BF16), pltpu.VMEM((256, SLOTS), BF16)],
+            "shvvvv",
+            [wire, dense, dense],
+            "hvv",
+            [pltpu.VMEM((SLOTS, 512), BF16), pltpu.VMEM((256, SLOTS), BF16), held, copies(WIRE_PARTS), held, copies(4)],
             4 << 30,
-        )(rows, slots, negative, rel_table, rel_ids)
+        )(at, rows, slots, negative, relation, rel_ids)
         grads = exchange(grads)
-        relation_total = relation_sum(relation_grad)
-        outs = (shape(table.shape, F32), shape((8, 128), F32)) + (() if last else (wire,))
-        scratch = [pltpu.VMEM((SLOTS, 512), BF16)] + ([] if last else [pltpu.VMEM((1024, 512), BF16)])
+        own = relation_scatter(at, keep, give)
+        if last:
+            own = relation_gather_y(at, own)
+        scratch = [copies(WIRE_PARTS), pltpu.SemaphoreType.DMA, copies(8), held]
+        scratch += [pltpu.VMEM((1024, WIDTH), F32), pltpu.VMEM((SLOTS, 512), BF16)]
+        if not last:
+            scratch += [pltpu.VMEM((1024, 512), BF16), held, copies(8)]
         table, accum, *rows = kernel(
-            lambda *refs, s=s, last=last: update(s, last, *refs), outs, scratch, 5 << 30
-        )(grads, flat, table, accum, named)
+            lambda *refs, s=s, last=last: update(s, last, *refs),
+            "hvhvva",
+            [shape(table.shape, F32), shape((8, 128), F32)] + ([] if last else [wire]),
+            "hv" if last else "hvh",
+            scratch,
+            5 << 30,
+        )(grads, flat, table, accum, named, own)
         rows = None if last else rows[0]
+        if not last:
+            own = relation_gather_y(at, own)
+        mine, other = relation_gather_x(at, own, accum)
         rel_table, rel_state = kernel(
-            relation_update, (shape((REL, WIDTH), F32), shape((8, 128), F32))
-        )(relation_total, rel_table, rel_state)
+            relation_update, "svvvv", [shape((REL, WIDTH), F32), shape((8, 128), F32)], "vv"
+        )(at, mine, other, rel_table, rel_state)
     return table, accum.reshape(1, 1024), rel_table[:rel_count], rel_state.reshape(REL)[:rel_count]
 
 

time: 482 us -> 352 us (0.73)
  waiting for transfers between devices: 261 us -> 172 us
  blocking collectives: 78.9 us -> 0 us
  starting transfers between devices: 45.4 us -> 101 us
  local copies, waits for them, and re-layouts: 36.7 us -> 16.6 us
  Pallas kernels: 39 us -> 55.4 us
  between operations: 14.3 us -> 1.31 us
    ppermute x0 -> x34, waiting for transfers between devices: none -> 97.7 us  [the longest x6 67.6 us: doubled(): lax.ppermute(x, 'edge', pairs)]
    all_to_all x6 -> x5, waiting for transfers between devices: 170 us -> 74.1 us  [exchange(): return lax.all_to_all(x, 'edge', split_axis=0, concat_axis=0, tiled=True)]
    all_to_all x3 -> x0, blocking collectives: 78.9 us -> none  [exchange(): return lax.all_to_all(x, 'edge', split_axis=0, concat_axis=0, tiled=True)]
    ppermute x0 -> x34, starting transfers between devices: none -> 59.1 us  [the longest x12 20.7 us: move(): lax.ppermute(x, 'edge', edge_pairs(d if axis == 1 else 0, d if axis == 2...]
    reduce_scatter x2 -> x0, waiting for transfers between devices: 56.2 us -> none  [relation_sum(): part = lax.psum_scatter(grad, 'rep', scatter_dimension=0, tiled=True)]
    all_gather x2 -> x0, waiting for transfers between devices: 34.9 us -> none  [relation_sum(): return lax.all_gather(part, 'rep', axis=0, tiled=True)]
    pallas_call x8 -> x27, Pallas kernels: 39 us -> 55.4 us  [kernel(): call(*[pltpu.with_memory_space_constraint(x, pltpu.HBM) if k == 'h' else...]
    unnamed x44 -> x26, local copies, waits for them, and re-layouts: 28.9 us -> 14.2 us
  transfers between devices with their start and end apart: 10 -> 39, of which waited for: 9 -> 26; matrix products, arithmetic and copies ran while one was open for 3% -> 3% of each run, Pallas kernels for 3% -> 5%
where the time goes in v3:
time: 352 us; the launch traced here: 347 us
  waiting for transfers between devices  172 us (49%)
  starting transfers between devices  101 us (29%)
  Pallas kernels  55.4 us (16%)
  local copies, waits for them, and re-layouts  16.6 us (5%)
    all_to_all x5, waiting for transfers between devices, exchange(): return lax.all_to_all(x, 'edge', split_axis=0, concat_axis=0, tiled=True)  74.1 us
    ppermute x6, waiting for transfers between devices, doubled(): lax.ppermute(x, 'edge', pairs)  67.6 us
    pallas_call x27, Pallas kernels, kernel(): call(*[pltpu.with_memory_space_constraint(x, pltpu.HBM) if k == 'h' else...  55.4 us
    all_to_all x5, starting transfers between devices, exchange(): return lax.all_to_all(x, 'edge', split_axis=0, concat_axis=0, tiled=True)  42.3 us
    ppermute x12, starting transfers between devices, move(): lax.ppermute(x, 'edge', edge_pairs(d if axis == 1 else 0, d if axis == 2...  20.7 us
    ppermute x12, starting transfers between devices, move(): return lax.ppermute(x, 'rep', [(k, (k + d) % 4) for k in range(4)])  20.1 us
    unnamed x26, local copies, waits for them, and re-layouts  14.2 us
    ppermute x12, waiting for transfers between devices, move(): lax.ppermute(x, 'edge', edge_pairs(d if axis == 1 else 0, d if axis == 2...  13.7 us
  transfers between devices with their start and end apart: 39, of which 26 were waited for; matrix products, arithmetic and copies ran while one was open for 3% of the time, Pallas kernels for 5%

profile of v3, /device:TPU:1, one launch (start us, length us, event | category | flops | bytes accessed | tf_op | source)
XLA Modules:
  0.0 346.7 jit_solution(14811237425148573653)
XLA Ops:
  4.4 13.2 %all-to-all-start = ((s32[64,1,128]{2,1,0:T(1,128)}), s32[64,1,128]{2,1,0:T(1,128)S(1)}, u32[]{:S(2)}, u32[]{:S(2)}) async-start(s32[64,1,128]{2,1,0:T(1,128)} %bitcast.5), calls=%async_computation | async-start | bytes 65536 | tf_op jit(solution)/shard_map/all_to_all | solution.py:383
  19.9 6.9 %all-to-all-done = s32[64,1,128]{2,1,0:T(1,128)S(1)} async-done(((s32[64,1,128]{2,1,0:T(1,128)}), s32[64,1,128]{2,1,0:T(1,128)S(1)}, u32[]{:S(2)}, u32[]{:S(2)}) %all-to-all-start) | async-done | bytes 32800 | tf_op jit(solution)/shard_map/all_to_all | solution.py:383
  26.8 3.9 %shard_map.113 = bf16[64,128,128]{2,1,0:T(8,128)(2,1)} custom-call(bf16[1024,512]{1,0:T(8,128)(2,1)S(1)} %shard_map.111.wide_ref, s32[64,128]{1,0:T(8,128)S(1)} %bitcast.14), custom_call_target="tpu_custom_call" | custom-call | flops 3221225472 | bytes 1048576 | tf_op jit(solution)/shard_map/pallas_call | solution.py:373
  30.7 6.0 %all-to-all-start.1 = ((bf16[64,128,128]{2,1,0:T(8,128)(2,1)}), bf16[64,128,128]{2,1,0:T(8,128)(2,1)}, u32[]{:S(2)}, u32[]{:S(2)}) async-start(bf16[64,128,128]{2,1,0:T(8,128)(2,1)} %shard_map.113), calls=%async_computation.1 | async-start | bytes 4194304 | tf_op jit(solution)/shard_map/all_to_all | solution.py:383
  37.0 2.9 copy.24
  42.6 45.2 %all-to-all-done.1.refs_1_ = bf16[64,128,128]{2,1,0:T(8,128)(2,1)} async-done(((bf16[64,128,128]{2,1,0:T(8,128)(2,1)}), bf16[64,128,128]{2,1,0:T(8,128)(2,1)}, u32[]{:S(2)}, u32[]{:S(2)}) %all-to-all-start.1) | async-done | bytes 2097184 | tf_op jit(solution)/shard_map/all_to_all | solution.py:383
  87.7 9.1 %shard_map.115 = (bf16[64,128,128]{2,1,0:T(8,128)(2,1)}, f32[1600,128]{1,0:T(8,128)S(1)}, f32[1600,128]{1,0:T(8,128)S(1)}) custom-call(s32[4]{0:T(128)S(1)} %pad_add_fusion.1.refs_0_.at_ref, bf16[64,128,128]{2,1,0:T(8,128)(2,1)} %all-to-all-done.1.refs_1_, s32[2,256]{1,0:T(2,128)S(1)} %get-tuple-element.39.refs_2_, f32[2,2560]{1,0:T(2,128)S(1)} %pad_maximum_fusion.refs_3_, ...), custom_call_target="tpu_custom_call" | custom-call | flops 4294967296 | bytes 1048576 | tf_op jit(solution)/shard_map/pallas_call | solution.py:373
  97.8 6.0 %all-to-all-start.2 = ((bf16[64,128,128]{2,1,0:T(8,128)(2,1)}), bf16[64,128,128]{2,1,0:T(8,128)(2,1)}, u32[]{:S(2)}, u32[]{:S(2)}) async-start(bf16[64,128,128]{2,1,0:T(8,128)(2,1)} %get-tuple-element.41), calls=%async_computation.2 | async-start | bytes 4194304 | tf_op jit(solution)/shard_map/all_to_all | solution.py:383
  112.8 3.2 collective-permute-done.2.refs_3_
  126.3 25.2 %collective-permute-done.7.refs_1_ = f32[104,128]{1,0:T(8,128)S(1)} collective-permute-done((f32[104,128]{1,0:T(8,128)S(1)}, f32[104,128]{1,0:T(8,128)S(1)}, u32[]{:S(2)}, u32[]{:S(2)}) %collective-permute-start.7) | collective-permute-done | bytes 53280 | tf_op jit(solution)/shard_map/ppermute | solution.py:409
  152.8 4.4 %collective-permute-done.8.refs_1_ = f32[104,128]{1,0:T(8,128)S(1)} collective-permute-done((f32[104,128]{1,0:T(8,128)S(1)}, f32[104,128]{1,0:T(8,128)S(1)}, u32[]{:S(2)}, u32[]{:S(2)}) %collective-permute-start.8) | collective-permute-done | bytes 53280 | tf_op jit(solution)/shard_map/ppermute | solution.py:409
  157.2 3.1 collective-permute-start.9
  160.2 4.0 %collective-permute-done.9.refs_1_ = f32[104,128]{1,0:T(8,128)S(1)} collective-permute-done((f32[104,128]{1,0:T(8,128)S(1)}, f32[104,128]{1,0:T(8,128)S(1)}, u32[]{:S(2)}, u32[]{:S(2)}) %collective-permute-start.9) | collective-permute-done | bytes 53280 | tf_op jit(solution)/shard_map/ppermute | solution.py:409
  164.3 9.4 %shard_map.122 = (f32[1,1024,400]{2,1,0:T(8,128)}, f32[8,128]{1,0:T(8,128)S(1)}, bf16[64,128,128]{2,1,0:T(8,128)(2,1)}) custom-call(bf16[64,128,128]{2,1,0:T(8,128)(2,1)} %all-to-all-done.2.refs_0_, s32[2,2560]{1,0:T(2,128)S(1)} %pad_add_fusion.refs_1_, f32[1,1024,400]{2,1,0:T(8,128)} %copy-done, f32[8,128]{1,0:T(8,128)S(1)} %bitcast.19, ...), custom_call_target="tpu_custom_call" | custom-call | flops 5368709120 | bytes 1048576 | tf_op jit(solution)/shard_map/pallas_call | solution.py:373
  173.7 11.2 %all-to-all-start.3 = ((bf16[64,128,128]{2,1,0:T(8,128)(2,1)}), bf16[64,128,128]{2,1,0:T(8,128)(2,1)}, u32[]{:S(2)}, u32[]{:S(2)}) async-start(bf16[64,128,128]{2,1,0:T(8,128)(2,1)} %get-tuple-element.52), calls=%async_computation.3 | async-start | bytes 4194304 | tf_op jit(solution)/shard_map/all_to_all | solution.py:383
  186.3 2.6 collective-permute-start.11
  192.4 3.2 collective-permute-done.11.refs_2_
  201.7 3.2 collective-permute-done.14.refs_2_
  208.2 3.6 %shard_map.125 = (f32[1024,400]{1,0:T(8,128)S(1)}, f32[8,128]{1,0:T(8,128)S(1)}) custom-call(s32[4]{0:T(128)S(1)} %pad_add_fusion.1.refs_0_.at_ref, bf16[1600,128]{1,0:T(8,128)(2,1)S(1)} %shard_map.124.mine_ref, bf16[1600,128]{1,0:T(8,128)(2,1)S(1)} %collective-permute-done.16.other_ref, f32[1024,400]{1,0:T(8,128)S(1)} %pad.8.refs_0_.table_ref, ...), custom_call_target="tpu_custom_call" | custom-call | bytes 1048576 | tf_op jit(solution)/shard_map/pallas_call | solution.py:373
  214.0 22.1 %all-to-all-done.3.refs_1_ = bf16[64,128,128]{2,1,0:T(8,128)(2,1)} async-done(((bf16[64,128,128]{2,1,0:T(8,128)(2,1)}), bf16[64,128,128]{2,1,0:T(8,128)(2,1)}, u32[]{:S(2)}, u32[]{:S(2)}) %all-to-all-start.3) | async-done | bytes 2097184 | tf_op jit(solution)/shard_map/all_to_all | solution.py:383
  236.0 9.1 %shard_map.127 = (bf16[64,128,128]{2,1,0:T(8,128)(2,1)}, f32[1600,128]{1,0:T(8,128)S(1)}, f32[1600,128]{1,0:T(8,128)S(1)}) custom-call(s32[4]{0:T(128)S(1)} %pad_add_fusion.1.refs_0_.at_ref, bf16[64,128,128]{2,1,0:T(8,128)(2,1)} %all-to-all-done.3.refs_1_, s32[2,256]{1,0:T(2,128)S(1)} %get-tuple-element.39.refs_2_, f32[2,2560]{1,0:T(2,128)S(1)} %pad_maximum_fusion.refs_3_, ...), custom_call_target="tpu_custom_call" | custom-call | flops 4294967296 | bytes 1048576 | tf_op jit(solution)/shard_map/pallas_call | solution.py:373
  245.1 6.0 %all-to-all-start.4 = ((bf16[64,128,128]{2,1,0:T(8,128)(2,1)}), bf16[64,128,128]{2,1,0:T(8,128)(2,1)}, u32[]{:S(2)}, u32[]{:S(2)}) async-start(bf16[64,128,128]{2,1,0:T(8,128)(2,1)} %get-tuple-element.55), calls=%async_computation.4 | async-start | bytes 4194304 | tf_op jit(solution)/shard_map/all_to_all | solution.py:383
  255.7 2.6 collective-permute-start.19
  259.9 3.2 collective-permute-done.19.refs_3_
  273.6 25.3 %collective-permute-done.24.refs_1_ = f32[104,128]{1,0:T(8,128)S(1)} collective-permute-done((f32[104,128]{1,0:T(8,128)S(1)}, f32[104,128]{1,0:T(8,128)S(1)}, u32[]{:S(2)}, u32[]{:S(2)}) %collective-permute-start.24) | collective-permute-done | bytes 53280 | tf_op jit(solution)/shard_map/ppermute | solution.py:409
  299.9 4.6 %collective-permute-done.25.refs_1_ = f32[104,128]{1,0:T(8,128)S(1)} collective-permute-done((f32[104,128]{1,0:T(8,128)S(1)}, f32[104,128]{1,0:T(8,128)S(1)}, u32[]{:S(2)}, u32[]{:S(2)}) %collective-permute-start.25) | collective-permute-done | bytes 53280 | tf_op jit(solution)/shard_map/ppermute | solution.py:409
  304.5 3.1 collective-permute-start.26
  307.6 4.0 %collective-permute-done.26.refs_1_ = f32[104,128]{1,0:T(8,128)S(1)} collective-permute-done((f32[104,128]{1,0:T(8,128)S(1)}, f32[104,128]{1,0:T(8,128)S(1)}, u32[]{:S(2)}, u32[]{:S(2)}) %collective-permute-start.26) | collective-permute-done | bytes 53280 | tf_op jit(solution)/shard_map/ppermute | solution.py:409
  324.4 7.4 %shard_map.135 = (f32[1,1024,400]{2,1,0:T(8,128)}, f32[8,128]{1,0:T(8,128)}) custom-call(bf16[64,128,128]{2,1,0:T(8,128)(2,1)} %all-to-all-done.4.refs_0_, s32[2,2560]{1,0:T(2,128)S(1)} %pad_add_fusion.refs_1_, f32[1,1024,400]{2,1,0:T(8,128)} %get-tuple-element.56.refs_2_, f32[8,128]{1,0:T(8,128)S(1)} %get-tuple-element.53._.refs_3_, ...), custom_call_target="tpu_custom_call" | custom-call | flops 5368709120 | bytes 1048576 | tf_op jit(solution)/shard_map/pallas_call | solution.py:373
  333.1 4.5 %collective-permute-start.33 = (bf16[1600,128]{1,0:T(8,128)(2,1)S(1)}, bf16[1600,128]{1,0:T(8,128)(2,1)S(1)}, u32[]{:S(2)}, u32[]{:S(2)}) collective-permute-start(bf16[1600,128]{1,0:T(8,128)(2,1)S(1)} %shard_map.136.mine_ref), channel_id=1, source_target_pairs={{0,4},{4,0},{8,12},{12,8},{16,20},{20,16},{24,28},{28,24},{32,36},... | collective-permute-start | bytes 1228808 | tf_op jit(solution)/shard_map/ppermute | solution.py:441
  337.6 2.7 copy.26
  340.4 4.1 %shard_map.137 = (f32[1024,400]{1,0:T(8,128)S(1)}, f32[8,128]{1,0:T(8,128)}) custom-call(s32[4]{0:T(128)S(1)} %pad_add_fusion.1.refs_0_.at_ref, bf16[1600,128]{1,0:T(8,128)(2,1)S(1)} %shard_map.136.mine_ref, bf16[1600,128]{1,0:T(8,128)(2,1)S(1)} %collective-permute-done.33.other_ref, f32[1024,400]{1,0:T(8,128)S(1)} %copy-done.2, ...), custom_call_target="tpu_custom_call" | custom-call | bytes 1048576 | tf_op jit(solution)/shard_map/pallas_call | solution.py:373
  (111 shorter events, 80.6 us)
Async XLA Ops:
  4.4 22.4 %all-to-all-start = ((s32[64,1,128]{2,1,0:T(1,128)}), s32[64,1,128]{2,1,0:T(1,128)S(1)}, u32[]{:S(2)}, u32[]{:S(2)}) async-start(s32[64,1,128]{2,1,0:T(1,128)} %bitcast.5), calls=%async_computation | async-start | bytes 65536 | tf_op jit(solution)/shard_map/all_to_all | solution.py:383
  30.7 57.0 %all-to-all-start.1 = ((bf16[64,128,128]{2,1,0:T(8,128)(2,1)}), bf16[64,128,128]{2,1,0:T(8,128)(2,1)}, u32[]{:S(2)}, u32[]{:S(2)}) async-start(bf16[64,128,128]{2,1,0:T(8,128)(2,1)} %shard_map.113), calls=%async_computation.1 | async-start | bytes 4194304 | tf_op jit(solution)/shard_map/all_to_all | solution.py:383
  97.8 66.5 %all-to-all-start.2 = ((bf16[64,128,128]{2,1,0:T(8,128)(2,1)}), bf16[64,128,128]{2,1,0:T(8,128)(2,1)}, u32[]{:S(2)}, u32[]{:S(2)}) async-start(bf16[64,128,128]{2,1,0:T(8,128)(2,1)} %get-tuple-element.41), calls=%async_computation.2 | async-start | bytes 4194304 | tf_op jit(solution)/shard_map/all_to_all | solution.py:383
  107.3 5.5 %collective-permute-start.1 = (bf16[400,128]{1,0:T(8,128)(2,1)S(1)}, bf16[400,128]{1,0:T(8,128)(2,1)S(1)}, u32[]{:S(2)}, u32[]{:S(2)}) collective-permute-start(bf16[400,128]{1,0:T(8,128)(2,1)S(1)} %get-tuple-element.45), channel_id=1, source_target_pairs={{0,1},{1,2},{2,3},{3,0},{4,5},{5,6},{6,7},{7,4},{8,9},{9,10},{10,1... | collective-permute-start | bytes 307208 | tf_op jit(solution)/shard_map/ppermute | solution.py:401
  108.5 7.4 %collective-permute-start.2 = (bf16[400,128]{1,0:T(8,128)(2,1)S(1)}, bf16[400,128]{1,0:T(8,128)(2,1)S(1)}, u32[]{:S(2)}, u32[]{:S(2)}) collective-permute-start(bf16[400,128]{1,0:T(8,128)(2,1)S(1)} %get-tuple-element.46), channel_id=1, source_target_pairs={{0,2},{1,3},{2,0},{3,1},{4,6},{5,7},{6,4},{7,5},{8,10},{9,11},{10,... | collective-permute-start | bytes 307208 | tf_op jit(solution)/shard_map/ppermute | solution.py:401
  111.0 4.9 %collective-permute-start.3 = (bf16[400,128]{1,0:T(8,128)(2,1)S(1)}, bf16[400,128]{1,0:T(8,128)(2,1)S(1)}, u32[]{:S(2)}, u32[]{:S(2)}) collective-permute-start(bf16[400,128]{1,0:T(8,128)(2,1)S(1)} %get-tuple-element.47), channel_id=1, source_target_pairs={{0,3},{1,0},{2,1},{3,2},{4,7},{5,4},{6,5},{7,6},{8,11},{9,8},{10,9... | collective-permute-start | bytes 307208 | tf_op jit(solution)/shard_map/ppermute | solution.py:401
  116.5 5.4 %collective-permute-start.4 = (f32[104,128]{1,0:T(8,128)S(1)}, f32[104,128]{1,0:T(8,128)S(1)}, u32[]{:S(2)}, u32[]{:S(2)}) collective-permute-start(f32[104,128]{1,0:T(8,128)S(1)} %get-tuple-element.49), channel_id=1, source_target_pairs={{0,64},{4,68},{8,72},{12,76},{16,80},{20,84},{24,88},{28,92},{32,9... | collective-permute-start | bytes 159752 | tf_op jit(solution)/shard_map/ppermute | solution.py:402
  117.9 5.2 %collective-permute-start.5 = (f32[104,128]{1,0:T(8,128)S(1)}, f32[104,128]{1,0:T(8,128)S(1)}, u32[]{:S(2)}, u32[]{:S(2)}) collective-permute-start(f32[104,128]{1,0:T(8,128)S(1)} %get-tuple-element.50), channel_id=1, source_target_pairs={{0,128},{4,132},{8,136},{12,140},{16,144},{20,148},{24,152},{28,15... | collective-permute-start | bytes 159752 | tf_op jit(solution)/shard_map/ppermute | solution.py:402
  124.7 26.8 %collective-permute-start.7 = (f32[104,128]{1,0:T(8,128)S(1)}, f32[104,128]{1,0:T(8,128)S(1)}, u32[]{:S(2)}, u32[]{:S(2)}) collective-permute-start(f32[104,128]{1,0:T(8,128)S(1)} %shard_map.118.refs_0_), channel_id=1, source_target_pairs={{0,8},{4,12},{8,0},{12,4},{16,24},{20,28},{24,16},{28,20},{32,40},... | collective-permute-start | bytes 159752 | tf_op jit(solution)/shard_map/ppermute | solution.py:409
  151.5 5.6 %collective-permute-start.8 = (f32[104,128]{1,0:T(8,128)S(1)}, f32[104,128]{1,0:T(8,128)S(1)}, u32[]{:S(2)}, u32[]{:S(2)}) collective-permute-start(f32[104,128]{1,0:T(8,128)S(1)} %shard_map.119.refs_0_), channel_id=1, source_target_pairs={{0,16},{4,20},{8,24},{12,28},{16,0},{20,4},{24,8},{28,12},{32,48},... | collective-permute-start | bytes 159752 | tf_op jit(solution)/shard_map/ppermute | solution.py:409
  157.2 7.1 %collective-permute-start.9 = (f32[104,128]{1,0:T(8,128)S(1)}, f32[104,128]{1,0:T(8,128)S(1)}, u32[]{:S(2)}, u32[]{:S(2)}) collective-permute-start(f32[104,128]{1,0:T(8,128)S(1)} %shard_map.120.refs_0_), channel_id=1, source_target_pairs={{0,32},{4,36},{8,40},{12,44},{16,48},{20,52},{24,56},{28,60},{32,0... | collective-permute-start | bytes 159752 | tf_op jit(solution)/shard_map/ppermute | solution.py:409
  173.7 62.4 %all-to-all-start.3 = ((bf16[64,128,128]{2,1,0:T(8,128)(2,1)}), bf16[64,128,128]{2,1,0:T(8,128)(2,1)}, u32[]{:S(2)}, u32[]{:S(2)}) async-start(bf16[64,128,128]{2,1,0:T(8,128)(2,1)} %get-tuple-element.52), calls=%async_computation.3 | async-start | bytes 4194304 | tf_op jit(solution)/shard_map/all_to_all | solution.py:383
  184.9 7.6 %collective-permute-start.10 = (f32[104,128]{1,0:T(8,128)S(1)}, f32[104,128]{1,0:T(8,128)S(1)}, u32[]{:S(2)}, u32[]{:S(2)}) collective-permute-start(f32[104,128]{1,0:T(8,128)S(1)} %shard_map.121.refs_5_.refs_0_), channel_id=1, source_target_pairs={{0,64},{4,68},{8,72},{12,76},{16,80},{20,84},{24,88},{28,92},{32,9... | collective-permute-start | bytes 159752 | tf_op jit(solution)/shard_map/ppermute | solution.py:402
  186.3 9.3 %collective-permute-start.11 = (f32[104,128]{1,0:T(8,128)S(1)}, f32[104,128]{1,0:T(8,128)S(1)}, u32[]{:S(2)}, u32[]{:S(2)}) collective-permute-start(f32[104,128]{1,0:T(8,128)S(1)} %shard_map.121.refs_5_.refs_0_), channel_id=1, source_target_pairs={{0,128},{4,132},{8,136},{12,140},{16,144},{20,148},{24,152},{28,15... | collective-permute-start | bytes 159752 | tf_op jit(solution)/shard_map/ppermute | solution.py:402
  188.9 6.7 %collective-permute-start.12 = (f32[104,128]{1,0:T(8,128)S(1)}, f32[104,128]{1,0:T(8,128)S(1)}, u32[]{:S(2)}, u32[]{:S(2)}) collective-permute-start(f32[104,128]{1,0:T(8,128)S(1)} %shard_map.121.refs_5_.refs_0_), channel_id=1, source_target_pairs={{0,192},{4,196},{8,200},{12,204},{16,208},{20,212},{24,216},{28,22... | collective-permute-start | bytes 159752 | tf_op jit(solution)/shard_map/ppermute | solution.py:402
  196.2 5.5 %collective-permute-start.13 = (bf16[400,128]{1,0:T(8,128)(2,1)S(1)}, bf16[400,128]{1,0:T(8,128)(2,1)S(1)}, u32[]{:S(2)}, u32[]{:S(2)}) collective-permute-start(bf16[400,128]{1,0:T(8,128)(2,1)S(1)} %shard_map.123.refs_0_), channel_id=1, source_target_pairs={{0,1},{1,2},{2,3},{3,0},{4,5},{5,6},{6,7},{7,4},{8,9},{9,10},{10,1... | collective-permute-start | bytes 307208 | tf_op jit(solution)/shard_map/ppermute | solution.py:401
  197.7 7.2 %collective-permute-start.14 = (bf16[400,128]{1,0:T(8,128)(2,1)S(1)}, bf16[400,128]{1,0:T(8,128)(2,1)S(1)}, u32[]{:S(2)}, u32[]{:S(2)}) collective-permute-start(bf16[400,128]{1,0:T(8,128)(2,1)S(1)} %shard_map.123.refs_0_), channel_id=1, source_target_pairs={{0,2},{1,3},{2,0},{3,1},{4,6},{5,7},{6,4},{7,5},{8,10},{9,11},{10,... | collective-permute-start | bytes 307208 | tf_op jit(solution)/shard_map/ppermute | solution.py:401
  200.1 4.7 %collective-permute-start.15 = (bf16[400,128]{1,0:T(8,128)(2,1)S(1)}, bf16[400,128]{1,0:T(8,128)(2,1)S(1)}, u32[]{:S(2)}, u32[]{:S(2)}) collective-permute-start(bf16[400,128]{1,0:T(8,128)(2,1)S(1)} %shard_map.123.refs_0_), channel_id=1, source_target_pairs={{0,3},{1,0},{2,1},{3,2},{4,7},{5,4},{6,5},{7,6},{8,11},{9,8},{10,9... | collective-permute-start | bytes 307208 | tf_op jit(solution)/shard_map/ppermute | solution.py:401
  245.1 79.3 %all-to-all-start.4 = ((bf16[64,128,128]{2,1,0:T(8,128)(2,1)}), bf16[64,128,128]{2,1,0:T(8,128)(2,1)}, u32[]{:S(2)}, u32[]{:S(2)}) async-start(bf16[64,128,128]{2,1,0:T(8,128)(2,1)} %get-tuple-element.55), calls=%async_computation.4 | async-start | bytes 4194304 | tf_op jit(solution)/shard_map/all_to_all | solution.py:383
  254.4 5.5 %collective-permute-start.18 = (bf16[400,128]{1,0:T(8,128)(2,1)S(1)}, bf16[400,128]{1,0:T(8,128)(2,1)S(1)}, u32[]{:S(2)}, u32[]{:S(2)}) collective-permute-start(bf16[400,128]{1,0:T(8,128)(2,1)S(1)} %get-tuple-element.60), channel_id=1, source_target_pairs={{0,1},{1,2},{2,3},{3,0},{4,5},{5,6},{6,7},{7,4},{8,9},{9,10},{10,1... | collective-permute-start | bytes 307208 | tf_op jit(solution)/shard_map/ppermute | solution.py:401
  255.7 7.4 %collective-permute-start.19 = (bf16[400,128]{1,0:T(8,128)(2,1)S(1)}, bf16[400,128]{1,0:T(8,128)(2,1)S(1)}, u32[]{:S(2)}, u32[]{:S(2)}) collective-permute-start(bf16[400,128]{1,0:T(8,128)(2,1)S(1)} %get-tuple-element.61), channel_id=1, source_target_pairs={{0,2},{1,3},{2,0},{3,1},{4,6},{5,7},{6,4},{7,5},{8,10},{9,11},{10,... | collective-permute-start | bytes 307208 | tf_op jit(solution)/shard_map/ppermute | solution.py:401
  258.4 4.7 %collective-permute-start.20 = (bf16[400,128]{1,0:T(8,128)(2,1)S(1)}, bf16[400,128]{1,0:T(8,128)(2,1)S(1)}, u32[]{:S(2)}, u32[]{:S(2)}) collective-permute-start(bf16[400,128]{1,0:T(8,128)(2,1)S(1)} %get-tuple-element.62), channel_id=1, source_target_pairs={{0,3},{1,0},{2,1},{3,2},{4,7},{5,4},{6,5},{7,6},{8,11},{9,8},{10,9... | collective-permute-start | bytes 307208 | tf_op jit(solution)/shard_map/ppermute | solution.py:401
  263.7 5.0 %collective-permute-start.21 = (f32[104,128]{1,0:T(8,128)S(1)}, f32[104,128]{1,0:T(8,128)S(1)}, u32[]{:S(2)}, u32[]{:S(2)}) collective-permute-start(f32[104,128]{1,0:T(8,128)S(1)} %get-tuple-element.64), channel_id=1, source_target_pairs={{0,64},{4,68},{8,72},{12,76},{16,80},{20,84},{24,88},{28,92},{32,9... | collective-permute-start | bytes 159752 | tf_op jit(solution)/shard_map/ppermute | solution.py:402
  265.0 5.4 %collective-permute-start.22 = (f32[104,128]{1,0:T(8,128)S(1)}, f32[104,128]{1,0:T(8,128)S(1)}, u32[]{:S(2)}, u32[]{:S(2)}) collective-permute-start(f32[104,128]{1,0:T(8,128)S(1)} %get-tuple-element.65), channel_id=1, source_target_pairs={{0,128},{4,132},{8,136},{12,140},{16,144},{20,148},{24,152},{28,15... | collective-permute-start | bytes 159752 | tf_op jit(solution)/shard_map/ppermute | solution.py:402
  272.0 26.8 %collective-permute-start.24 = (f32[104,128]{1,0:T(8,128)S(1)}, f32[104,128]{1,0:T(8,128)S(1)}, u32[]{:S(2)}, u32[]{:S(2)}) collective-permute-start(f32[104,128]{1,0:T(8,128)S(1)} %shard_map.130.refs_0_), channel_id=1, source_target_pairs={{0,8},{4,12},{8,0},{12,4},{16,24},{20,28},{24,16},{28,20},{32,40},... | collective-permute-start | bytes 159752 | tf_op jit(solution)/shard_map/ppermute | solution.py:409
  298.9 5.6 %collective-permute-start.25 = (f32[104,128]{1,0:T(8,128)S(1)}, f32[104,128]{1,0:T(8,128)S(1)}, u32[]{:S(2)}, u32[]{:S(2)}) collective-permute-start(f32[104,128]{1,0:T(8,128)S(1)} %shard_map.131.refs_0_), channel_id=1, source_target_pairs={{0,16},{4,20},{8,24},{12,28},{16,0},{20,4},{24,8},{28,12},{32,48},... | collective-permute-start | bytes 159752 | tf_op jit(solution)/shard_map/ppermute | solution.py:409
  304.5 7.1 %collective-permute-start.26 = (f32[104,128]{1,0:T(8,128)S(1)}, f32[104,128]{1,0:T(8,128)S(1)}, u32[]{:S(2)}, u32[]{:S(2)}) collective-permute-start(f32[104,128]{1,0:T(8,128)S(1)} %shard_map.132.refs_0_), channel_id=1, source_target_pairs={{0,32},{4,36},{8,40},{12,44},{16,48},{20,52},{24,56},{28,60},{32,0... | collective-permute-start | bytes 159752 | tf_op jit(solution)/shard_map/ppermute | solution.py:409
  311.6 5.1 %collective-permute-start.27 = (f32[104,128]{1,0:T(8,128)S(1)}, f32[104,128]{1,0:T(8,128)S(1)}, u32[]{:S(2)}, u32[]{:S(2)}) collective-permute-start(f32[104,128]{1,0:T(8,128)S(1)} %shard_map.133.refs_0_), channel_id=1, source_target_pairs={{0,64},{4,68},{8,72},{12,76},{16,80},{20,84},{24,88},{28,92},{32,9... | collective-permute-start | bytes 159752 | tf_op jit(solution)/shard_map/ppermute | solution.py:402
  319.3 12.5 %collective-permute-start.30 = (bf16[400,128]{1,0:T(8,128)(2,1)S(1)}, bf16[400,128]{1,0:T(8,128)(2,1)S(1)}, u32[]{:S(2)}, u32[]{:S(2)}) collective-permute-start(bf16[400,128]{1,0:T(8,128)(2,1)S(1)} %shard_map.134.refs_5_.refs_0_), channel_id=1, source_target_pairs={{0,1},{1,2},{2,3},{3,0},{4,5},{5,6},{6,7},{7,4},{8,9},{9,10},{10,1... | collective-permute-start | bytes 307208 | tf_op jit(solution)/shard_map/ppermute | solution.py:401
  320.6 11.2 %collective-permute-start.31 = (bf16[400,128]{1,0:T(8,128)(2,1)S(1)}, bf16[400,128]{1,0:T(8,128)(2,1)S(1)}, u32[]{:S(2)}, u32[]{:S(2)}) collective-permute-start(bf16[400,128]{1,0:T(8,128)(2,1)S(1)} %shard_map.134.refs_5_.refs_0_), channel_id=1, source_target_pairs={{0,2},{1,3},{2,0},{3,1},{4,6},{5,7},{6,4},{7,5},{8,10},{9,11},{10,... | collective-permute-start | bytes 307208 | tf_op jit(solution)/shard_map/ppermute | solution.py:401
  323.0 8.8 %collective-permute-start.32 = (bf16[400,128]{1,0:T(8,128)(2,1)S(1)}, bf16[400,128]{1,0:T(8,128)(2,1)S(1)}, u32[]{:S(2)}, u32[]{:S(2)}) collective-permute-start(bf16[400,128]{1,0:T(8,128)(2,1)S(1)} %shard_map.134.refs_5_.refs_0_), channel_id=1, source_target_pairs={{0,3},{1,0},{2,1},{3,2},{4,7},{5,4},{6,5},{7,6},{8,11},{9,8},{10,9... | collective-permute-start | bytes 307208 | tf_op jit(solution)/shard_map/ppermute | solution.py:401
  333.1 7.2 %collective-permute-start.33 = (bf16[1600,128]{1,0:T(8,128)(2,1)S(1)}, bf16[1600,128]{1,0:T(8,128)(2,1)S(1)}, u32[]{:S(2)}, u32[]{:S(2)}) collective-permute-start(bf16[1600,128]{1,0:T(8,128)(2,1)S(1)} %shard_map.136.mine_ref), channel_id=1, source_target_pairs={{0,4},{4,0},{8,12},{12,8},{16,20},{20,16},{24,28},{28,24},{32,36},... | collective-permute-start | bytes 1228808 | tf_op jit(solution)/shard_map/ppermute | solution.py:441
  (18 other events, 144.2 us)

commit v4 on v3

--- a/solution.py
+++ b/solution.py
@@ -16,6 +16,7 @@
 REL = 1024
 DENSE = REL // 64 * 200
 WIRE_PARTS = 4
+Y_ROWS = 112
 
 
 def iota(shape, dim):
@@ -103,9 +104,19 @@
     return jnp.transpose(jnp.broadcast_to(row, (128, 128)))
 
 
-def prepare(heads_ref, tails_ref, negatives_ref, send_ref, negative_ref, slots_ref):
+def prepare(heads_in, tails_in, negatives_in, send_ref, negative_ref, slots_ref, heads_ref, tails_ref, negatives_ref, held_ref, sems):
     count = 2 * heads_ref.shape[2] + negatives_ref.shape[2]
     steps = heads_ref.shape[1]
+    fetches = [
+        pltpu.make_async_copy(source, held, sems.at[k])
+        for k, (source, held) in enumerate(
+            ((heads_in, heads_ref), (tails_in, tails_ref), (negatives_in, negatives_ref))
+        )
+    ]
+    for copy in fetches:
+        copy.start()
+    for copy in fetches:
+        copy.wait()
     before = one_hot(iota((128, 128), 0) < iota((128, 128), 1))
     send = jnp.zeros((OWN, 128), F32)
     negative = jnp.zeros((OWN, 128), F32)
@@ -132,8 +143,11 @@
         chosen = jnp.where(iota((OWN, count), 1) >= 256, at_owner, 0.0).astype(BF16)
         negative = negative + dot(chosen, at_rank, last)
         slots_ref[s : s + 1, :] = (owner * CAP + rank)[:, :256]
-    send_ref[...] = send.astype(I32)
+    held_ref[...] = send.astype(I32)
+    sending = pltpu.make_async_copy(held_ref, send_ref, sems.at[3])
+    sending.start()
     negative_ref[...] = negative
+    sending.wait()
 
 
 def gather_rows(named_ref, step, wide_ref, wire_ref, held_ref, sems):
@@ -313,11 +327,22 @@
         outs[d][...] = sum_ref[pl.ds(start, rows), :].astype(outs[d].dtype)
 
 
-def sum_stage(*refs):
+def sum_y(own_ref, *refs):
     *parts, out_ref = refs
-    total = parts[0][...]
-    for ref in parts[1:]:
+    total = own_ref[...]
+    for ref in parts:
         total = total + ref[...]
+    out_ref[...] = total.astype(BF16)
+
+
+def sum_z(at_ref, *refs):
+    *parts, out_ref, all_ref = refs
+    n = len(parts)
+    for d in range(n):
+        all_ref[lax.rem(at_ref[2] + n - d, n)] = parts[d][...].astype(F32)
+    total = all_ref[0]
+    for z in range(1, n):
+        total = total + all_ref[z]
     out_ref[...] = total
 
 
@@ -402,18 +427,11 @@
     return lax.ppermute(x, "edge", edge_pairs(d if axis == 1 else 0, d if axis == 2 else 0))
 
 
-def doubled(x, bit):
-    pairs = [
-        (edge_of(y, z, core), edge_of(y, z ^ bit, core)) for y in range(4) for z in range(8) for core in range(2)
-    ]
-    return kernel(sum_stage, "vv", [jax.ShapeDtypeStruct(x.shape, F32)], "v")(x, lax.ppermute(x, "edge", pairs))[0]
-
-
 def relation_scatter(at, keep, give):
     shape = jax.ShapeDtypeStruct
     arrived = [lax.ppermute(give, "edge", edge_pairs(0, 0, 1))]
     own = keep
-    for axis, (rows, sent) in enumerate(((DENSE // 8, BF16), (104, F32))):
+    for axis, (rows, sent) in enumerate(((DENSE // 8, BF16), (Y_ROWS, F32))):
         own, *parts = kernel(
             lambda *refs, axis=axis: scatter_stage(axis, *refs),
             "sv" + "v" * len(arrived),
@@ -422,15 +440,15 @@
             [pltpu.VMEM((4 * rows, 128), F32)],
         )(at, own, *arrived)
         arrived = [move(part, axis, d + 1) for d, part in enumerate(parts)]
-    own = kernel(sum_stage, "vvvv", [shape(own.shape, F32)], "v")(own, *arrived)[0]
-    for bit in (1, 2, 4):
-        own = doubled(own, bit)
-    return own
+    own = kernel(sum_y, "vvvv", [shape(own.shape, BF16)], "v")(own, *arrived)[0]
+    return kernel(sum_z, "s" + "v" * 8, [shape(own.shape, F32)], "v", [pltpu.VMEM((8, *own.shape), F32)])(
+        at, own, *[move(own, 2, d) for d in range(1, 8)]
+    )[0]
 
 
 def relation_gather_y(at, own):
     return kernel(
-        gather_y, "svvvv", [jax.ShapeDtypeStruct((DENSE // 8, 128), BF16)], "v", [pltpu.VMEM((416, 128), F32)]
+        gather_y, "svvvv", [jax.ShapeDtypeStruct((DENSE // 8, 128), BF16)], "v", [pltpu.VMEM((4 * Y_ROWS, 128), F32)]
     )(at, own, *[move(own, 1, d) for d in (1, 2, 3)])[0]
 
 
@@ -453,7 +471,11 @@
     edge = lax.axis_index("edge")
     at = jnp.stack([lax.axis_index("rep"), edge // 16, edge // 2 % 8, edge % 2]).astype(I32)
     send, negative, slots = kernel(
-        prepare, "vvv", [shape((OWN, 128), I32), shape((OWN, 128), F32), shape((steps, 256), I32)], "vvv"
+        prepare,
+        "hhh",
+        [shape((OWN, 128), I32), shape((OWN, 128), F32), shape((steps, 256), I32)],
+        "hvv",
+        [pltpu.VMEM(x.shape, I32) for x in (heads, tails, negatives)] + [pltpu.VMEM((OWN, 128), I32), copies(4)],
     )(heads, tails, negatives)
     named = exchange(send.reshape(OWN, 1, 128)).reshape(OWN, 128)
     wide = kernel(widen, "v", [shape((1024, 512), BF16)], "v")(table)[0]

time: 352 us -> 338 us (0.960)
  waiting for transfers between devices: 172 us -> 144 us
  starting transfers between devices: 101 us -> 116 us
    ppermute x6 -> x0, waiting for transfers between devices: 67.6 us -> none  [doubled(): lax.ppermute(x, 'edge', pairs)]
    ppermute x12 -> x26, waiting for transfers between devices: 13.7 us -> 52.9 us  [move(): lax.ppermute(x, 'edge', edge_pairs(d if axis == 1 else 0, d if axis == 2...]
    ppermute x12 -> x26, starting transfers between devices: 20.7 us -> 50 us  [move(): lax.ppermute(x, 'edge', edge_pairs(d if axis == 1 else 0, d if axis == 2...]
    ppermute x6 -> x0, starting transfers between devices: 11.2 us -> none  [doubled(): lax.ppermute(x, 'edge', pairs)]
    unnamed x26 -> x20, local copies, waits for them, and re-layouts: 14.2 us -> 12.1 us
    pallas_call x27 -> x23, Pallas kernels: 55.4 us -> 57.3 us  [kernel(): call(*[pltpu.with_memory_space_constraint(x, pltpu.HBM) if k == 'h' else...]
  transfers between devices with their start and end apart: 39 -> 47, of which waited for: 26 -> 26; matrix products, arithmetic and copies ran while one was open for 3% -> 3% of each run, Pallas kernels for 5% -> 6%
where the time goes in v4:
time: 338 us; the launch traced here: 333 us
  waiting for transfers between devices  144 us (43%)
  starting transfers between devices  116 us (34%)
  Pallas kernels  57.3 us (17%)
  local copies, waits for them, and re-layouts  14.6 us (4%)
    all_to_all x5, waiting for transfers between devices, exchange(): return lax.all_to_all(x, 'edge', split_axis=0, concat_axis=0, tiled=True)  74.1 us
    pallas_call x23, Pallas kernels, kernel(): call(*[pltpu.with_memory_space_constraint(x, pltpu.HBM) if k == 'h' else...  57.3 us
    ppermute x26, waiting for transfers between devices, move(): lax.ppermute(x, 'edge', edge_pairs(d if axis == 1 else 0, d if axis == 2...  52.9 us
    ppermute x26, starting transfers between devices, move(): lax.ppermute(x, 'edge', edge_pairs(d if axis == 1 else 0, d if axis == 2...  50 us
    all_to_all x5, starting transfers between devices, exchange(): return lax.all_to_all(x, 'edge', split_axis=0, concat_axis=0, tiled=True)  39.1 us
    ppermute x12, starting transfers between devices, move(): return lax.ppermute(x, 'rep', [(k, (k + d) % 4) for k in range(4)])  19.8 us
    unnamed x20, local copies, waits for them, and re-layouts  12.1 us
    ppermute x12, waiting for transfers between devices, move(): return lax.ppermute(x, 'rep', [(k, (k + d) % 4) for k in range(4)])  11.1 us
  transfers between devices with their start and end apart: 47, of which 26 were waited for; matrix products, arithmetic and copies ran while one was open for 3% of the time, Pallas kernels for 6%

profile of v4, /device:TPU:1, one launch (start us, length us, event | category | flops | bytes accessed | tf_op | source)
XLA Modules:
  0.0 332.9 jit_solution(377018843977382526)
XLA Ops:
  3.1 13.2 %all-to-all-start = ((s32[64,1,128]{2,1,0:T(1,128)}), s32[64,1,128]{2,1,0:T(1,128)S(1)}, u32[]{:S(2)}, u32[]{:S(2)}) async-start(s32[64,1,128]{2,1,0:T(1,128)} %bitcast.20), calls=%async_computation | async-start | bytes 65536 | tf_op jit(solution)/shard_map/all_to_all | solution.py:408
  18.6 6.9 %all-to-all-done = s32[64,1,128]{2,1,0:T(1,128)S(1)} async-done(((s32[64,1,128]{2,1,0:T(1,128)}), s32[64,1,128]{2,1,0:T(1,128)S(1)}, u32[]{:S(2)}, u32[]{:S(2)}) %all-to-all-start) | async-done | bytes 32800 | tf_op jit(solution)/shard_map/all_to_all | solution.py:408
  25.5 3.9 %shard_map.113 = bf16[64,128,128]{2,1,0:T(8,128)(2,1)} custom-call(bf16[1024,512]{1,0:T(8,128)(2,1)S(1)} %shard_map.111.wide_ref, s32[64,128]{1,0:T(8,128)S(1)} %bitcast.14), custom_call_target="tpu_custom_call" | custom-call | flops 3221225472 | bytes 1048576 | tf_op jit(solution)/shard_map/pallas_call | solution.py:398
  29.4 6.0 %all-to-all-start.1 = ((bf16[64,128,128]{2,1,0:T(8,128)(2,1)}), bf16[64,128,128]{2,1,0:T(8,128)(2,1)}, u32[]{:S(2)}, u32[]{:S(2)}) async-start(bf16[64,128,128]{2,1,0:T(8,128)(2,1)} %shard_map.113), calls=%async_computation.1 | async-start | bytes 4194304 | tf_op jit(solution)/shard_map/all_to_all | solution.py:408
  35.8 2.9 copy.24
  41.3 45.2 %all-to-all-done.1.refs_1_ = bf16[64,128,128]{2,1,0:T(8,128)(2,1)} async-done(((bf16[64,128,128]{2,1,0:T(8,128)(2,1)}), bf16[64,128,128]{2,1,0:T(8,128)(2,1)}, u32[]{:S(2)}, u32[]{:S(2)}) %all-to-all-start.1) | async-done | bytes 2097184 | tf_op jit(solution)/shard_map/all_to_all | solution.py:408
  86.5 9.1 %shard_map.115 = (bf16[64,128,128]{2,1,0:T(8,128)(2,1)}, f32[1600,128]{1,0:T(8,128)S(1)}, f32[1600,128]{1,0:T(8,128)S(1)}) custom-call(s32[4]{0:T(128)S(1)} %pad_add_fusion.1.refs_0_.at_ref, bf16[64,128,128]{2,1,0:T(8,128)(2,1)} %all-to-all-done.1.refs_1_, s32[2,256]{1,0:T(2,128)S(1)} %get-tuple-element.39.refs_2_, f32[2,2560]{1,0:T(2,128)S(1)} %pad_maximum_fusion.refs_3_, ...), custom_call_target="tpu_custom_call" | custom-call | flops 4294967296 | bytes 1048576 | tf_op jit(solution)/shard_map/pallas_call | solution.py:398
  96.5 6.0 %all-to-all-start.2 = ((bf16[64,128,128]{2,1,0:T(8,128)(2,1)}), bf16[64,128,128]{2,1,0:T(8,128)(2,1)}, u32[]{:S(2)}, u32[]{:S(2)}) async-start(bf16[64,128,128]{2,1,0:T(8,128)(2,1)} %get-tuple-element.41), calls=%async_computation.2 | async-start | bytes 4194304 | tf_op jit(solution)/shard_map/all_to_all | solution.py:408
  111.5 3.2 collective-permute-done.2.refs_3_
  116.7 2.5 collective-permute-start.5
  125.3 3.2 collective-permute-start.8
  135.3 15.0 %collective-permute-done.7.refs_1_ = bf16[112,128]{1,0:T(8,128)(2,1)S(1)} collective-permute-done((bf16[112,128]{1,0:T(8,128)(2,1)S(1)}, bf16[112,128]{1,0:T(8,128)(2,1)S(1)}, u32[]{:S(2)}, u32[]{:S(2)}) %collective-permute-start.7) | collective-permute-done | bytes 28704 | tf_op jit(solution)/shard_map/ppermute | solution.py:427
  155.0 3.5 %collective-permute-done.10.refs_4_ = bf16[112,128]{1,0:T(8,128)(2,1)S(1)} collective-permute-done((bf16[112,128]{1,0:T(8,128)(2,1)S(1)}, bf16[112,128]{1,0:T(8,128)(2,1)S(1)}, u32[]{:S(2)}, u32[]{:S(2)}) %collective-permute-start.10) | collective-permute-done | bytes 28704 | tf_op jit(solution)/shard_map/ppermute | solution.py:427
  159.1 9.4 %shard_map.120 = (f32[1,1024,400]{2,1,0:T(8,128)}, f32[8,128]{1,0:T(8,128)S(1)}, bf16[64,128,128]{2,1,0:T(8,128)(2,1)}) custom-call(bf16[64,128,128]{2,1,0:T(8,128)(2,1)} %all-to-all-done.2.refs_0_, s32[2,2560]{1,0:T(2,128)S(1)} %pad_add_fusion.refs_1_, f32[1,1024,400]{2,1,0:T(8,128)} %copy-done, f32[8,128]{1,0:T(8,128)S(1)} %bitcast.19, ...), custom_call_target="tpu_custom_call" | custom-call | flops 5368709120 | bytes 1048576 | tf_op jit(solution)/shard_map/pallas_call | solution.py:398
  168.5 7.9 %all-to-all-start.3 = ((bf16[64,128,128]{2,1,0:T(8,128)(2,1)}), bf16[64,128,128]{2,1,0:T(8,128)(2,1)}, u32[]{:S(2)}, u32[]{:S(2)}) async-start(bf16[64,128,128]{2,1,0:T(8,128)(2,1)} %get-tuple-element.52), calls=%async_computation.3 | async-start | bytes 4194304 | tf_op jit(solution)/shard_map/all_to_all | solution.py:408
  177.8 2.6 collective-permute-start.15
  181.5 2.7 collective-permute-done.14.refs_1_
  184.2 3.1 collective-permute-done.15.refs_2_
  193.1 3.2 collective-permute-done.18.refs_2_
  199.7 3.6 %shard_map.123 = (f32[1024,400]{1,0:T(8,128)S(1)}, f32[8,128]{1,0:T(8,128)S(1)}) custom-call(s32[4]{0:T(128)S(1)} %pad_add_fusion.1.refs_0_.at_ref, bf16[1600,128]{1,0:T(8,128)(2,1)S(1)} %shard_map.122.mine_ref, bf16[1600,128]{1,0:T(8,128)(2,1)S(1)} %collective-permute-done.20.other_ref, f32[1024,400]{1,0:T(8,128)S(1)} %pad.8.refs_0_.table_ref, ...), custom_call_target="tpu_custom_call" | custom-call | bytes 1048576 | tf_op jit(solution)/shard_map/pallas_call | solution.py:398
  205.4 22.1 %all-to-all-done.3.refs_1_ = bf16[64,128,128]{2,1,0:T(8,128)(2,1)} async-done(((bf16[64,128,128]{2,1,0:T(8,128)(2,1)}), bf16[64,128,128]{2,1,0:T(8,128)(2,1)}, u32[]{:S(2)}, u32[]{:S(2)}) %all-to-all-start.3) | async-done | bytes 2097184 | tf_op jit(solution)/shard_map/all_to_all | solution.py:408
  227.5 9.1 %shard_map.125 = (bf16[64,128,128]{2,1,0:T(8,128)(2,1)}, f32[1600,128]{1,0:T(8,128)S(1)}, f32[1600,128]{1,0:T(8,128)S(1)}) custom-call(s32[4]{0:T(128)S(1)} %pad_add_fusion.1.refs_0_.at_ref, bf16[64,128,128]{2,1,0:T(8,128)(2,1)} %all-to-all-done.3.refs_1_, s32[2,256]{1,0:T(2,128)S(1)} %get-tuple-element.39.refs_2_, f32[2,2560]{1,0:T(2,128)S(1)} %pad_maximum_fusion.refs_3_, ...), custom_call_target="tpu_custom_call" | custom-call | flops 4294967296 | bytes 1048576 | tf_op jit(solution)/shard_map/pallas_call | solution.py:398
  236.6 6.0 %all-to-all-start.4 = ((bf16[64,128,128]{2,1,0:T(8,128)(2,1)}), bf16[64,128,128]{2,1,0:T(8,128)(2,1)}, u32[]{:S(2)}, u32[]{:S(2)}) async-start(bf16[64,128,128]{2,1,0:T(8,128)(2,1)} %get-tuple-element.55), calls=%async_computation.4 | async-start | bytes 4194304 | tf_op jit(solution)/shard_map/all_to_all | solution.py:408
  251.4 3.2 collective-permute-done.23.refs_3_
  256.5 2.7 collective-permute-start.26
  265.3 2.9 collective-permute-start.29
  275.0 15.4 %collective-permute-done.28.refs_1_ = bf16[112,128]{1,0:T(8,128)(2,1)S(1)} collective-permute-done((bf16[112,128]{1,0:T(8,128)(2,1)S(1)}, bf16[112,128]{1,0:T(8,128)(2,1)S(1)}, u32[]{:S(2)}, u32[]{:S(2)}) %collective-permute-start.28) | collective-permute-done | bytes 28704 | tf_op jit(solution)/shard_map/ppermute | solution.py:427
  295.0 3.5 %collective-permute-done.31.refs_4_ = bf16[112,128]{1,0:T(8,128)(2,1)S(1)} collective-permute-done((bf16[112,128]{1,0:T(8,128)(2,1)S(1)}, bf16[112,128]{1,0:T(8,128)(2,1)S(1)}, u32[]{:S(2)}, u32[]{:S(2)}) %collective-permute-start.31) | collective-permute-done | bytes 28704 | tf_op jit(solution)/shard_map/ppermute | solution.py:427
  310.7 7.4 %shard_map.131 = (f32[1,1024,400]{2,1,0:T(8,128)}, f32[8,128]{1,0:T(8,128)}) custom-call(bf16[64,128,128]{2,1,0:T(8,128)(2,1)} %all-to-all-done.4.refs_0_, s32[2,2560]{1,0:T(2,128)S(1)} %pad_add_fusion.refs_1_, f32[1,1024,400]{2,1,0:T(8,128)} %get-tuple-element.56.refs_2_, f32[8,128]{1,0:T(8,128)S(1)} %get-tuple-element.53._.refs_3_, ...), custom_call_target="tpu_custom_call" | custom-call | flops 5368709120 | bytes 1048576 | tf_op jit(solution)/shard_map/pallas_call | solution.py:398
  319.4 4.3 %collective-permute-start.41 = (bf16[1600,128]{1,0:T(8,128)(2,1)S(1)}, bf16[1600,128]{1,0:T(8,128)(2,1)S(1)}, u32[]{:S(2)}, u32[]{:S(2)}) collective-permute-start(bf16[1600,128]{1,0:T(8,128)(2,1)S(1)} %shard_map.132.mine_ref), channel_id=1, source_target_pairs={{0,4},{4,0},{8,12},{12,8},{16,20},{20,16},{24,28},{28,24},{32,36},... | collective-permute-start | bytes 1228808 | tf_op jit(solution)/shard_map/ppermute | solution.py:459
  323.7 2.7 copy.26
  326.4 4.1 %shard_map.133 = (f32[1024,400]{1,0:T(8,128)S(1)}, f32[8,128]{1,0:T(8,128)}) custom-call(s32[4]{0:T(128)S(1)} %pad_add_fusion.1.refs_0_.at_ref, bf16[1600,128]{1,0:T(8,128)(2,1)S(1)} %shard_map.132.mine_ref, bf16[1600,128]{1,0:T(8,128)(2,1)S(1)} %collective-permute-done.41.other_ref, f32[1024,400]{1,0:T(8,128)S(1)} %copy-done.2, ...), custom_call_target="tpu_custom_call" | custom-call | bytes 1048576 | tf_op jit(solution)/shard_map/pallas_call | solution.py:398
  (117 shorter events, 95.1 us)
Async XLA Ops:
  3.1 22.4 %all-to-all-start = ((s32[64,1,128]{2,1,0:T(1,128)}), s32[64,1,128]{2,1,0:T(1,128)S(1)}, u32[]{:S(2)}, u32[]{:S(2)}) async-start(s32[64,1,128]{2,1,0:T(1,128)} %bitcast.20), calls=%async_computation | async-start | bytes 65536 | tf_op jit(solution)/shard_map/all_to_all | solution.py:408
  29.4 57.1 %all-to-all-start.1 = ((bf16[64,128,128]{2,1,0:T(8,128)(2,1)}), bf16[64,128,128]{2,1,0:T(8,128)(2,1)}, u32[]{:S(2)}, u32[]{:S(2)}) async-start(bf16[64,128,128]{2,1,0:T(8,128)(2,1)} %shard_map.113), calls=%async_computation.1 | async-start | bytes 4194304 | tf_op jit(solution)/shard_map/all_to_all | solution.py:408
  96.5 62.5 %all-to-all-start.2 = ((bf16[64,128,128]{2,1,0:T(8,128)(2,1)}), bf16[64,128,128]{2,1,0:T(8,128)(2,1)}, u32[]{:S(2)}, u32[]{:S(2)}) async-start(bf16[64,128,128]{2,1,0:T(8,128)(2,1)} %get-tuple-element.41), calls=%async_computation.2 | async-start | bytes 4194304 | tf_op jit(solution)/shard_map/all_to_all | solution.py:408
  106.0 5.5 %collective-permute-start.1 = (bf16[400,128]{1,0:T(8,128)(2,1)S(1)}, bf16[400,128]{1,0:T(8,128)(2,1)S(1)}, u32[]{:S(2)}, u32[]{:S(2)}) collective-permute-start(bf16[400,128]{1,0:T(8,128)(2,1)S(1)} %get-tuple-element.45), channel_id=1, source_target_pairs={{0,1},{1,2},{2,3},{3,0},{4,5},{5,6},{6,7},{7,4},{8,9},{9,10},{10,1... | collective-permute-start | bytes 307208 | tf_op jit(solution)/shard_map/ppermute | solution.py:426
  107.3 7.4 %collective-permute-start.2 = (bf16[400,128]{1,0:T(8,128)(2,1)S(1)}, bf16[400,128]{1,0:T(8,128)(2,1)S(1)}, u32[]{:S(2)}, u32[]{:S(2)}) collective-permute-start(bf16[400,128]{1,0:T(8,128)(2,1)S(1)} %get-tuple-element.46), channel_id=1, source_target_pairs={{0,2},{1,3},{2,0},{3,1},{4,6},{5,7},{6,4},{7,5},{8,10},{9,11},{10,... | collective-permute-start | bytes 307208 | tf_op jit(solution)/shard_map/ppermute | solution.py:426
  115.3 5.4 %collective-permute-start.4 = (f32[112,128]{1,0:T(8,128)S(1)}, f32[112,128]{1,0:T(8,128)S(1)}, u32[]{:S(2)}, u32[]{:S(2)}) collective-permute-start(f32[112,128]{1,0:T(8,128)S(1)} %get-tuple-element.49), channel_id=1, source_target_pairs={{0,64},{4,68},{8,72},{12,76},{16,80},{20,84},{24,88},{28,92},{32,9... | collective-permute-start | bytes 172040 | tf_op jit(solution)/shard_map/ppermute | solution.py:427
  123.6 26.7 %collective-permute-start.7 = (bf16[112,128]{1,0:T(8,128)(2,1)S(1)}, bf16[112,128]{1,0:T(8,128)(2,1)S(1)}, u32[]{:S(2)}, u32[]{:S(2)}) collective-permute-start(bf16[112,128]{1,0:T(8,128)(2,1)S(1)} %shard_map.118.refs_0_), channel_id=1, source_target_pairs={{0,8},{4,12},{8,16},{12,20},{16,24},{20,28},{24,32},{28,36},{32,40... | collective-permute-start | bytes 86024 | tf_op jit(solution)/shard_map/ppermute | solution.py:427
  125.3 27.4 %collective-permute-start.8 = (bf16[112,128]{1,0:T(8,128)(2,1)S(1)}, bf16[112,128]{1,0:T(8,128)(2,1)S(1)}, u32[]{:S(2)}, u32[]{:S(2)}) collective-permute-start(bf16[112,128]{1,0:T(8,128)(2,1)S(1)} %shard_map.118.refs_0_), channel_id=1, source_target_pairs={{0,16},{4,20},{8,24},{12,28},{16,32},{20,36},{24,40},{28,44},{32,4... | collective-permute-start | bytes 86024 | tf_op jit(solution)/shard_map/ppermute | solution.py:427
  128.8 26.2 %collective-permute-start.9 = (bf16[112,128]{1,0:T(8,128)(2,1)S(1)}, bf16[112,128]{1,0:T(8,128)(2,1)S(1)}, u32[]{:S(2)}, u32[]{:S(2)}) collective-permute-start(bf16[112,128]{1,0:T(8,128)(2,1)S(1)} %shard_map.118.refs_0_), channel_id=1, source_target_pairs={{0,24},{4,28},{8,32},{12,36},{16,40},{20,44},{24,48},{28,52},{32,5... | collective-permute-start | bytes 86024 | tf_op jit(solution)/shard_map/ppermute | solution.py:427
  130.7 27.8 %collective-permute-start.10 = (bf16[112,128]{1,0:T(8,128)(2,1)S(1)}, bf16[112,128]{1,0:T(8,128)(2,1)S(1)}, u32[]{:S(2)}, u32[]{:S(2)}) collective-permute-start(bf16[112,128]{1,0:T(8,128)(2,1)S(1)} %shard_map.118.refs_0_), channel_id=1, source_target_pairs={{0,32},{4,36},{8,40},{12,44},{16,48},{20,52},{24,56},{28,60},{32,0... | collective-permute-start | bytes 86024 | tf_op jit(solution)/shard_map/ppermute | solution.py:427
  133.1 25.3 %collective-permute-start.11 = (bf16[112,128]{1,0:T(8,128)(2,1)S(1)}, bf16[112,128]{1,0:T(8,128)(2,1)S(1)}, u32[]{:S(2)}, u32[]{:S(2)}) collective-permute-start(bf16[112,128]{1,0:T(8,128)(2,1)S(1)} %shard_map.118.refs_0_), channel_id=1, source_target_pairs={{0,40},{4,44},{8,48},{12,52},{16,56},{20,60},{24,0},{28,4},{32,8},... | collective-permute-start | bytes 86024 | tf_op jit(solution)/shard_map/ppermute | solution.py:427
  150.3 8.1 %collective-permute-start.12 = (bf16[112,128]{1,0:T(8,128)(2,1)S(1)}, bf16[112,128]{1,0:T(8,128)(2,1)S(1)}, u32[]{:S(2)}, u32[]{:S(2)}) collective-permute-start(bf16[112,128]{1,0:T(8,128)(2,1)S(1)} %shard_map.118.refs_0_), channel_id=1, source_target_pairs={{0,48},{4,52},{8,56},{12,60},{16,0},{20,4},{24,8},{28,12},{32,16},... | collective-permute-start | bytes 86024 | tf_op jit(solution)/shard_map/ppermute | solution.py:427
  152.7 5.7 %collective-permute-start.13 = (bf16[112,128]{1,0:T(8,128)(2,1)S(1)}, bf16[112,128]{1,0:T(8,128)(2,1)S(1)}, u32[]{:S(2)}, u32[]{:S(2)}) collective-permute-start(bf16[112,128]{1,0:T(8,128)(2,1)S(1)} %shard_map.118.refs_0_), channel_id=1, source_target_pairs={{0,56},{4,60},{8,0},{12,4},{16,8},{20,12},{24,16},{28,20},{32,24},... | collective-permute-start | bytes 86024 | tf_op jit(solution)/shard_map/ppermute | solution.py:427
  168.5 59.0 %all-to-all-start.3 = ((bf16[64,128,128]{2,1,0:T(8,128)(2,1)}), bf16[64,128,128]{2,1,0:T(8,128)(2,1)}, u32[]{:S(2)}, u32[]{:S(2)}) async-start(bf16[64,128,128]{2,1,0:T(8,128)(2,1)} %get-tuple-element.52), calls=%async_computation.3 | async-start | bytes 4194304 | tf_op jit(solution)/shard_map/all_to_all | solution.py:408
  176.3 7.9 %collective-permute-start.14 = (f32[112,128]{1,0:T(8,128)S(1)}, f32[112,128]{1,0:T(8,128)S(1)}, u32[]{:S(2)}, u32[]{:S(2)}) collective-permute-start(f32[112,128]{1,0:T(8,128)S(1)} %shard_map.119.refs_5_.refs_0_), channel_id=1, source_target_pairs={{0,64},{4,68},{8,72},{12,76},{16,80},{20,84},{24,88},{28,92},{32,9... | collective-permute-start | bytes 172040 | tf_op jit(solution)/shard_map/ppermute | solution.py:427
  177.8 9.5 %collective-permute-start.15 = (f32[112,128]{1,0:T(8,128)S(1)}, f32[112,128]{1,0:T(8,128)S(1)}, u32[]{:S(2)}, u32[]{:S(2)}) collective-permute-start(f32[112,128]{1,0:T(8,128)S(1)} %shard_map.119.refs_5_.refs_0_), channel_id=1, source_target_pairs={{0,128},{4,132},{8,136},{12,140},{16,144},{20,148},{24,152},{28,15... | collective-permute-start | bytes 172040 | tf_op jit(solution)/shard_map/ppermute | solution.py:427
  180.4 6.9 %collective-permute-start.16 = (f32[112,128]{1,0:T(8,128)S(1)}, f32[112,128]{1,0:T(8,128)S(1)}, u32[]{:S(2)}, u32[]{:S(2)}) collective-permute-start(f32[112,128]{1,0:T(8,128)S(1)} %shard_map.119.refs_5_.refs_0_), channel_id=1, source_target_pairs={{0,192},{4,196},{8,200},{12,204},{16,208},{20,212},{24,216},{28,22... | collective-permute-start | bytes 172040 | tf_op jit(solution)/shard_map/ppermute | solution.py:427
  189.2 7.1 %collective-permute-start.18 = (bf16[400,128]{1,0:T(8,128)(2,1)S(1)}, bf16[400,128]{1,0:T(8,128)(2,1)S(1)}, u32[]{:S(2)}, u32[]{:S(2)}) collective-permute-start(bf16[400,128]{1,0:T(8,128)(2,1)S(1)} %shard_map.121.refs_0_), channel_id=1, source_target_pairs={{0,2},{1,3},{2,0},{3,1},{4,6},{5,7},{6,4},{7,5},{8,10},{9,11},{10,... | collective-permute-start | bytes 307208 | tf_op jit(solution)/shard_map/ppermute | solution.py:426
  236.6 74.1 %all-to-all-start.4 = ((bf16[64,128,128]{2,1,0:T(8,128)(2,1)}), bf16[64,128,128]{2,1,0:T(8,128)(2,1)}, u32[]{:S(2)}, u32[]{:S(2)}) async-start(bf16[64,128,128]{2,1,0:T(8,128)(2,1)} %get-tuple-element.55), calls=%async_computation.4 | async-start | bytes 4194304 | tf_op jit(solution)/shard_map/all_to_all | solution.py:408
  245.9 5.5 %collective-permute-start.22 = (bf16[400,128]{1,0:T(8,128)(2,1)S(1)}, bf16[400,128]{1,0:T(8,128)(2,1)S(1)}, u32[]{:S(2)}, u32[]{:S(2)}) collective-permute-start(bf16[400,128]{1,0:T(8,128)(2,1)S(1)} %get-tuple-element.60), channel_id=1, source_target_pairs={{0,1},{1,2},{2,3},{3,0},{4,5},{5,6},{6,7},{7,4},{8,9},{9,10},{10,1... | collective-permute-start | bytes 307208 | tf_op jit(solution)/shard_map/ppermute | solution.py:426
  247.2 7.4 %collective-permute-start.23 = (bf16[400,128]{1,0:T(8,128)(2,1)S(1)}, bf16[400,128]{1,0:T(8,128)(2,1)S(1)}, u32[]{:S(2)}, u32[]{:S(2)}) collective-permute-start(bf16[400,128]{1,0:T(8,128)(2,1)S(1)} %get-tuple-element.61), channel_id=1, source_target_pairs={{0,2},{1,3},{2,0},{3,1},{4,6},{5,7},{6,4},{7,5},{8,10},{9,11},{10,... | collective-permute-start | bytes 307208 | tf_op jit(solution)/shard_map/ppermute | solution.py:426
  263.7 26.7 %collective-permute-start.28 = (bf16[112,128]{1,0:T(8,128)(2,1)S(1)}, bf16[112,128]{1,0:T(8,128)(2,1)S(1)}, u32[]{:S(2)}, u32[]{:S(2)}) collective-permute-start(bf16[112,128]{1,0:T(8,128)(2,1)S(1)} %shard_map.128.refs_0_), channel_id=1, source_target_pairs={{0,8},{4,12},{8,16},{12,20},{16,24},{20,28},{24,32},{28,36},{32,40... | collective-permute-start | bytes 86024 | tf_op jit(solution)/shard_map/ppermute | solution.py:427
  265.3 27.5 %collective-permute-start.29 = (bf16[112,128]{1,0:T(8,128)(2,1)S(1)}, bf16[112,128]{1,0:T(8,128)(2,1)S(1)}, u32[]{:S(2)}, u32[]{:S(2)}) collective-permute-start(bf16[112,128]{1,0:T(8,128)(2,1)S(1)} %shard_map.128.refs_0_), channel_id=1, source_target_pairs={{0,16},{4,20},{8,24},{12,28},{16,32},{20,36},{24,40},{28,44},{32,4... | collective-permute-start | bytes 86024 | tf_op jit(solution)/shard_map/ppermute | solution.py:427
  268.3 26.8 %collective-permute-start.30 = (bf16[112,128]{1,0:T(8,128)(2,1)S(1)}, bf16[112,128]{1,0:T(8,128)(2,1)S(1)}, u32[]{:S(2)}, u32[]{:S(2)}) collective-permute-start(bf16[112,128]{1,0:T(8,128)(2,1)S(1)} %shard_map.128.refs_0_), channel_id=1, source_target_pairs={{0,24},{4,28},{8,32},{12,36},{16,40},{20,44},{24,48},{28,52},{32,5... | collective-permute-start | bytes 86024 | tf_op jit(solution)/shard_map/ppermute | solution.py:427
  270.6 28.0 %collective-permute-start.31 = (bf16[112,128]{1,0:T(8,128)(2,1)S(1)}, bf16[112,128]{1,0:T(8,128)(2,1)S(1)}, u32[]{:S(2)}, u32[]{:S(2)}) collective-permute-start(bf16[112,128]{1,0:T(8,128)(2,1)S(1)} %shard_map.128.refs_0_), channel_id=1, source_target_pairs={{0,32},{4,36},{8,40},{12,44},{16,48},{20,52},{24,56},{28,60},{32,0... | collective-permute-start | bytes 86024 | tf_op jit(solution)/shard_map/ppermute | solution.py:427
  273.0 25.5 %collective-permute-start.32 = (bf16[112,128]{1,0:T(8,128)(2,1)S(1)}, bf16[112,128]{1,0:T(8,128)(2,1)S(1)}, u32[]{:S(2)}, u32[]{:S(2)}) collective-permute-start(bf16[112,128]{1,0:T(8,128)(2,1)S(1)} %shard_map.128.refs_0_), channel_id=1, source_target_pairs={{0,40},{4,44},{8,48},{12,52},{16,56},{20,60},{24,0},{28,4},{32,8},... | collective-permute-start | bytes 86024 | tf_op jit(solution)/shard_map/ppermute | solution.py:427
  290.4 8.1 %collective-permute-start.33 = (bf16[112,128]{1,0:T(8,128)(2,1)S(1)}, bf16[112,128]{1,0:T(8,128)(2,1)S(1)}, u32[]{:S(2)}, u32[]{:S(2)}) collective-permute-start(bf16[112,128]{1,0:T(8,128)(2,1)S(1)} %shard_map.128.refs_0_), channel_id=1, source_target_pairs={{0,48},{4,52},{8,56},{12,60},{16,0},{20,4},{24,8},{28,12},{32,16},... | collective-permute-start | bytes 86024 | tf_op jit(solution)/shard_map/ppermute | solution.py:427
  292.8 5.7 %collective-permute-start.34 = (bf16[112,128]{1,0:T(8,128)(2,1)S(1)}, bf16[112,128]{1,0:T(8,128)(2,1)S(1)}, u32[]{:S(2)}, u32[]{:S(2)}) collective-permute-start(bf16[112,128]{1,0:T(8,128)(2,1)S(1)} %shard_map.128.refs_0_), channel_id=1, source_target_pairs={{0,56},{4,60},{8,0},{12,4},{16,8},{20,12},{24,16},{28,20},{32,24},... | collective-permute-start | bytes 86024 | tf_op jit(solution)/shard_map/ppermute | solution.py:427
  305.6 12.5 %collective-permute-start.38 = (bf16[400,128]{1,0:T(8,128)(2,1)S(1)}, bf16[400,128]{1,0:T(8,128)(2,1)S(1)}, u32[]{:S(2)}, u32[]{:S(2)}) collective-permute-start(bf16[400,128]{1,0:T(8,128)(2,1)S(1)} %shard_map.130.refs_5_.refs_0_), channel_id=1, source_target_pairs={{0,1},{1,2},{2,3},{3,0},{4,5},{5,6},{6,7},{7,4},{8,9},{9,10},{10,1... | collective-permute-start | bytes 307208 | tf_op jit(solution)/shard_map/ppermute | solution.py:426
  306.9 11.2 %collective-permute-start.39 = (bf16[400,128]{1,0:T(8,128)(2,1)S(1)}, bf16[400,128]{1,0:T(8,128)(2,1)S(1)}, u32[]{:S(2)}, u32[]{:S(2)}) collective-permute-start(bf16[400,128]{1,0:T(8,128)(2,1)S(1)} %shard_map.130.refs_5_.refs_0_), channel_id=1, source_target_pairs={{0,2},{1,3},{2,0},{3,1},{4,6},{5,7},{6,4},{7,5},{8,10},{9,11},{10,... | collective-permute-start | bytes 307208 | tf_op jit(solution)/shard_map/ppermute | solution.py:426
  309.3 8.8 %collective-permute-start.40 = (bf16[400,128]{1,0:T(8,128)(2,1)S(1)}, bf16[400,128]{1,0:T(8,128)(2,1)S(1)}, u32[]{:S(2)}, u32[]{:S(2)}) collective-permute-start(bf16[400,128]{1,0:T(8,128)(2,1)S(1)} %shard_map.130.refs_5_.refs_0_), channel_id=1, source_target_pairs={{0,3},{1,0},{2,1},{3,2},{4,7},{5,4},{6,5},{7,6},{8,11},{9,8},{10,9... | collective-permute-start | bytes 307208 | tf_op jit(solution)/shard_map/ppermute | solution.py:426
  319.4 7.0 %collective-permute-start.41 = (bf16[1600,128]{1,0:T(8,128)(2,1)S(1)}, bf16[1600,128]{1,0:T(8,128)(2,1)S(1)}, u32[]{:S(2)}, u32[]{:S(2)}) collective-permute-start(bf16[1600,128]{1,0:T(8,128)(2,1)S(1)} %shard_map.132.mine_ref), channel_id=1, source_target_pairs={{0,4},{4,0},{8,12},{12,8},{16,20},{20,16},{24,28},{28,24},{32,36},... | collective-permute-start | bytes 1228808 | tf_op jit(solution)/shard_map/ppermute | solution.py:459
  (23 other events, 176.6 us)

commit v5 on v4

--- a/solution.py
+++ b/solution.py
@@ -16,6 +16,7 @@
 REL = 1024
 DENSE = REL // 64 * 200
 WIRE_PARTS = 4
+FIRST_ROWS = 2 * CAP
 Y_ROWS = 112
 
 
@@ -86,7 +87,17 @@
     ]
 
 
-def unpack_all(copies, held_ref, rows_ref):
+def unpack_first(block):
+    return jnp.concatenate([block[:CAP], block[CAP:]], axis=1)
+
+
+def unpack_second(block):
+    group = iota((8, 128), 1) // 16
+    tail = jnp.concatenate([jnp.where(group == i, block[CAP:], 0.0) for i in range(5)], axis=0)
+    return jnp.concatenate([block[:CAP], tail], axis=1)
+
+
+def unpack_all(copies, held_ref, rows_ref, unpack=unpack):
     per = OWN // WIRE_PARTS // 2
     for g, copy in enumerate(copies):
         copy.wait()
@@ -177,12 +188,20 @@
     gather_rows(named_ref, 0, wide_ref, wire_ref, held_ref, sems)
 
 
-def update(step, last, wire_in_ref, flat_ref, table_ref, accum_ref, named_ref, _, *rest):
-    if last:
-        new_table_ref, new_accum_ref, in_sems, table_sem, out_sems, held_ref, rows_ref, grads_ref = rest
-    else:
-        new_table_ref, new_accum_ref, wire_ref, in_sems, table_sem, out_sems, held_ref, rows_ref, grads_ref, *rest = rest
-        wide_ref, sent_ref, sent_sems = rest
+def apply_rows(b, total, accum_ref, new_accum_ref, rows_ref):
+    rows = slice(128 * b, 128 * b + 128)
+    accum = lane_to_column(accum_ref[b : b + 1, :])
+    accum = accum + jnp.sum(total * total, axis=1, keepdims=True) / WIDTH
+    new_accum_ref[b : b + 1, :] = jnp.transpose(accum)[:1]
+    new = rows_ref[rows, :] - total * (RATE * lax.rsqrt(accum[:, :1]))
+    rows_ref[rows, :] = new
+    return new
+
+
+def update(
+    step, wire_in_ref, flat_ref, table_ref, accum_ref, named_ref, _, new_table_ref, new_accum_ref, wire_ref,
+    in_sems, table_sem, out_sems, held_ref, rows_ref, grads_ref, wide_ref, sent_ref, sent_sems,
+):
     copies = wire_copies(wire_in_ref, held_ref, in_sems)
     for copy in copies:
         copy.start()
@@ -192,24 +211,53 @@
     table_copy.wait()
     outs = []
     for b in range(8):
-        rows = slice(128 * b, 128 * b + 128)
+        here = pl.ds(128 * b, 128)
         hit = one_hot(iota((128, SLOTS), 0) + 128 * b == flat_ref[step : step + 1, :])
-        total = dot(hit, grads_ref[...])
-        total = to_narrow(total)
-        accum = lane_to_column(accum_ref[b : b + 1, :])
-        accum = accum + jnp.sum(total * total, axis=1, keepdims=True) / WIDTH
-        new_accum_ref[b : b + 1, :] = jnp.transpose(accum)[:1]
-        new = rows_ref[rows, :] - total * (RATE * lax.rsqrt(accum[:, :1]))
-        rows_ref[rows, :] = new
-        here = pl.ds(128 * b, 128)
+        total = to_narrow(dot(hit, grads_ref[...]))
+        new = apply_rows(b, total, accum_ref, new_accum_ref, rows_ref)
         outs.append(pltpu.make_async_copy(rows_ref.at[here], new_table_ref.at[0, here], out_sems.at[b]))
         outs[-1].start()
-        if not last:
-            wide_ref[rows, :] = to_wide(new).astype(BF16)
-    if not last:
-        gather_rows(named_ref, step + 1, wide_ref, wire_ref, sent_ref, sent_sems)
+        wide_ref[here, :] = to_wide(new).astype(BF16)
+    gather_rows(named_ref, step + 1, wide_ref, wire_ref, sent_ref, sent_sems)
     for copy in outs:
         copy.wait()
+
+
+def first_sums(step, wire_in_ref, flat_ref, sums_ref, in_sems, held_ref, grads_ref):
+    copies = wire_copies(wire_in_ref, held_ref, in_sems)
+    for copy in copies:
+        copy.start()
+    unpack_all(copies, held_ref, grads_ref, unpack_first)
+    for b in range(8):
+        hit = one_hot(iota((128, SLOTS), 0) + 128 * b == flat_ref[step : step + 1, :])
+        sums_ref[128 * b : 128 * b + 128, :] = dot(hit, grads_ref[...])
+
+
+def last_update(
+    step, wire_in_ref, flat_ref, sums_ref, table_ref, accum_ref, new_table_ref, new_accum_ref,
+    in_sems, table_sem, out_sems, held_ref, rows_ref, grads_ref,
+):
+    copies = wire_copies(wire_in_ref, held_ref, in_sems)
+    for copy in copies:
+        copy.start()
+    table_copy = pltpu.make_async_copy(table_ref.at[0], rows_ref, table_sem)
+    table_copy.start()
+    unpack_all(copies, held_ref, grads_ref, unpack_second)
+    table_copy.wait()
+    outs = []
+    for b in range(8):
+        here = pl.ds(128 * b, 128)
+        hit = one_hot(iota((128, SLOTS), 0) + 128 * b == flat_ref[step : step + 1, :])
+        total = to_narrow(jnp.concatenate([sums_ref[here, :], dot(hit, grads_ref[...])], axis=1))
+        apply_rows(b, total, accum_ref, new_accum_ref, rows_ref)
+        outs.append(pltpu.make_async_copy(rows_ref.at[here], new_table_ref.at[0, here], out_sems.at[b]))
+        outs[-1].start()
+    for copy in outs:
+        copy.wait()
+
+
+def pass_on(ref, after_ref, out_ref):
+    del ref, after_ref, out_ref
 
 
 def complex_parts(x):
@@ -235,9 +283,9 @@
 
 
 def block(
-    step, at_ref, wire_in_ref, slots_ref, negative_ref, relation_ref, rel_ids_ref,
-    wire_ref, keep_ref, give_ref, rows_ref, weights_ref, held_ref, in_sems, sent_ref, out_sems,
+    step, at_ref, wire_in_ref, slots_ref, negative_ref, relation_ref, rel_ids_ref, *rest
 ):
+    *wire_refs, keep_ref, give_ref, rows_ref, weights_ref, held_ref, in_sems, sent_ref, out_sems = rest
     edges, parts = 128, 4
     part = SLOTS // parts
     per = OWN // parts
@@ -288,8 +336,14 @@
         for j in range(per):
             sent_ref[per * g + j] = pack(grads[CAP * j : CAP * j + CAP]).astype(BF16)
         blocks = pl.ds(per * g, per)
-        outs.append(pltpu.make_async_copy(sent_ref.at[blocks], wire_ref.at[blocks], out_sems.at[g]))
-        outs[-1].start()
+        start = 0
+        for k, wire_ref in enumerate(wire_refs):
+            dense = pl.ds(start, wire_ref.shape[1])
+            start += wire_ref.shape[1]
+            outs.append(
+                pltpu.make_async_copy(sent_ref.at[blocks, dense], wire_ref.at[blocks], out_sems.at[k, g])
+            )
+            outs[-1].start()
     grad_relation = to_wide(
         join(
             pull_re * head_re + pull_im * head_im + push_re * tail_re + push_im * tail_im,
@@ -355,7 +409,7 @@
     out_ref[...] = all_ref[: out_ref.shape[0], :].astype(BF16)
 
 
-def gather_x(at_ref, _, *refs):
+def gather_x(at_ref, *refs):
     *parts, out_ref = refs
     rows = parts[0].shape[0]
     for d in range(4):
@@ -385,13 +439,14 @@
 }
 
 
-def kernel(body, ins, outs, places, scratch=(), flops=0):
+def kernel(body, ins, outs, places, scratch=(), flops=0, aliases=None):
     call = pl.pallas_call(
         body,
         out_shape=[pltpu.HBM(o.shape, o.dtype) if k == "h" else o for o, k in zip(outs, places)],
         in_specs=[SPACES[k] for k in ins],
         out_specs=[SPACES[k] for k in places],
         scratch_shapes=scratch,
+        input_output_aliases=aliases or {},
         compiler_params=pltpu.CompilerParams(vmem_limit_bytes=40 << 20),
         cost_estimate=pl.CostEstimate(flops=flops, bytes_accessed=1 << 20, transcendentals=0),
     )
@@ -452,9 +507,9 @@
     )(at, own, *[move(own, 1, d) for d in (1, 2, 3)])[0]
 
 
-def relation_gather_x(at, own, after):
-    own = kernel(gather_x, "savvvv", [jax.ShapeDtypeStruct((DENSE // 2, 128), BF16)], "v")(
-        at, after, own, *[move(own, 0, d) for d in (1, 2, 3)]
+def relation_gather_x(at, own):
+    own = kernel(gather_x, "svvvv", [jax.ShapeDtypeStruct((DENSE // 2, 128), BF16)], "v")(
+        at, own, *[move(own, 0, d) for d in (1, 2, 3)]
     )[0]
     return own, lax.ppermute(own, "edge", edge_pairs(0, 0, 1))
 
@@ -489,34 +544,54 @@
         )(rel_table, rel_ids)[0]
         rows = exchange(rows)
         dense = shape((DENSE // 2, 128), F32)
-        grads, keep, give = kernel(
+        wires = [shape((OWN, n, 128), BF16) for n in ((FIRST_ROWS, 128 - FIRST_ROWS) if last else (128,))]
+        *grads, keep, give = kernel(
             lambda *refs, s=s: block(s, *refs),
             "shvvvv",
-            [wire, dense, dense],
-            "hvv",
-            [pltpu.VMEM((SLOTS, 512), BF16), pltpu.VMEM((256, SLOTS), BF16), held, copies(WIRE_PARTS), held, copies(4)],
+            wires + [dense, dense],
+            "h" * len(wires) + "vv",
+            [
+                pltpu.VMEM((SLOTS, 512), BF16), pltpu.VMEM((256, SLOTS), BF16), held, copies(WIRE_PARTS), held,
+                pltpu.SemaphoreType.DMA((2, 4)),
+            ],
             4 << 30,
         )(at, rows, slots, negative, relation, rel_ids)
-        grads = exchange(grads)
+        grads[0] = exchange(grads[0])
         own = relation_scatter(at, keep, give)
+        scratch = [copies(WIRE_PARTS), pltpu.SemaphoreType.DMA, copies(8)]
+        outs = [shape(table.shape, F32), shape((8, 128), F32)]
         if last:
-            own = relation_gather_y(at, own)
-        scratch = [copies(WIRE_PARTS), pltpu.SemaphoreType.DMA, copies(8), held]
-        scratch += [pltpu.VMEM((1024, WIDTH), F32), pltpu.VMEM((SLOTS, 512), BF16)]
-        if not last:
-            scratch += [pltpu.VMEM((1024, 512), BF16), held, copies(8)]
-        table, accum, *rows = kernel(
-            lambda *refs, s=s, last=last: update(s, last, *refs),
-            "hvhvva",
-            [shape(table.shape, F32), shape((8, 128), F32)] + ([] if last else [wire]),
-            "hv" if last else "hvh",
-            scratch,
-            5 << 30,
-        )(grads, flat, table, accum, named, own)
-        rows = None if last else rows[0]
-        if not last:
-            own = relation_gather_y(at, own)
-        mine, other = relation_gather_x(at, own, accum)
+            second = kernel(pass_on, "ha", [wires[1]], "h", aliases={0: 0})(grads[1], own)[0]
+            second = exchange(second)
+            sums = kernel(
+                lambda *refs, s=s: first_sums(s, *refs),
+                "hv",
+                [shape((1024, 256), F32)],
+                "v",
+                [copies(WIRE_PARTS), pltpu.VMEM((OWN, FIRST_ROWS, 128), BF16), pltpu.VMEM((SLOTS, 256), BF16)],
+                2 << 30,
+            )(grads[0], flat)[0]
+            scratch += [pltpu.VMEM((OWN, 128 - FIRST_ROWS, 128), BF16), pltpu.VMEM((1024, WIDTH), F32)]
+            table, accum = kernel(
+                lambda *refs, s=s: last_update(s, *refs),
+                "hvvhv",
+                outs,
+                "hv",
+                scratch + [pltpu.VMEM((SLOTS, 256), BF16)],
+                2 << 30,
+            )(second, flat, sums, table, accum)
+        else:
+            scratch += [held, pltpu.VMEM((1024, WIDTH), F32), pltpu.VMEM((SLOTS, 512), BF16)]
+            table, accum, rows = kernel(
+                lambda *refs, s=s: update(s, *refs),
+                "hvhvva",
+                outs + [wire],
+                "hvh",
+                scratch + [pltpu.VMEM((1024, 512), BF16), held, copies(8)],
+                5 << 30,
+            )(grads[0], flat, table, accum, named, own)
+        own = relation_gather_y(at, own)
+        mine, other = relation_gather_x(at, own)
         rel_table, rel_state = kernel(
             relation_update, "svvvv", [shape((REL, WIDTH), F32), shape((8, 128), F32)], "vv"
         )(at, mine, other, rel_table, rel_state)

time: 338 us -> 338 us (level)
  waiting for transfers between devices: 144 us -> 134 us
  starting transfers between devices: 116 us -> 125 us
    ppermute x26, waiting for transfers between devices: 52.9 us -> 38.6 us  [move(): lax.ppermute(x, 'edge', edge_pairs(d if axis == 1 else 0, d if axis == 2...]
    all_to_all x5 -> x6, starting transfers between devices: 39.1 us -> 50.7 us  [exchange(): return lax.all_to_all(x, 'edge', split_axis=0, concat_axis=0, tiled=True)]
    pallas_call x23 -> x25, Pallas kernels: 57.3 us -> 58.8 us  [kernel(): call(*[pltpu.with_memory_space_constraint(x, pltpu.HBM) if k == 'h' else...]
    all_to_all x5 -> x6, waiting for transfers between devices: 74.1 us -> 74 us  [exchange(): return lax.all_to_all(x, 'edge', split_axis=0, concat_axis=0, tiled=True)]
  transfers between devices with their start and end apart: 47 -> 48, of which waited for: 26 -> 29; matrix products, arithmetic and copies ran while one was open for 3% -> 3% of each run, Pallas kernels for 6% -> 6%
where the time goes in v5:
time: 338 us; the launch traced here: 332 us
  waiting for transfers between devices  134 us (40%)
  starting transfers between devices  125 us (37%)
  Pallas kernels  58.8 us (17%)
  local copies, waits for them, and re-layouts  13.9 us (4%)
    all_to_all x6, waiting for transfers between devices, exchange(): return lax.all_to_all(x, 'edge', split_axis=0, concat_axis=0, tiled=True)  74 us
    pallas_call x25, Pallas kernels, kernel(): call(*[pltpu.with_memory_space_constraint(x, pltpu.HBM) if k == 'h' else...  58.8 us
    all_to_all x6, starting transfers between devices, exchange(): return lax.all_to_all(x, 'edge', split_axis=0, concat_axis=0, tiled=True)  50.7 us
    ppermute x26, starting transfers between devices, move(): lax.ppermute(x, 'edge', edge_pairs(d if axis == 1 else 0, d if axis == 2...  49.9 us
    ppermute x26, waiting for transfers between devices, move(): lax.ppermute(x, 'edge', edge_pairs(d if axis == 1 else 0, d if axis == 2...  38.6 us
    ppermute x12, starting transfers between devices, move(): return lax.ppermute(x, 'rep', [(k, (k + d) % 4) for k in range(4)])  18.7 us
    ppermute x12, waiting for transfers between devices, move(): return lax.ppermute(x, 'rep', [(k, (k + d) % 4) for k in range(4)])  14 us
    unnamed x20, local copies, waits for them, and re-layouts  11.5 us
  transfers between devices with their start and end apart: 48, of which 29 were waited for; matrix products, arithmetic and copies ran while one was open for 3% of the time, Pallas kernels for 6%

profile of v5, /device:TPU:1, one launch (start us, length us, event | category | flops | bytes accessed | tf_op | source)
XLA Modules:
  0.0 332.4 jit_solution(9690749056567930528)
XLA Ops:
  3.1 13.2 %all-to-all-start = ((s32[64,1,128]{2,1,0:T(1,128)}), s32[64,1,128]{2,1,0:T(1,128)S(1)}, u32[]{:S(2)}, u32[]{:S(2)}) async-start(s32[64,1,128]{2,1,0:T(1,128)} %bitcast.18), calls=%async_computation | async-start | bytes 65536 | tf_op jit(solution)/shard_map/all_to_all | solution.py:463
  18.6 6.8 %all-to-all-done = s32[64,1,128]{2,1,0:T(1,128)S(1)} async-done(((s32[64,1,128]{2,1,0:T(1,128)}), s32[64,1,128]{2,1,0:T(1,128)S(1)}, u32[]{:S(2)}, u32[]{:S(2)}) %all-to-all-start) | async-done | bytes 32800 | tf_op jit(solution)/shard_map/all_to_all | solution.py:463
  25.5 3.9 %shard_map.113 = bf16[64,128,128]{2,1,0:T(8,128)(2,1)} custom-call(bf16[1024,512]{1,0:T(8,128)(2,1)S(1)} %shard_map.111.wide_ref, s32[64,128]{1,0:T(8,128)S(1)} %bitcast.14), custom_call_target="tpu_custom_call" | custom-call | flops 3221225472 | bytes 1048576 | tf_op jit(solution)/shard_map/pallas_call | solution.py:453
  29.4 6.0 %all-to-all-start.1 = ((bf16[64,128,128]{2,1,0:T(8,128)(2,1)}), bf16[64,128,128]{2,1,0:T(8,128)(2,1)}, u32[]{:S(2)}, u32[]{:S(2)}) async-start(bf16[64,128,128]{2,1,0:T(8,128)(2,1)} %shard_map.113), calls=%async_computation.1 | async-start | bytes 4194304 | tf_op jit(solution)/shard_map/all_to_all | solution.py:463
  35.7 2.9 copy.25
  41.3 45.2 %all-to-all-done.1.refs_1_ = bf16[64,128,128]{2,1,0:T(8,128)(2,1)} async-done(((bf16[64,128,128]{2,1,0:T(8,128)(2,1)}), bf16[64,128,128]{2,1,0:T(8,128)(2,1)}, u32[]{:S(2)}, u32[]{:S(2)}) %all-to-all-start.1) | async-done | bytes 2097184 | tf_op jit(solution)/shard_map/all_to_all | solution.py:463
  86.5 9.2 %shard_map.115 = (bf16[64,128,128]{2,1,0:T(8,128)(2,1)}, f32[1600,128]{1,0:T(8,128)S(1)}, f32[1600,128]{1,0:T(8,128)S(1)}) custom-call(s32[4]{0:T(128)S(1)} %pad_add_fusion.1.refs_0_.at_ref, bf16[64,128,128]{2,1,0:T(8,128)(2,1)} %all-to-all-done.1.refs_1_, s32[2,256]{1,0:T(2,128)S(1)} %get-tuple-element.40.refs_2_, f32[2,2560]{1,0:T(2,128)S(1)} %pad_maximum_fusion.refs_3_, ...), custom_call_target="tpu_custom_call" | custom-call | flops 4294967296 | bytes 1048576 | tf_op jit(solution)/shard_map/pallas_call | solution.py:453
  96.6 6.0 %all-to-all-start.2 = ((bf16[64,128,128]{2,1,0:T(8,128)(2,1)}), bf16[64,128,128]{2,1,0:T(8,128)(2,1)}, u32[]{:S(2)}, u32[]{:S(2)}) async-start(bf16[64,128,128]{2,1,0:T(8,128)(2,1)} %get-tuple-element.42), calls=%async_computation.2 | async-start | bytes 4194304 | tf_op jit(solution)/shard_map/all_to_all | solution.py:463
  111.6 3.2 collective-permute-done.2.refs_3_
  125.3 3.3 collective-permute-start.8
  135.3 15.0 %collective-permute-done.7.refs_1_ = bf16[112,128]{1,0:T(8,128)(2,1)S(1)} collective-permute-done((bf16[112,128]{1,0:T(8,128)(2,1)S(1)}, bf16[112,128]{1,0:T(8,128)(2,1)S(1)}, u32[]{:S(2)}, u32[]{:S(2)}) %collective-permute-start.7) | collective-permute-done | bytes 28704 | tf_op jit(solution)/shard_map/ppermute | solution.py:482
  155.0 3.5 %collective-permute-done.10.refs_4_ = bf16[112,128]{1,0:T(8,128)(2,1)S(1)} collective-permute-done((bf16[112,128]{1,0:T(8,128)(2,1)S(1)}, bf16[112,128]{1,0:T(8,128)(2,1)S(1)}, u32[]{:S(2)}, u32[]{:S(2)}) %collective-permute-start.10) | collective-permute-done | bytes 28704 | tf_op jit(solution)/shard_map/ppermute | solution.py:482
  159.1 9.3 %shard_map.120 = (f32[1,1024,400]{2,1,0:T(8,128)}, f32[8,128]{1,0:T(8,128)S(1)}, bf16[64,128,128]{2,1,0:T(8,128)(2,1)}) custom-call(bf16[64,128,128]{2,1,0:T(8,128)(2,1)} %all-to-all-done.2.refs_0_, s32[2,2560]{1,0:T(2,128)S(1)} %pad_add_fusion.refs_1_, f32[1,1024,400]{2,1,0:T(8,128)} %copy-done, f32[8,128]{1,0:T(8,128)S(1)} %bitcast.17, ...), custom_call_target="tpu_custom_call" | custom-call | flops 5368709120 | bytes 1048576 | tf_op jit(solution)/shard_map/pallas_call | solution.py:453
  168.5 7.9 %all-to-all-start.3 = ((bf16[64,128,128]{2,1,0:T(8,128)(2,1)}), bf16[64,128,128]{2,1,0:T(8,128)(2,1)}, u32[]{:S(2)}, u32[]{:S(2)}) async-start(bf16[64,128,128]{2,1,0:T(8,128)(2,1)} %get-tuple-element.53), calls=%async_computation.3 | async-start | bytes 4194304 | tf_op jit(solution)/shard_map/all_to_all | solution.py:463
  181.5 2.7 collective-permute-done.14.refs_1_
  184.3 3.1 collective-permute-done.15.refs_2_
  193.2 3.2 collective-permute-done.18.refs_2_
  199.7 3.6 %shard_map.123 = (f32[1024,400]{1,0:T(8,128)S(1)}, f32[8,128]{1,0:T(8,128)S(1)}) custom-call(s32[4]{0:T(128)S(1)} %pad_add_fusion.1.refs_0_.at_ref, bf16[1600,128]{1,0:T(8,128)(2,1)S(1)} %shard_map.122.mine_ref, bf16[1600,128]{1,0:T(8,128)(2,1)S(1)} %collective-permute-done.20.other_ref, f32[1024,400]{1,0:T(8,128)S(1)} %pad.8.refs_0_.table_ref, ...), custom_call_target="tpu_custom_call" | custom-call | bytes 1048576 | tf_op jit(solution)/shard_map/pallas_call | solution.py:453
  205.5 22.0 %all-to-all-done.3.refs_1_ = bf16[64,128,128]{2,1,0:T(8,128)(2,1)} async-done(((bf16[64,128,128]{2,1,0:T(8,128)(2,1)}), bf16[64,128,128]{2,1,0:T(8,128)(2,1)}, u32[]{:S(2)}, u32[]{:S(2)}) %all-to-all-start.3) | async-done | bytes 2097184 | tf_op jit(solution)/shard_map/all_to_all | solution.py:463
  227.5 9.2 %shard_map.125 = (bf16[64,80,128]{2,1,0:T(8,128)(2,1)}, bf16[64,48,128]{2,1,0:T(8,128)(2,1)}, f32[1600,128]{1,0:T(8,128)S(1)}, f32[1600,128]{1,0:T(8,128)S(1)}) custom-call(s32[4]{0:T(128)S(1)} %pad_add_fusion.1.refs_0_.at_ref, bf16[64,128,128]{2,1,0:T(8,128)(2,1)} %all-to-all-done.3.refs_1_, s32[2,256]{1,0:T(2,128)S(1)} %get-tuple-element.40.refs_2_, ...), custom_call_target="tpu_custom_call" | custom-call | flops 4294967296 | bytes 1048576 | tf_op jit(solution)/shard_map/pallas_call | solution.py:453
  236.7 5.8 %all-to-all-start.5 = ((bf16[64,80,128]{2,1,0:T(8,128)(2,1)}), bf16[64,80,128]{2,1,0:T(8,128)(2,1)S(1)}, u32[]{:S(2)}, u32[]{:S(2)}) async-start(bf16[64,80,128]{2,1,0:T(8,128)(2,1)} %get-tuple-element.66), calls=%async_computation.5 | async-start | bytes 2621440 | tf_op jit(solution)/shard_map/all_to_all | solution.py:463
  251.1 3.2 collective-permute-done.23.refs_3_
  256.3 2.8 collective-permute-start.26
  260.2 5.3 %collective-permute-done.26.refs_1_ = f32[112,128]{1,0:T(8,128)S(1)} collective-permute-done((f32[112,128]{1,0:T(8,128)S(1)}, f32[112,128]{1,0:T(8,128)S(1)}, u32[]{:S(2)}, u32[]{:S(2)}) %collective-permute-start.26) | collective-permute-done | bytes 57376 | tf_op jit(solution)/shard_map/ppermute | solution.py:482
  267.4 3.2 collective-permute-start.30
  271.6 3.3 %collective-permute-start.32 = (bf16[112,128]{1,0:T(8,128)(2,1)S(1)}, bf16[112,128]{1,0:T(8,128)(2,1)S(1)}, u32[]{:S(2)}, u32[]{:S(2)}) collective-permute-start(bf16[112,128]{1,0:T(8,128)(2,1)S(1)} %shard_map.128.refs_0_), channel_id=1, source_target_pairs={{0,40},{4,44},{8,48},{12,52},{16,56},{20,60},{24,0},{28,4},{32,8},... | collective-permute-start | bytes 86024 | tf_op jit(solution)/shard_map/ppermute | solution.py:482
  274.9 3.2 collective-permute-start.33
  282.3 11.8 %all-to-all-start.4 = ((bf16[64,48,128]{2,1,0:T(8,128)(2,1)}), bf16[64,48,128]{2,1,0:T(8,128)(2,1)}, u32[]{:S(2)}, u32[]{:S(2)}) async-start(bf16[64,48,128]{2,1,0:T(8,128)(2,1)} %shard_map.130), calls=%async_computation.4 | async-start | bytes 1572864 | tf_op jit(solution)/shard_map/all_to_all | solution.py:463
  314.5 4.1 %shard_map.135 = (f32[1024,400]{1,0:T(8,128)S(1)}, f32[8,128]{1,0:T(8,128)}) custom-call(s32[4]{0:T(128)S(1)} %pad_add_fusion.1.refs_0_.at_ref, bf16[1600,128]{1,0:T(8,128)(2,1)S(1)} %shard_map.134.mine_ref, bf16[1600,128]{1,0:T(8,128)(2,1)S(1)} %collective-permute-done.41.other_ref, f32[1024,400]{1,0:T(8,128)S(1)} %copy-done.2, ...), custom_call_target="tpu_custom_call" | custom-call | bytes 1048576 | tf_op jit(solution)/shard_map/pallas_call | solution.py:453
  320.5 2.9 shard_map.131.refs_2_
  323.4 5.8 %shard_map.132 = (f32[1,1024,400]{2,1,0:T(8,128)}, f32[8,128]{1,0:T(8,128)}) custom-call(bf16[64,48,128]{2,1,0:T(8,128)(2,1)} %all-to-all-done.4.refs_0_, s32[2,2560]{1,0:T(2,128)S(1)} %pad_add_fusion.refs_1_, f32[1024,256]{1,0:T(8,128)S(1)} %shard_map.131.refs_2_, f32[1,1024,400]{2,1,0:T(8,128)} %get-tuple-element.67.refs_3_, ...), custom_call_target="tpu_custom_call" | custom-call | flops 2147483648 | bytes 1048576 | tf_op jit(solution)/shard_map/pallas_call | solution.py:453
  329.2 2.7 copy.27
  (121 shorter events, 97.5 us)
Async XLA Ops:
  3.1 22.4 %all-to-all-start = ((s32[64,1,128]{2,1,0:T(1,128)}), s32[64,1,128]{2,1,0:T(1,128)S(1)}, u32[]{:S(2)}, u32[]{:S(2)}) async-start(s32[64,1,128]{2,1,0:T(1,128)} %bitcast.18), calls=%async_computation | async-start | bytes 65536 | tf_op jit(solution)/shard_map/all_to_all | solution.py:463
  29.4 57.1 %all-to-all-start.1 = ((bf16[64,128,128]{2,1,0:T(8,128)(2,1)}), bf16[64,128,128]{2,1,0:T(8,128)(2,1)}, u32[]{:S(2)}, u32[]{:S(2)}) async-start(bf16[64,128,128]{2,1,0:T(8,128)(2,1)} %shard_map.113), calls=%async_computation.1 | async-start | bytes 4194304 | tf_op jit(solution)/shard_map/all_to_all | solution.py:463
  96.6 62.6 %all-to-all-start.2 = ((bf16[64,128,128]{2,1,0:T(8,128)(2,1)}), bf16[64,128,128]{2,1,0:T(8,128)(2,1)}, u32[]{:S(2)}, u32[]{:S(2)}) async-start(bf16[64,128,128]{2,1,0:T(8,128)(2,1)} %get-tuple-element.42), calls=%async_computation.2 | async-start | bytes 4194304 | tf_op jit(solution)/shard_map/all_to_all | solution.py:463
  106.1 5.5 %collective-permute-start.1 = (bf16[400,128]{1,0:T(8,128)(2,1)S(1)}, bf16[400,128]{1,0:T(8,128)(2,1)S(1)}, u32[]{:S(2)}, u32[]{:S(2)}) collective-permute-start(bf16[400,128]{1,0:T(8,128)(2,1)S(1)} %get-tuple-element.46), channel_id=1, source_target_pairs={{0,1},{1,2},{2,3},{3,0},{4,5},{5,6},{6,7},{7,4},{8,9},{9,10},{10,1... | collective-permute-start | bytes 307208 | tf_op jit(solution)/shard_map/ppermute | solution.py:481
  107.4 7.4 %collective-permute-start.2 = (bf16[400,128]{1,0:T(8,128)(2,1)S(1)}, bf16[400,128]{1,0:T(8,128)(2,1)S(1)}, u32[]{:S(2)}, u32[]{:S(2)}) collective-permute-start(bf16[400,128]{1,0:T(8,128)(2,1)S(1)} %get-tuple-element.47), channel_id=1, source_target_pairs={{0,2},{1,3},{2,0},{3,1},{4,6},{5,7},{6,4},{7,5},{8,10},{9,11},{10,... | collective-permute-start | bytes 307208 | tf_op jit(solution)/shard_map/ppermute | solution.py:481
  115.4 5.4 %collective-permute-start.4 = (f32[112,128]{1,0:T(8,128)S(1)}, f32[112,128]{1,0:T(8,128)S(1)}, u32[]{:S(2)}, u32[]{:S(2)}) collective-permute-start(f32[112,128]{1,0:T(8,128)S(1)} %get-tuple-element.50), channel_id=1, source_target_pairs={{0,64},{4,68},{8,72},{12,76},{16,80},{20,84},{24,88},{28,92},{32,9... | collective-permute-start | bytes 172040 | tf_op jit(solution)/shard_map/ppermute | solution.py:482
  123.7 26.7 %collective-permute-start.7 = (bf16[112,128]{1,0:T(8,128)(2,1)S(1)}, bf16[112,128]{1,0:T(8,128)(2,1)S(1)}, u32[]{:S(2)}, u32[]{:S(2)}) collective-permute-start(bf16[112,128]{1,0:T(8,128)(2,1)S(1)} %shard_map.118.refs_0_), channel_id=1, source_target_pairs={{0,8},{4,12},{8,16},{12,20},{16,24},{20,28},{24,32},{28,36},{32,40... | collective-permute-start | bytes 86024 | tf_op jit(solution)/shard_map/ppermute | solution.py:482
  125.3 27.5 %collective-permute-start.8 = (bf16[112,128]{1,0:T(8,128)(2,1)S(1)}, bf16[112,128]{1,0:T(8,128)(2,1)S(1)}, u32[]{:S(2)}, u32[]{:S(2)}) collective-permute-start(bf16[112,128]{1,0:T(8,128)(2,1)S(1)} %shard_map.118.refs_0_), channel_id=1, source_target_pairs={{0,16},{4,20},{8,24},{12,28},{16,32},{20,36},{24,40},{28,44},{32,4... | collective-permute-start | bytes 86024 | tf_op jit(solution)/shard_map/ppermute | solution.py:482
  128.9 26.2 %collective-permute-start.9 = (bf16[112,128]{1,0:T(8,128)(2,1)S(1)}, bf16[112,128]{1,0:T(8,128)(2,1)S(1)}, u32[]{:S(2)}, u32[]{:S(2)}) collective-permute-start(bf16[112,128]{1,0:T(8,128)(2,1)S(1)} %shard_map.118.refs_0_), channel_id=1, source_target_pairs={{0,24},{4,28},{8,32},{12,36},{16,40},{20,44},{24,48},{28,52},{32,5... | collective-permute-start | bytes 86024 | tf_op jit(solution)/shard_map/ppermute | solution.py:482
  130.7 27.8 %collective-permute-start.10 = (bf16[112,128]{1,0:T(8,128)(2,1)S(1)}, bf16[112,128]{1,0:T(8,128)(2,1)S(1)}, u32[]{:S(2)}, u32[]{:S(2)}) collective-permute-start(bf16[112,128]{1,0:T(8,128)(2,1)S(1)} %shard_map.118.refs_0_), channel_id=1, source_target_pairs={{0,32},{4,36},{8,40},{12,44},{16,48},{20,52},{24,56},{28,60},{32,0... | collective-permute-start | bytes 86024 | tf_op jit(solution)/shard_map/ppermute | solution.py:482
  133.1 25.4 %collective-permute-start.11 = (bf16[112,128]{1,0:T(8,128)(2,1)S(1)}, bf16[112,128]{1,0:T(8,128)(2,1)S(1)}, u32[]{:S(2)}, u32[]{:S(2)}) collective-permute-start(bf16[112,128]{1,0:T(8,128)(2,1)S(1)} %shard_map.118.refs_0_), channel_id=1, source_target_pairs={{0,40},{4,44},{8,48},{12,52},{16,56},{20,60},{24,0},{28,4},{32,8},... | collective-permute-start | bytes 86024 | tf_op jit(solution)/shard_map/ppermute | solution.py:482
  150.4 8.1 %collective-permute-start.12 = (bf16[112,128]{1,0:T(8,128)(2,1)S(1)}, bf16[112,128]{1,0:T(8,128)(2,1)S(1)}, u32[]{:S(2)}, u32[]{:S(2)}) collective-permute-start(bf16[112,128]{1,0:T(8,128)(2,1)S(1)} %shard_map.118.refs_0_), channel_id=1, source_target_pairs={{0,48},{4,52},{8,56},{12,60},{16,0},{20,4},{24,8},{28,12},{32,16},... | collective-permute-start | bytes 86024 | tf_op jit(solution)/shard_map/ppermute | solution.py:482
  152.8 5.7 %collective-permute-start.13 = (bf16[112,128]{1,0:T(8,128)(2,1)S(1)}, bf16[112,128]{1,0:T(8,128)(2,1)S(1)}, u32[]{:S(2)}, u32[]{:S(2)}) collective-permute-start(bf16[112,128]{1,0:T(8,128)(2,1)S(1)} %shard_map.118.refs_0_), channel_id=1, source_target_pairs={{0,56},{4,60},{8,0},{12,4},{16,8},{20,12},{24,16},{28,20},{32,24},... | collective-permute-start | bytes 86024 | tf_op jit(solution)/shard_map/ppermute | solution.py:482
  168.5 59.0 %all-to-all-start.3 = ((bf16[64,128,128]{2,1,0:T(8,128)(2,1)}), bf16[64,128,128]{2,1,0:T(8,128)(2,1)}, u32[]{:S(2)}, u32[]{:S(2)}) async-start(bf16[64,128,128]{2,1,0:T(8,128)(2,1)} %get-tuple-element.53), calls=%async_computation.3 | async-start | bytes 4194304 | tf_op jit(solution)/shard_map/all_to_all | solution.py:463
  176.4 7.9 %collective-permute-start.14 = (f32[112,128]{1,0:T(8,128)S(1)}, f32[112,128]{1,0:T(8,128)S(1)}, u32[]{:S(2)}, u32[]{:S(2)}) collective-permute-start(f32[112,128]{1,0:T(8,128)S(1)} %shard_map.119.refs_5_.refs_0_), channel_id=1, source_target_pairs={{0,64},{4,68},{8,72},{12,76},{16,80},{20,84},{24,88},{28,92},{32,9... | collective-permute-start | bytes 172040 | tf_op jit(solution)/shard_map/ppermute | solution.py:482
  177.9 9.5 %collective-permute-start.15 = (f32[112,128]{1,0:T(8,128)S(1)}, f32[112,128]{1,0:T(8,128)S(1)}, u32[]{:S(2)}, u32[]{:S(2)}) collective-permute-start(f32[112,128]{1,0:T(8,128)S(1)} %shard_map.119.refs_5_.refs_0_), channel_id=1, source_target_pairs={{0,128},{4,132},{8,136},{12,140},{16,144},{20,148},{24,152},{28,15... | collective-permute-start | bytes 172040 | tf_op jit(solution)/shard_map/ppermute | solution.py:482
  180.5 6.9 %collective-permute-start.16 = (f32[112,128]{1,0:T(8,128)S(1)}, f32[112,128]{1,0:T(8,128)S(1)}, u32[]{:S(2)}, u32[]{:S(2)}) collective-permute-start(f32[112,128]{1,0:T(8,128)S(1)} %shard_map.119.refs_5_.refs_0_), channel_id=1, source_target_pairs={{0,192},{4,196},{8,200},{12,204},{16,208},{20,212},{24,216},{28,22... | collective-permute-start | bytes 172040 | tf_op jit(solution)/shard_map/ppermute | solution.py:482
  189.2 7.1 %collective-permute-start.18 = (bf16[400,128]{1,0:T(8,128)(2,1)S(1)}, bf16[400,128]{1,0:T(8,128)(2,1)S(1)}, u32[]{:S(2)}, u32[]{:S(2)}) collective-permute-start(bf16[400,128]{1,0:T(8,128)(2,1)S(1)} %shard_map.121.refs_0_), channel_id=1, source_target_pairs={{0,2},{1,3},{2,0},{3,1},{4,6},{5,7},{6,4},{7,5},{8,10},{9,11},{10,... | collective-permute-start | bytes 307208 | tf_op jit(solution)/shard_map/ppermute | solution.py:481
  236.7 45.5 %all-to-all-start.5 = ((bf16[64,80,128]{2,1,0:T(8,128)(2,1)}), bf16[64,80,128]{2,1,0:T(8,128)(2,1)S(1)}, u32[]{:S(2)}, u32[]{:S(2)}) async-start(bf16[64,80,128]{2,1,0:T(8,128)(2,1)} %get-tuple-element.66), calls=%async_computation.5 | async-start | bytes 2621440 | tf_op jit(solution)/shard_map/all_to_all | solution.py:463
  247.0 7.3 %collective-permute-start.23 = (bf16[400,128]{1,0:T(8,128)(2,1)S(1)}, bf16[400,128]{1,0:T(8,128)(2,1)S(1)}, u32[]{:S(2)}, u32[]{:S(2)}) collective-permute-start(bf16[400,128]{1,0:T(8,128)(2,1)S(1)} %get-tuple-element.60), channel_id=1, source_target_pairs={{0,2},{1,3},{2,0},{3,1},{4,6},{5,7},{6,4},{7,5},{8,10},{9,11},{10,... | collective-permute-start | bytes 307208 | tf_op jit(solution)/shard_map/ppermute | solution.py:481
  256.3 9.2 %collective-permute-start.26 = (f32[112,128]{1,0:T(8,128)S(1)}, f32[112,128]{1,0:T(8,128)S(1)}, u32[]{:S(2)}, u32[]{:S(2)}) collective-permute-start(f32[112,128]{1,0:T(8,128)S(1)} %get-tuple-element.64), channel_id=1, source_target_pairs={{0,128},{4,132},{8,136},{12,140},{16,144},{20,148},{24,152},{28,15... | collective-permute-start | bytes 172040 | tf_op jit(solution)/shard_map/ppermute | solution.py:482
  259.1 6.4 %collective-permute-start.27 = (f32[112,128]{1,0:T(8,128)S(1)}, f32[112,128]{1,0:T(8,128)S(1)}, u32[]{:S(2)}, u32[]{:S(2)}) collective-permute-start(f32[112,128]{1,0:T(8,128)S(1)} %get-tuple-element.65), channel_id=1, source_target_pairs={{0,192},{4,196},{8,200},{12,204},{16,208},{20,212},{24,216},{28,22... | collective-permute-start | bytes 172040 | tf_op jit(solution)/shard_map/ppermute | solution.py:482
  265.6 9.3 %collective-permute-start.28 = (bf16[112,128]{1,0:T(8,128)(2,1)S(1)}, bf16[112,128]{1,0:T(8,128)(2,1)S(1)}, u32[]{:S(2)}, u32[]{:S(2)}) collective-permute-start(bf16[112,128]{1,0:T(8,128)(2,1)S(1)} %shard_map.128.refs_0_), channel_id=1, source_target_pairs={{0,8},{4,12},{8,16},{12,20},{16,24},{20,28},{24,32},{28,36},{32,40... | collective-permute-start | bytes 86024 | tf_op jit(solution)/shard_map/ppermute | solution.py:482
  265.7 12.4 %collective-permute-start.29 = (bf16[112,128]{1,0:T(8,128)(2,1)S(1)}, bf16[112,128]{1,0:T(8,128)(2,1)S(1)}, u32[]{:S(2)}, u32[]{:S(2)}) collective-permute-start(bf16[112,128]{1,0:T(8,128)(2,1)S(1)} %shard_map.128.refs_0_), channel_id=1, source_target_pairs={{0,16},{4,20},{8,24},{12,28},{16,32},{20,36},{24,40},{28,44},{32,4... | collective-permute-start | bytes 86024 | tf_op jit(solution)/shard_map/ppermute | solution.py:482
  267.4 11.8 %collective-permute-start.30 = (bf16[112,128]{1,0:T(8,128)(2,1)S(1)}, bf16[112,128]{1,0:T(8,128)(2,1)S(1)}, u32[]{:S(2)}, u32[]{:S(2)}) collective-permute-start(bf16[112,128]{1,0:T(8,128)(2,1)S(1)} %shard_map.128.refs_0_), channel_id=1, source_target_pairs={{0,24},{4,28},{8,32},{12,36},{16,40},{20,44},{24,48},{28,52},{32,5... | collective-permute-start | bytes 86024 | tf_op jit(solution)/shard_map/ppermute | solution.py:482
  270.6 10.9 %collective-permute-start.31 = (bf16[112,128]{1,0:T(8,128)(2,1)S(1)}, bf16[112,128]{1,0:T(8,128)(2,1)S(1)}, u32[]{:S(2)}, u32[]{:S(2)}) collective-permute-start(bf16[112,128]{1,0:T(8,128)(2,1)S(1)} %shard_map.128.refs_0_), channel_id=1, source_target_pairs={{0,32},{4,36},{8,40},{12,44},{16,48},{20,52},{24,56},{28,60},{32,0... | collective-permute-start | bytes 86024 | tf_op jit(solution)/shard_map/ppermute | solution.py:482
  271.6 10.0 %collective-permute-start.32 = (bf16[112,128]{1,0:T(8,128)(2,1)S(1)}, bf16[112,128]{1,0:T(8,128)(2,1)S(1)}, u32[]{:S(2)}, u32[]{:S(2)}) collective-permute-start(bf16[112,128]{1,0:T(8,128)(2,1)S(1)} %shard_map.128.refs_0_), channel_id=1, source_target_pairs={{0,40},{4,44},{8,48},{12,52},{16,56},{20,60},{24,0},{28,4},{32,8},... | collective-permute-start | bytes 86024 | tf_op jit(solution)/shard_map/ppermute | solution.py:482
  274.9 6.7 %collective-permute-start.33 = (bf16[112,128]{1,0:T(8,128)(2,1)S(1)}, bf16[112,128]{1,0:T(8,128)(2,1)S(1)}, u32[]{:S(2)}, u32[]{:S(2)}) collective-permute-start(bf16[112,128]{1,0:T(8,128)(2,1)S(1)} %shard_map.128.refs_0_), channel_id=1, source_target_pairs={{0,48},{4,52},{8,56},{12,60},{16,0},{20,4},{24,8},{28,12},{32,16},... | collective-permute-start | bytes 86024 | tf_op jit(solution)/shard_map/ppermute | solution.py:482
  282.3 41.1 %all-to-all-start.4 = ((bf16[64,48,128]{2,1,0:T(8,128)(2,1)}), bf16[64,48,128]{2,1,0:T(8,128)(2,1)}, u32[]{:S(2)}, u32[]{:S(2)}) async-start(bf16[64,48,128]{2,1,0:T(8,128)(2,1)} %shard_map.130), calls=%async_computation.4 | async-start | bytes 1572864 | tf_op jit(solution)/shard_map/all_to_all | solution.py:463
  294.1 5.8 %collective-permute-start.35 = (f32[112,128]{1,0:T(8,128)S(1)}, f32[112,128]{1,0:T(8,128)S(1)}, u32[]{:S(2)}, u32[]{:S(2)}) collective-permute-start(f32[112,128]{1,0:T(8,128)S(1)} %shard_map.129.after_ref.refs_0_), channel_id=1, source_target_pairs={{0,64},{4,68},{8,72},{12,76},{16,80},{20,84},{24,88},{28,92},{32,9... | collective-permute-start | bytes 172040 | tf_op jit(solution)/shard_map/ppermute | solution.py:482
  295.6 5.6 %collective-permute-start.36 = (f32[112,128]{1,0:T(8,128)S(1)}, f32[112,128]{1,0:T(8,128)S(1)}, u32[]{:S(2)}, u32[]{:S(2)}) collective-permute-start(f32[112,128]{1,0:T(8,128)S(1)} %shard_map.129.after_ref.refs_0_), channel_id=1, source_target_pairs={{0,128},{4,132},{8,136},{12,140},{16,144},{20,148},{24,152},{28,15... | collective-permute-start | bytes 172040 | tf_op jit(solution)/shard_map/ppermute | solution.py:482
  303.4 6.1 %collective-permute-start.39 = (bf16[400,128]{1,0:T(8,128)(2,1)S(1)}, bf16[400,128]{1,0:T(8,128)(2,1)S(1)}, u32[]{:S(2)}, u32[]{:S(2)}) collective-permute-start(bf16[400,128]{1,0:T(8,128)(2,1)S(1)} %shard_map.133.refs_0_), channel_id=1, source_target_pairs={{0,2},{1,3},{2,0},{3,1},{4,6},{5,7},{6,4},{7,5},{8,10},{9,11},{10,... | collective-permute-start | bytes 307208 | tf_op jit(solution)/shard_map/ppermute | solution.py:481
  (24 other events, 239.6 us)

commit v6 on v5

--- a/solution.py
+++ b/solution.py
@@ -188,20 +188,21 @@
     gather_rows(named_ref, 0, wide_ref, wire_ref, held_ref, sems)
 
 
-def apply_rows(b, total, accum_ref, new_accum_ref, rows_ref):
-    rows = slice(128 * b, 128 * b + 128)
-    accum = lane_to_column(accum_ref[b : b + 1, :])
-    accum = accum + jnp.sum(total * total, axis=1, keepdims=True) / WIDTH
-    new_accum_ref[b : b + 1, :] = jnp.transpose(accum)[:1]
-    new = rows_ref[rows, :] - total * (RATE * lax.rsqrt(accum[:, :1]))
-    rows_ref[rows, :] = new
-    return new
+def to_columns(state_ref):
+    return jnp.transpose(jnp.concatenate([state_ref[...], jnp.zeros((120, 128), F32)], axis=0))
+
+
+def adagrad(b, total, old, states):
+    state = states[:, b : b + 1] + jnp.sum(total * total, axis=1, keepdims=True) / WIDTH
+    new = old - total * (RATE * lax.rsqrt(state))
+    return new, jnp.where(iota((128, 128), 1) == b, state, states)
 
 
 def update(
-    step, wire_in_ref, flat_ref, table_ref, accum_ref, named_ref, _, new_table_ref, new_accum_ref, wire_ref,
-    in_sems, table_sem, out_sems, held_ref, rows_ref, grads_ref, wide_ref, sent_ref, sent_sems,
+    step, wire_in_ref, flat_ref, table_ref, accum_ref, named_ref, *rest
 ):
+    new_table_ref, new_accum_ref, wire_ref, in_sems, table_sem, out_sems, *rest = rest[7:]
+    held_ref, rows_ref, grads_ref, wide_ref, sent_ref, sent_sems = rest
     copies = wire_copies(wire_in_ref, held_ref, in_sems)
     for copy in copies:
         copy.start()
@@ -210,14 +211,17 @@
     unpack_all(copies, held_ref, grads_ref)
     table_copy.wait()
     outs = []
+    states = to_columns(accum_ref)
     for b in range(8):
         here = pl.ds(128 * b, 128)
         hit = one_hot(iota((128, SLOTS), 0) + 128 * b == flat_ref[step : step + 1, :])
         total = to_narrow(dot(hit, grads_ref[...]))
-        new = apply_rows(b, total, accum_ref, new_accum_ref, rows_ref)
+        new, states = adagrad(b, total, rows_ref[here, :], states)
+        rows_ref[here, :] = new
         outs.append(pltpu.make_async_copy(rows_ref.at[here], new_table_ref.at[0, here], out_sems.at[b]))
         outs[-1].start()
         wide_ref[here, :] = to_wide(new).astype(BF16)
+    new_accum_ref[...] = jnp.transpose(states)[:8]
     gather_rows(named_ref, step + 1, wide_ref, wire_ref, sent_ref, sent_sems)
     for copy in outs:
         copy.wait()
@@ -235,7 +239,7 @@
 
 def last_update(
     step, wire_in_ref, flat_ref, sums_ref, table_ref, accum_ref, new_table_ref, new_accum_ref,
-    in_sems, table_sem, out_sems, held_ref, rows_ref, grads_ref,
+    in_sems, table_sem, out_sems, held_ref, rows_ref, grads_ref, turned_ref,
 ):
     copies = wire_copies(wire_in_ref, held_ref, in_sems)
     for copy in copies:
@@ -245,13 +249,16 @@
     unpack_all(copies, held_ref, grads_ref, unpack_second)
     table_copy.wait()
     outs = []
+    states = to_columns(accum_ref)
     for b in range(8):
         here = pl.ds(128 * b, 128)
         hit = one_hot(iota((128, SLOTS), 0) + 128 * b == flat_ref[step : step + 1, :])
         total = to_narrow(jnp.concatenate([sums_ref[here, :], dot(hit, grads_ref[...])], axis=1))
-        apply_rows(b, total, accum_ref, new_accum_ref, rows_ref)
-        outs.append(pltpu.make_async_copy(rows_ref.at[here], new_table_ref.at[0, here], out_sems.at[b]))
+        new, states = adagrad(b, total, rows_ref[here, :], states)
+        turned_ref[b] = jnp.transpose(new)
+        outs.append(pltpu.make_async_copy(turned_ref.at[b], new_table_ref.at[0, :, here], out_sems.at[b]))
         outs[-1].start()
+    new_accum_ref[...] = jnp.transpose(states)[:8]
     for copy in outs:
         copy.wait()
 
@@ -285,7 +292,8 @@
 def block(
     step, at_ref, wire_in_ref, slots_ref, negative_ref, relation_ref, rel_ids_ref, *rest
 ):
-    *wire_refs, keep_ref, give_ref, rows_ref, weights_ref, held_ref, in_sems, sent_ref, out_sems = rest
+    *rest, sent_ref, out_sems, kept_ref, keep_sems = rest
+    *wire_refs, keep_ref, give_ref, rows_ref, weights_ref, held_ref, in_sems = rest
     edges, parts = 128, 4
     part = SLOTS // parts
     per = OWN // parts
@@ -299,8 +307,10 @@
     ).astype(I32)
     fetched = jnp.zeros((2 * edges, 512), F32)
     for g in range(parts):
+        here = slice(part * g, part * g + part)
         hit = one_hot(slots_column == iota((2 * edges, part), 1) + part * g)
-        fetched = fetched + dot(hit, rows_ref[part * g : part * g + part, :])
+        weights_ref[2 * edges :, here] = hit
+        fetched = fetched + dot(hit, rows_ref[here, :])
     fetched = to_narrow(fetched)
     head, tail = fetched[:edges], fetched[edges:]
     head_re, head_im = complex_parts(head)
@@ -316,7 +326,7 @@
         scores = dot(queries, rows_ref[here, :], ((1,), (1,)))
         weights = jax.nn.sigmoid(scores) * (negative_ref[step : step + 1, here] / 1024)
         weights = weights.astype(BF16)
-        weights_ref[:, here] = weights
+        weights_ref[: 2 * edges, here] = weights
         pull = pull + dot(weights, rows_ref[here, :])
     pull = to_narrow(pull)
     positive_weight = -jax.nn.sigmoid(-positive)
@@ -327,12 +337,11 @@
         push_re * rel_re - push_im * rel_im, push_re * rel_im + push_im * rel_re
     )
     edge_grads = to_wide(jnp.concatenate([grad_head, grad_tail], axis=0)).astype(BF16)
+    edge_grads = jnp.concatenate([queries, edge_grads], axis=0)
     outs = []
     for g in range(parts):
         here = slice(part * g, part * g + part)
-        grads = dot(weights_ref[:, here], queries, ((0,), (0,)))
-        hit = one_hot(iota((part, 2 * edges), 0) + part * g == slots)
-        grads = grads + dot(hit, edge_grads)
+        grads = dot(weights_ref[:, here], edge_grads, ((0,), (0,)))
         for j in range(per):
             sent_ref[per * g + j] = pack(grads[CAP * j : CAP * j + CAP]).astype(BF16)
         blocks = pl.ds(per * g, per)
@@ -360,8 +369,14 @@
             hit = one_hot(iota((64, edges), 0) + 64 * (half * k + i) == rel_ids)
             dense.append(pack_relations(dot(hit, high) + dot(hit, low)))
         here = slice(200 * i, 200 * i + 200)
-        keep_ref[here, :] = jnp.where(at_ref[3] == 0, dense[0], dense[1])
-        give_ref[here, :] = jnp.where(at_ref[3] == 0, dense[1], dense[0])
+        kept_ref[0, here, :] = jnp.where(at_ref[3] == 0, dense[0], dense[1])
+        kept_ref[1, here, :] = jnp.where(at_ref[3] == 0, dense[1], dense[0])
+        dense = pl.ds(200 * i, 200)
+        for k, out_ref in enumerate((give_ref, keep_ref)):
+            outs.append(
+                pltpu.make_async_copy(kept_ref.at[1 - k, dense], out_ref.at[dense], keep_sems.at[k, i])
+            )
+            outs[-1].start()
     for copy in outs:
         copy.wait()
 
@@ -419,16 +434,15 @@
 
 def relation_update(at_ref, mine_ref, other_ref, table_ref, state_ref, new_table_ref, new_state_ref):
     count = REL // 128
+    states = to_columns(state_ref)
     for b in range(count):
         rows = slice(128 * b, 128 * b + 128)
         here = slice(400 * (b % (count // 2)), 400 * (b % (count // 2)) + 400)
-        mine, other = mine_ref[here, :].astype(F32), other_ref[here, :].astype(F32)
-        dense = jnp.where(at_ref[3] == b // (count // 2), mine, other)
+        mine, other = mine_ref[here, :], other_ref[here, :]
+        dense = jnp.where(at_ref[3] == b // (count // 2), mine, other).astype(F32)
         total = jnp.concatenate([unpack_relations(dense[:200]), unpack_relations(dense[200:])], axis=0)
-        state = lane_to_column(state_ref[b : b + 1, :])
-        state = state + jnp.sum(total * total, axis=1, keepdims=True) / WIDTH
-        new_state_ref[b : b + 1, :] = jnp.transpose(state)[:1]
-        new_table_ref[rows, :] = table_ref[rows, :] - total * (RATE * lax.rsqrt(state[:, :1]))
+        new_table_ref[rows, :], states = adagrad(b, total, table_ref[rows, :], states)
+    new_state_ref[...] = jnp.transpose(states)[:8]
 
 
 SPACES = {
@@ -447,7 +461,7 @@
         out_specs=[SPACES[k] for k in places],
         scratch_shapes=scratch,
         input_output_aliases=aliases or {},
-        compiler_params=pltpu.CompilerParams(vmem_limit_bytes=40 << 20),
+        compiler_params=pltpu.CompilerParams(vmem_limit_bytes=30 << 20),
         cost_estimate=pl.CostEstimate(flops=flops, bytes_accessed=1 << 20, transcendentals=0),
     )
     return lambda *args: call(
@@ -496,9 +510,11 @@
         )(at, own, *arrived)
         arrived = [move(part, axis, d + 1) for d, part in enumerate(parts)]
     own = kernel(sum_y, "vvvv", [shape(own.shape, BF16)], "v")(own, *arrived)[0]
-    return kernel(sum_z, "s" + "v" * 8, [shape(own.shape, F32)], "v", [pltpu.VMEM((8, *own.shape), F32)])(
-        at, own, *[move(own, 2, d) for d in range(1, 8)]
+    arrived = [move(own, 2, d) for d in range(1, 8)]
+    own = kernel(sum_z, "s" + "v" * 8, [shape(own.shape, F32)], "v", [pltpu.VMEM((8, *own.shape), F32)])(
+        at, own, *arrived
     )[0]
+    return own, arrived
 
 
 def relation_gather_y(at, own):
@@ -549,15 +565,16 @@
             lambda *refs, s=s: block(s, *refs),
             "shvvvv",
             wires + [dense, dense],
-            "h" * len(wires) + "vv",
+            "h" * len(wires) + "hh",
             [
-                pltpu.VMEM((SLOTS, 512), BF16), pltpu.VMEM((256, SLOTS), BF16), held, copies(WIRE_PARTS), held,
-                pltpu.SemaphoreType.DMA((2, 4)),
+                pltpu.VMEM((SLOTS, 512), BF16), pltpu.VMEM((512, SLOTS), BF16), held, copies(WIRE_PARTS), held,
+                pltpu.SemaphoreType.DMA((2, 4)), pltpu.VMEM((2, DENSE // 2, 128), F32),
+                pltpu.SemaphoreType.DMA((2, REL // 128)),
             ],
             4 << 30,
         )(at, rows, slots, negative, relation, rel_ids)
         grads[0] = exchange(grads[0])
-        own = relation_scatter(at, keep, give)
+        own, arrived = relation_scatter(at, keep, give)
         scratch = [copies(WIRE_PARTS), pltpu.SemaphoreType.DMA, copies(8)]
         outs = [shape(table.shape, F32), shape((8, 128), F32)]
         if last:
@@ -575,21 +592,22 @@
             table, accum = kernel(
                 lambda *refs, s=s: last_update(s, *refs),
                 "hvvhv",
-                outs,
+                [shape((1, WIDTH, 1024), F32), outs[1]],
                 "hv",
-                scratch + [pltpu.VMEM((SLOTS, 256), BF16)],
+                scratch + [pltpu.VMEM((SLOTS, 256), BF16), pltpu.VMEM((8, WIDTH, 128), F32)],
                 2 << 30,
             )(second, flat, sums, table, accum)
+            table = jnp.swapaxes(table, 1, 2)
         else:
             scratch += [held, pltpu.VMEM((1024, WIDTH), F32), pltpu.VMEM((SLOTS, 512), BF16)]
             table, accum, rows = kernel(
                 lambda *refs, s=s: update(s, *refs),
-                "hvhvva",
+                "hvhvv" + "a" * len(arrived),
                 outs + [wire],
                 "hvh",
                 scratch + [pltpu.VMEM((1024, 512), BF16), held, copies(8)],
                 5 << 30,
-            )(grads[0], flat, table, accum, named, own)
+            )(grads[0], flat, table, accum, named, *arrived)
         own = relation_gather_y(at, own)
         mine, other = relation_gather_x(at, own)
         rel_table, rel_state = kernel(

time: 338 us -> 336 us (level)
  local copies, waits for them, and re-layouts: 13.9 us -> 10.3 us
    unnamed x20 -> x23, local copies, waits for them, and re-layouts: 11.5 us -> 7.87 us
where the time goes in v6:
time: 336 us; the launch traced here: 330 us
  waiting for transfers between devices  133 us (40%)
  starting transfers between devices  125 us (37%)
  Pallas kernels  60.2 us (18%)
  local copies, waits for them, and re-layouts  10.3 us (3%)
    all_to_all x6, waiting for transfers between devices, exchange(): return lax.all_to_all(x, 'edge', split_axis=0, concat_axis=0, tiled=True)  74.1 us
    pallas_call x25, Pallas kernels, kernel(): call(*[pltpu.with_memory_space_constraint(x, pltpu.HBM) if k == 'h' else...  60.2 us
    all_to_all x6, starting transfers between devices, exchange(): return lax.all_to_all(x, 'edge', split_axis=0, concat_axis=0, tiled=True)  51 us
    ppermute x26, starting transfers between devices, move(): lax.ppermute(x, 'edge', edge_pairs(d if axis == 1 else 0, d if axis == 2...  49.9 us
    ppermute x26, waiting for transfers between devices, move(): lax.ppermute(x, 'edge', edge_pairs(d if axis == 1 else 0, d if axis == 2...  38 us
    ppermute x12, starting transfers between devices, move(): return lax.ppermute(x, 'rep', [(k, (k + d) % 4) for k in range(4)])  18.7 us
    ppermute x12, waiting for transfers between devices, move(): return lax.ppermute(x, 'rep', [(k, (k + d) % 4) for k in range(4)])  14 us
    unnamed x23, local copies, waits for them, and re-layouts  7.87 us
  transfers between devices with their start and end apart: 48, of which 29 were waited for; matrix products, arithmetic and copies ran while one was open for 3% of the time, Pallas kernels for 6%

profile of v6, /device:TPU:1, one launch (start us, length us, event | category | flops | bytes accessed | tf_op | source)
XLA Modules:
  0.0 330.0 jit_solution(6721242215104615602)
XLA Ops:
  3.1 13.2 %all-to-all-start = ((s32[64,1,128]{2,1,0:T(1,128)}), s32[64,1,128]{2,1,0:T(1,128)S(1)}, u32[]{:S(2)}, u32[]{:S(2)}) async-start(s32[64,1,128]{2,1,0:T(1,128)} %bitcast.19), calls=%async_computation | async-start | bytes 65536 | tf_op jit(solution)/shard_map/all_to_all | solution.py:477
  18.6 6.8 %all-to-all-done = s32[64,1,128]{2,1,0:T(1,128)S(1)} async-done(((s32[64,1,128]{2,1,0:T(1,128)}), s32[64,1,128]{2,1,0:T(1,128)S(1)}, u32[]{:S(2)}, u32[]{:S(2)}) %all-to-all-start) | async-done | bytes 32800 | tf_op jit(solution)/shard_map/all_to_all | solution.py:477
  25.5 3.9 %shard_map.113 = bf16[64,128,128]{2,1,0:T(8,128)(2,1)} custom-call(bf16[1024,512]{1,0:T(8,128)(2,1)S(1)} %shard_map.111.wide_ref, s32[64,128]{1,0:T(8,128)S(1)} %bitcast.15), custom_call_target="tpu_custom_call" | custom-call | flops 3221225472 | bytes 1048576 | tf_op jit(solution)/shard_map/pallas_call | solution.py:467
  29.4 6.0 %all-to-all-start.1 = ((bf16[64,128,128]{2,1,0:T(8,128)(2,1)}), bf16[64,128,128]{2,1,0:T(8,128)(2,1)}, u32[]{:S(2)}, u32[]{:S(2)}) async-start(bf16[64,128,128]{2,1,0:T(8,128)(2,1)} %shard_map.113), calls=%async_computation.1 | async-start | bytes 4194304 | tf_op jit(solution)/shard_map/all_to_all | solution.py:477
  35.7 2.9 copy.23
  41.3 45.2 %all-to-all-done.1.refs_1_ = bf16[64,128,128]{2,1,0:T(8,128)(2,1)} async-done(((bf16[64,128,128]{2,1,0:T(8,128)(2,1)}), bf16[64,128,128]{2,1,0:T(8,128)(2,1)}, u32[]{:S(2)}, u32[]{:S(2)}) %all-to-all-start.1) | async-done | bytes 2097184 | tf_op jit(solution)/shard_map/all_to_all | solution.py:477
  86.5 9.6 %shard_map.115 = (bf16[64,128,128]{2,1,0:T(8,128)(2,1)}, f32[1600,128]{1,0:T(8,128)}, f32[1600,128]{1,0:T(8,128)}) custom-call(s32[4]{0:T(128)S(1)} %pad_add_fusion.1.refs_0_.at_ref, bf16[64,128,128]{2,1,0:T(8,128)(2,1)} %all-to-all-done.1.refs_1_, s32[2,256]{1,0:T(2,128)S(1)} %get-tuple-element.40.refs_2_, f32[2,2560]{1,0:T(2,128)S(1)} %pad_maximum_fusion.refs_3_, ...), custom_call_target="tpu_custom_call" | custom-call | flops 4294967296 | bytes 1048576 | tf_op jit(solution)/shard_map/pallas_call | solution.py:467
  96.2 6.2 %all-to-all-start.2 = ((bf16[64,128,128]{2,1,0:T(8,128)(2,1)}), bf16[64,128,128]{2,1,0:T(8,128)(2,1)}, u32[]{:S(2)}, u32[]{:S(2)}) async-start(bf16[64,128,128]{2,1,0:T(8,128)(2,1)} %get-tuple-element.42), calls=%async_computation.2 | async-start | bytes 4194304 | tf_op jit(solution)/shard_map/all_to_all | solution.py:477
  111.3 3.2 collective-permute-done.2.refs_3_
  125.1 3.3 collective-permute-start.8
  135.0 15.0 %collective-permute-done.7.refs_5_.refs_1_ = bf16[112,128]{1,0:T(8,128)(2,1)S(1)} collective-permute-done((bf16[112,128]{1,0:T(8,128)(2,1)S(1)}, bf16[112,128]{1,0:T(8,128)(2,1)S(1)}, u32[]{:S(2)}, u32[]{:S(2)}) %collective-permute-start.7) | collective-permute-done | bytes 28704 | tf_op jit(solution)/shard_map/ppermute | solution.py:496
  154.8 3.5 %collective-permute-done.10.refs_8_.refs_4_ = bf16[112,128]{1,0:T(8,128)(2,1)S(1)} collective-permute-done((bf16[112,128]{1,0:T(8,128)(2,1)S(1)}, bf16[112,128]{1,0:T(8,128)(2,1)S(1)}, u32[]{:S(2)}, u32[]{:S(2)}) %collective-permute-start.10) | collective-permute-done | bytes 28704 | tf_op jit(solution)/shard_map/ppermute | solution.py:496
  158.3 9.6 %shard_map.119 = (f32[1,1024,400]{2,1,0:T(8,128)}, f32[8,128]{1,0:T(8,128)S(1)}, bf16[64,128,128]{2,1,0:T(8,128)(2,1)}) custom-call(bf16[64,128,128]{2,1,0:T(8,128)(2,1)} %all-to-all-done.2.refs_0_, s32[2,2560]{1,0:T(2,128)S(1)} %pad_add_fusion.refs_1_, f32[1,1024,400]{2,1,0:T(8,128)} %copy-done, f32[8,128]{1,0:T(8,128)S(1)} %bitcast.18, ...), custom_call_target="tpu_custom_call" | custom-call | flops 5368709120 | bytes 1048576 | tf_op jit(solution)/shard_map/pallas_call | solution.py:467
  167.9 7.9 %all-to-all-start.3 = ((bf16[64,128,128]{2,1,0:T(8,128)(2,1)}), bf16[64,128,128]{2,1,0:T(8,128)(2,1)}, u32[]{:S(2)}, u32[]{:S(2)}) async-start(bf16[64,128,128]{2,1,0:T(8,128)(2,1)} %get-tuple-element.53), calls=%async_computation.3 | async-start | bytes 4194304 | tf_op jit(solution)/shard_map/all_to_all | solution.py:477
  177.8 2.6 collective-permute-start.15
  183.6 3.1 collective-permute-done.15.refs_2_
  192.5 3.2 collective-permute-done.18.refs_2_
  199.1 3.5 %shard_map.123 = (f32[1024,400]{1,0:T(8,128)S(1)}, f32[8,128]{1,0:T(8,128)S(1)}) custom-call(s32[4]{0:T(128)S(1)} %pad_add_fusion.1.refs_0_.at_ref, bf16[1600,128]{1,0:T(8,128)(2,1)S(1)} %shard_map.122.mine_ref, bf16[1600,128]{1,0:T(8,128)(2,1)S(1)} %collective-permute-done.20.other_ref, f32[1024,400]{1,0:T(8,128)S(1)} %pad.8.refs_0_.table_ref, ...), custom_call_target="tpu_custom_call" | custom-call | bytes 1048576 | tf_op jit(solution)/shard_map/pallas_call | solution.py:467
  204.8 22.1 %all-to-all-done.3.refs_1_ = bf16[64,128,128]{2,1,0:T(8,128)(2,1)} async-done(((bf16[64,128,128]{2,1,0:T(8,128)(2,1)}), bf16[64,128,128]{2,1,0:T(8,128)(2,1)}, u32[]{:S(2)}, u32[]{:S(2)}) %all-to-all-start.3) | async-done | bytes 2097184 | tf_op jit(solution)/shard_map/all_to_all | solution.py:477
  226.9 9.7 %shard_map.125 = (bf16[64,80,128]{2,1,0:T(8,128)(2,1)}, bf16[64,48,128]{2,1,0:T(8,128)(2,1)}, f32[1600,128]{1,0:T(8,128)}, f32[1600,128]{1,0:T(8,128)}) custom-call(s32[4]{0:T(128)S(1)} %pad_add_fusion.1.refs_0_.at_ref, bf16[64,128,128]{2,1,0:T(8,128)(2,1)} %all-to-all-done.3.refs_1_, s32[2,256]{1,0:T(2,128)S(1)} %get-tuple-element.40.refs_2_, ...), custom_call_target="tpu_custom_call" | custom-call | flops 4294967296 | bytes 1048576 | tf_op jit(solution)/shard_map/pallas_call | solution.py:467
  236.6 6.0 %all-to-all-start.5 = ((bf16[64,80,128]{2,1,0:T(8,128)(2,1)}), bf16[64,80,128]{2,1,0:T(8,128)(2,1)S(1)}, u32[]{:S(2)}, u32[]{:S(2)}) async-start(bf16[64,80,128]{2,1,0:T(8,128)(2,1)} %get-tuple-element.66), calls=%async_computation.5 | async-start | bytes 2621440 | tf_op jit(solution)/shard_map/all_to_all | solution.py:477
  251.2 3.2 collective-permute-done.23.refs_3_
  256.4 2.8 collective-permute-start.26
  260.2 5.4 %collective-permute-done.26.refs_1_ = f32[112,128]{1,0:T(8,128)S(1)} collective-permute-done((f32[112,128]{1,0:T(8,128)S(1)}, f32[112,128]{1,0:T(8,128)S(1)}, u32[]{:S(2)}, u32[]{:S(2)}) %collective-permute-start.26) | collective-permute-done | bytes 57376 | tf_op jit(solution)/shard_map/ppermute | solution.py:496
  267.5 3.2 collective-permute-start.30
  271.6 3.3 %collective-permute-start.32 = (bf16[112,128]{1,0:T(8,128)(2,1)S(1)}, bf16[112,128]{1,0:T(8,128)(2,1)S(1)}, u32[]{:S(2)}, u32[]{:S(2)}) collective-permute-start(bf16[112,128]{1,0:T(8,128)(2,1)S(1)} %shard_map.128.refs_0_), channel_id=1, source_target_pairs={{0,40},{4,44},{8,48},{12,52},{16,56},{20,60},{24,0},{28,4},{32,8},... | collective-permute-start | bytes 86024 | tf_op jit(solution)/shard_map/ppermute | solution.py:496
  274.9 3.2 collective-permute-start.33
  282.3 11.8 %all-to-all-start.4 = ((bf16[64,48,128]{2,1,0:T(8,128)(2,1)}), bf16[64,48,128]{2,1,0:T(8,128)(2,1)}, u32[]{:S(2)}, u32[]{:S(2)}) async-start(bf16[64,48,128]{2,1,0:T(8,128)(2,1)} %shard_map.130), calls=%async_computation.4 | async-start | bytes 1572864 | tf_op jit(solution)/shard_map/all_to_all | solution.py:477
  310.5 2.6 collective-permute-start.41
  314.5 4.1 %shard_map.135 = (f32[1024,400]{1,0:T(8,128)S(1)}, f32[8,128]{1,0:T(8,128)}) custom-call(s32[4]{0:T(128)S(1)} %pad_add_fusion.1.refs_0_.at_ref, bf16[1600,128]{1,0:T(8,128)(2,1)S(1)} %shard_map.134.mine_ref, bf16[1600,128]{1,0:T(8,128)(2,1)S(1)} %collective-permute-done.41.other_ref, f32[1024,400]{1,0:T(8,128)S(1)} %copy-done.2, ...), custom_call_target="tpu_custom_call" | custom-call | bytes 1048576 | tf_op jit(solution)/shard_map/pallas_call | solution.py:467
  320.5 2.9 shard_map.131.refs_2_
  323.4 6.1 %shard_map.132 = (f32[1,400,1024]{2,1,0:T(8,128)}, f32[8,128]{1,0:T(8,128)}) custom-call(bf16[64,48,128]{2,1,0:T(8,128)(2,1)} %all-to-all-done.4.refs_0_, s32[2,2560]{1,0:T(2,128)S(1)} %pad_add_fusion.refs_1_, f32[1024,256]{1,0:T(8,128)S(1)} %shard_map.131.refs_2_, f32[1,1024,400]{2,1,0:T(8,128)} %get-tuple-element.67.refs_3_, ...), custom_call_target="tpu_custom_call" | custom-call | flops 2147483648 | bytes 1048576 | tf_op jit(solution)/shard_map/pallas_call | solution.py:467
  (124 shorter events, 93.6 us)
Async XLA Ops:
  3.1 22.4 %all-to-all-start = ((s32[64,1,128]{2,1,0:T(1,128)}), s32[64,1,128]{2,1,0:T(1,128)S(1)}, u32[]{:S(2)}, u32[]{:S(2)}) async-start(s32[64,1,128]{2,1,0:T(1,128)} %bitcast.19), calls=%async_computation | async-start | bytes 65536 | tf_op jit(solution)/shard_map/all_to_all | solution.py:477
  29.4 57.1 %all-to-all-start.1 = ((bf16[64,128,128]{2,1,0:T(8,128)(2,1)}), bf16[64,128,128]{2,1,0:T(8,128)(2,1)}, u32[]{:S(2)}, u32[]{:S(2)}) async-start(bf16[64,128,128]{2,1,0:T(8,128)(2,1)} %shard_map.113), calls=%async_computation.1 | async-start | bytes 4194304 | tf_op jit(solution)/shard_map/all_to_all | solution.py:477
  96.2 62.1 %all-to-all-start.2 = ((bf16[64,128,128]{2,1,0:T(8,128)(2,1)}), bf16[64,128,128]{2,1,0:T(8,128)(2,1)}, u32[]{:S(2)}, u32[]{:S(2)}) async-start(bf16[64,128,128]{2,1,0:T(8,128)(2,1)} %get-tuple-element.42), calls=%async_computation.2 | async-start | bytes 4194304 | tf_op jit(solution)/shard_map/all_to_all | solution.py:477
  105.8 5.5 %collective-permute-start.1 = (bf16[400,128]{1,0:T(8,128)(2,1)S(1)}, bf16[400,128]{1,0:T(8,128)(2,1)S(1)}, u32[]{:S(2)}, u32[]{:S(2)}) collective-permute-start(bf16[400,128]{1,0:T(8,128)(2,1)S(1)} %get-tuple-element.46), channel_id=1, source_target_pairs={{0,1},{1,2},{2,3},{3,0},{4,5},{5,6},{6,7},{7,4},{8,9},{9,10},{10,1... | collective-permute-start | bytes 307208 | tf_op jit(solution)/shard_map/ppermute | solution.py:495
  107.1 7.4 %collective-permute-start.2 = (bf16[400,128]{1,0:T(8,128)(2,1)S(1)}, bf16[400,128]{1,0:T(8,128)(2,1)S(1)}, u32[]{:S(2)}, u32[]{:S(2)}) collective-permute-start(bf16[400,128]{1,0:T(8,128)(2,1)S(1)} %get-tuple-element.47), channel_id=1, source_target_pairs={{0,2},{1,3},{2,0},{3,1},{4,6},{5,7},{6,4},{7,5},{8,10},{9,11},{10,... | collective-permute-start | bytes 307208 | tf_op jit(solution)/shard_map/ppermute | solution.py:495
  115.1 5.4 %collective-permute-start.4 = (f32[112,128]{1,0:T(8,128)S(1)}, f32[112,128]{1,0:T(8,128)S(1)}, u32[]{:S(2)}, u32[]{:S(2)}) collective-permute-start(f32[112,128]{1,0:T(8,128)S(1)} %get-tuple-element.50), channel_id=1, source_target_pairs={{0,64},{4,68},{8,72},{12,76},{16,80},{20,84},{24,88},{28,92},{32,9... | collective-permute-start | bytes 172040 | tf_op jit(solution)/shard_map/ppermute | solution.py:496
  123.4 26.7 %collective-permute-start.7 = (bf16[112,128]{1,0:T(8,128)(2,1)S(1)}, bf16[112,128]{1,0:T(8,128)(2,1)S(1)}, u32[]{:S(2)}, u32[]{:S(2)}) collective-permute-start(bf16[112,128]{1,0:T(8,128)(2,1)S(1)} %shard_map.118.refs_0_), channel_id=1, source_target_pairs={{0,8},{4,12},{8,16},{12,20},{16,24},{20,28},{24,32},{28,36},{32,40... | collective-permute-start | bytes 86024 | tf_op jit(solution)/shard_map/ppermute | solution.py:496
  125.1 27.5 %collective-permute-start.8 = (bf16[112,128]{1,0:T(8,128)(2,1)S(1)}, bf16[112,128]{1,0:T(8,128)(2,1)S(1)}, u32[]{:S(2)}, u32[]{:S(2)}) collective-permute-start(bf16[112,128]{1,0:T(8,128)(2,1)S(1)} %shard_map.118.refs_0_), channel_id=1, source_target_pairs={{0,16},{4,20},{8,24},{12,28},{16,32},{20,36},{24,40},{28,44},{32,4... | collective-permute-start | bytes 86024 | tf_op jit(solution)/shard_map/ppermute | solution.py:496
  128.6 26.2 %collective-permute-start.9 = (bf16[112,128]{1,0:T(8,128)(2,1)S(1)}, bf16[112,128]{1,0:T(8,128)(2,1)S(1)}, u32[]{:S(2)}, u32[]{:S(2)}) collective-permute-start(bf16[112,128]{1,0:T(8,128)(2,1)S(1)} %shard_map.118.refs_0_), channel_id=1, source_target_pairs={{0,24},{4,28},{8,32},{12,36},{16,40},{20,44},{24,48},{28,52},{32,5... | collective-permute-start | bytes 86024 | tf_op jit(solution)/shard_map/ppermute | solution.py:496
  130.5 27.8 %collective-permute-start.10 = (bf16[112,128]{1,0:T(8,128)(2,1)S(1)}, bf16[112,128]{1,0:T(8,128)(2,1)S(1)}, u32[]{:S(2)}, u32[]{:S(2)}) collective-permute-start(bf16[112,128]{1,0:T(8,128)(2,1)S(1)} %shard_map.118.refs_0_), channel_id=1, source_target_pairs={{0,32},{4,36},{8,40},{12,44},{16,48},{20,52},{24,56},{28,60},{32,0... | collective-permute-start | bytes 86024 | tf_op jit(solution)/shard_map/ppermute | solution.py:496
  132.9 25.3 %collective-permute-start.11 = (bf16[112,128]{1,0:T(8,128)(2,1)S(1)}, bf16[112,128]{1,0:T(8,128)(2,1)S(1)}, u32[]{:S(2)}, u32[]{:S(2)}) collective-permute-start(bf16[112,128]{1,0:T(8,128)(2,1)S(1)} %shard_map.118.refs_0_), channel_id=1, source_target_pairs={{0,40},{4,44},{8,48},{12,52},{16,56},{20,60},{24,0},{28,4},{32,8},... | collective-permute-start | bytes 86024 | tf_op jit(solution)/shard_map/ppermute | solution.py:496
  150.1 8.1 %collective-permute-start.12 = (bf16[112,128]{1,0:T(8,128)(2,1)S(1)}, bf16[112,128]{1,0:T(8,128)(2,1)S(1)}, u32[]{:S(2)}, u32[]{:S(2)}) collective-permute-start(bf16[112,128]{1,0:T(8,128)(2,1)S(1)} %shard_map.118.refs_0_), channel_id=1, source_target_pairs={{0,48},{4,52},{8,56},{12,60},{16,0},{20,4},{24,8},{28,12},{32,16},... | collective-permute-start | bytes 86024 | tf_op jit(solution)/shard_map/ppermute | solution.py:496
  152.5 5.7 %collective-permute-start.13 = (bf16[112,128]{1,0:T(8,128)(2,1)S(1)}, bf16[112,128]{1,0:T(8,128)(2,1)S(1)}, u32[]{:S(2)}, u32[]{:S(2)}) collective-permute-start(bf16[112,128]{1,0:T(8,128)(2,1)S(1)} %shard_map.118.refs_0_), channel_id=1, source_target_pairs={{0,56},{4,60},{8,0},{12,4},{16,8},{20,12},{24,16},{28,20},{32,24},... | collective-permute-start | bytes 86024 | tf_op jit(solution)/shard_map/ppermute | solution.py:496
  167.9 59.0 %all-to-all-start.3 = ((bf16[64,128,128]{2,1,0:T(8,128)(2,1)}), bf16[64,128,128]{2,1,0:T(8,128)(2,1)}, u32[]{:S(2)}, u32[]{:S(2)}) async-start(bf16[64,128,128]{2,1,0:T(8,128)(2,1)} %get-tuple-element.53), calls=%async_computation.3 | async-start | bytes 4194304 | tf_op jit(solution)/shard_map/all_to_all | solution.py:477
  176.4 7.3 %collective-permute-start.14 = (f32[112,128]{1,0:T(8,128)S(1)}, f32[112,128]{1,0:T(8,128)S(1)}, u32[]{:S(2)}, u32[]{:S(2)}) collective-permute-start(f32[112,128]{1,0:T(8,128)S(1)} %shard_map.120.refs_0_), channel_id=1, source_target_pairs={{0,64},{4,68},{8,72},{12,76},{16,80},{20,84},{24,88},{28,92},{32,9... | collective-permute-start | bytes 172040 | tf_op jit(solution)/shard_map/ppermute | solution.py:496
  177.8 8.9 %collective-permute-start.15 = (f32[112,128]{1,0:T(8,128)S(1)}, f32[112,128]{1,0:T(8,128)S(1)}, u32[]{:S(2)}, u32[]{:S(2)}) collective-permute-start(f32[112,128]{1,0:T(8,128)S(1)} %shard_map.120.refs_0_), channel_id=1, source_target_pairs={{0,128},{4,132},{8,136},{12,140},{16,144},{20,148},{24,152},{28,15... | collective-permute-start | bytes 172040 | tf_op jit(solution)/shard_map/ppermute | solution.py:496
  180.4 6.3 %collective-permute-start.16 = (f32[112,128]{1,0:T(8,128)S(1)}, f32[112,128]{1,0:T(8,128)S(1)}, u32[]{:S(2)}, u32[]{:S(2)}) collective-permute-start(f32[112,128]{1,0:T(8,128)S(1)} %shard_map.120.refs_0_), channel_id=1, source_target_pairs={{0,192},{4,196},{8,200},{12,204},{16,208},{20,212},{24,216},{28,22... | collective-permute-start | bytes 172040 | tf_op jit(solution)/shard_map/ppermute | solution.py:496
  188.6 7.1 %collective-permute-start.18 = (bf16[400,128]{1,0:T(8,128)(2,1)S(1)}, bf16[400,128]{1,0:T(8,128)(2,1)S(1)}, u32[]{:S(2)}, u32[]{:S(2)}) collective-permute-start(bf16[400,128]{1,0:T(8,128)(2,1)S(1)} %shard_map.121.refs_0_), channel_id=1, source_target_pairs={{0,2},{1,3},{2,0},{3,1},{4,6},{5,7},{6,4},{7,5},{8,10},{9,11},{10,... | collective-permute-start | bytes 307208 | tf_op jit(solution)/shard_map/ppermute | solution.py:495
  236.6 45.7 %all-to-all-start.5 = ((bf16[64,80,128]{2,1,0:T(8,128)(2,1)}), bf16[64,80,128]{2,1,0:T(8,128)(2,1)S(1)}, u32[]{:S(2)}, u32[]{:S(2)}) async-start(bf16[64,80,128]{2,1,0:T(8,128)(2,1)} %get-tuple-element.66), calls=%async_computation.5 | async-start | bytes 2621440 | tf_op jit(solution)/shard_map/all_to_all | solution.py:477
  247.1 7.3 %collective-permute-start.23 = (bf16[400,128]{1,0:T(8,128)(2,1)S(1)}, bf16[400,128]{1,0:T(8,128)(2,1)S(1)}, u32[]{:S(2)}, u32[]{:S(2)}) collective-permute-start(bf16[400,128]{1,0:T(8,128)(2,1)S(1)} %get-tuple-element.60), channel_id=1, source_target_pairs={{0,2},{1,3},{2,0},{3,1},{4,6},{5,7},{6,4},{7,5},{8,10},{9,11},{10,... | collective-permute-start | bytes 307208 | tf_op jit(solution)/shard_map/ppermute | solution.py:495
  256.4 9.2 %collective-permute-start.26 = (f32[112,128]{1,0:T(8,128)S(1)}, f32[112,128]{1,0:T(8,128)S(1)}, u32[]{:S(2)}, u32[]{:S(2)}) collective-permute-start(f32[112,128]{1,0:T(8,128)S(1)} %get-tuple-element.64), channel_id=1, source_target_pairs={{0,128},{4,132},{8,136},{12,140},{16,144},{20,148},{24,152},{28,15... | collective-permute-start | bytes 172040 | tf_op jit(solution)/shard_map/ppermute | solution.py:496
  259.2 6.4 %collective-permute-start.27 = (f32[112,128]{1,0:T(8,128)S(1)}, f32[112,128]{1,0:T(8,128)S(1)}, u32[]{:S(2)}, u32[]{:S(2)}) collective-permute-start(f32[112,128]{1,0:T(8,128)S(1)} %get-tuple-element.65), channel_id=1, source_target_pairs={{0,192},{4,196},{8,200},{12,204},{16,208},{20,212},{24,216},{28,22... | collective-permute-start | bytes 172040 | tf_op jit(solution)/shard_map/ppermute | solution.py:496
  265.6 9.3 %collective-permute-start.28 = (bf16[112,128]{1,0:T(8,128)(2,1)S(1)}, bf16[112,128]{1,0:T(8,128)(2,1)S(1)}, u32[]{:S(2)}, u32[]{:S(2)}) collective-permute-start(bf16[112,128]{1,0:T(8,128)(2,1)S(1)} %shard_map.128.refs_0_), channel_id=1, source_target_pairs={{0,8},{4,12},{8,16},{12,20},{16,24},{20,28},{24,32},{28,36},{32,40... | collective-permute-start | bytes 86024 | tf_op jit(solution)/shard_map/ppermute | solution.py:496
  265.7 12.4 %collective-permute-start.29 = (bf16[112,128]{1,0:T(8,128)(2,1)S(1)}, bf16[112,128]{1,0:T(8,128)(2,1)S(1)}, u32[]{:S(2)}, u32[]{:S(2)}) collective-permute-start(bf16[112,128]{1,0:T(8,128)(2,1)S(1)} %shard_map.128.refs_0_), channel_id=1, source_target_pairs={{0,16},{4,20},{8,24},{12,28},{16,32},{20,36},{24,40},{28,44},{32,4... | collective-permute-start | bytes 86024 | tf_op jit(solution)/shard_map/ppermute | solution.py:496
  267.5 11.8 %collective-permute-start.30 = (bf16[112,128]{1,0:T(8,128)(2,1)S(1)}, bf16[112,128]{1,0:T(8,128)(2,1)S(1)}, u32[]{:S(2)}, u32[]{:S(2)}) collective-permute-start(bf16[112,128]{1,0:T(8,128)(2,1)S(1)} %shard_map.128.refs_0_), channel_id=1, source_target_pairs={{0,24},{4,28},{8,32},{12,36},{16,40},{20,44},{24,48},{28,52},{32,5... | collective-permute-start | bytes 86024 | tf_op jit(solution)/shard_map/ppermute | solution.py:496
  270.6 10.9 %collective-permute-start.31 = (bf16[112,128]{1,0:T(8,128)(2,1)S(1)}, bf16[112,128]{1,0:T(8,128)(2,1)S(1)}, u32[]{:S(2)}, u32[]{:S(2)}) collective-permute-start(bf16[112,128]{1,0:T(8,128)(2,1)S(1)} %shard_map.128.refs_0_), channel_id=1, source_target_pairs={{0,32},{4,36},{8,40},{12,44},{16,48},{20,52},{24,56},{28,60},{32,0... | collective-permute-start | bytes 86024 | tf_op jit(solution)/shard_map/ppermute | solution.py:496
  271.6 10.0 %collective-permute-start.32 = (bf16[112,128]{1,0:T(8,128)(2,1)S(1)}, bf16[112,128]{1,0:T(8,128)(2,1)S(1)}, u32[]{:S(2)}, u32[]{:S(2)}) collective-permute-start(bf16[112,128]{1,0:T(8,128)(2,1)S(1)} %shard_map.128.refs_0_), channel_id=1, source_target_pairs={{0,40},{4,44},{8,48},{12,52},{16,56},{20,60},{24,0},{28,4},{32,8},... | collective-permute-start | bytes 86024 | tf_op jit(solution)/shard_map/ppermute | solution.py:496
  274.9 6.6 %collective-permute-start.33 = (bf16[112,128]{1,0:T(8,128)(2,1)S(1)}, bf16[112,128]{1,0:T(8,128)(2,1)S(1)}, u32[]{:S(2)}, u32[]{:S(2)}) collective-permute-start(bf16[112,128]{1,0:T(8,128)(2,1)S(1)} %shard_map.128.refs_0_), channel_id=1, source_target_pairs={{0,48},{4,52},{8,56},{12,60},{16,0},{20,4},{24,8},{28,12},{32,16},... | collective-permute-start | bytes 86024 | tf_op jit(solution)/shard_map/ppermute | solution.py:496
  282.3 41.1 %all-to-all-start.4 = ((bf16[64,48,128]{2,1,0:T(8,128)(2,1)}), bf16[64,48,128]{2,1,0:T(8,128)(2,1)}, u32[]{:S(2)}, u32[]{:S(2)}) async-start(bf16[64,48,128]{2,1,0:T(8,128)(2,1)} %shard_map.130), calls=%async_computation.4 | async-start | bytes 1572864 | tf_op jit(solution)/shard_map/all_to_all | solution.py:477
  294.1 5.8 %collective-permute-start.35 = (f32[112,128]{1,0:T(8,128)S(1)}, f32[112,128]{1,0:T(8,128)S(1)}, u32[]{:S(2)}, u32[]{:S(2)}) collective-permute-start(f32[112,128]{1,0:T(8,128)S(1)} %shard_map.129.after_ref.refs_0_), channel_id=1, source_target_pairs={{0,64},{4,68},{8,72},{12,76},{16,80},{20,84},{24,88},{28,92},{32,9... | collective-permute-start | bytes 172040 | tf_op jit(solution)/shard_map/ppermute | solution.py:496
  295.6 5.6 %collective-permute-start.36 = (f32[112,128]{1,0:T(8,128)S(1)}, f32[112,128]{1,0:T(8,128)S(1)}, u32[]{:S(2)}, u32[]{:S(2)}) collective-permute-start(f32[112,128]{1,0:T(8,128)S(1)} %shard_map.129.after_ref.refs_0_), channel_id=1, source_target_pairs={{0,128},{4,132},{8,136},{12,140},{16,144},{20,148},{24,152},{28,15... | collective-permute-start | bytes 172040 | tf_op jit(solution)/shard_map/ppermute | solution.py:496
  303.4 6.2 %collective-permute-start.39 = (bf16[400,128]{1,0:T(8,128)(2,1)S(1)}, bf16[400,128]{1,0:T(8,128)(2,1)S(1)}, u32[]{:S(2)}, u32[]{:S(2)}) collective-permute-start(bf16[400,128]{1,0:T(8,128)(2,1)S(1)} %shard_map.133.refs_0_), channel_id=1, source_target_pairs={{0,2},{1,3},{2,0},{3,1},{4,6},{5,7},{6,4},{7,5},{8,10},{9,11},{10,... | collective-permute-start | bytes 307208 | tf_op jit(solution)/shard_map/ppermute | solution.py:495
  (26 other events, 261.5 us)

commit v7 on v6

--- a/solution.py
+++ b/solution.py
@@ -198,6 +198,13 @@
     return new, jnp.where(iota((128, 128), 1) == b, state, states)
 
 
+def apply_rows(b, total, accum_ref, new_accum_ref, rows_ref):
+    accum = lane_to_column(accum_ref[b : b + 1, :])
+    accum = accum + jnp.sum(total * total, axis=1, keepdims=True) / WIDTH
+    new_accum_ref[b : b + 1, :] = jnp.transpose(accum)[:1]
+    return rows_ref[128 * b : 128 * b + 128, :] - total * (RATE * lax.rsqrt(accum[:, :1]))
+
+
 def update(
     step, wire_in_ref, flat_ref, table_ref, accum_ref, named_ref, *rest
 ):
@@ -211,17 +218,15 @@
     unpack_all(copies, held_ref, grads_ref)
     table_copy.wait()
     outs = []
-    states = to_columns(accum_ref)
     for b in range(8):
         here = pl.ds(128 * b, 128)
         hit = one_hot(iota((128, SLOTS), 0) + 128 * b == flat_ref[step : step + 1, :])
         total = to_narrow(dot(hit, grads_ref[...]))
-        new, states = adagrad(b, total, rows_ref[here, :], states)
+        new = apply_rows(b, total, accum_ref, new_accum_ref, rows_ref)
         rows_ref[here, :] = new
         outs.append(pltpu.make_async_copy(rows_ref.at[here], new_table_ref.at[0, here], out_sems.at[b]))
         outs[-1].start()
         wide_ref[here, :] = to_wide(new).astype(BF16)
-    new_accum_ref[...] = jnp.transpose(states)[:8]
     gather_rows(named_ref, step + 1, wide_ref, wire_ref, sent_ref, sent_sems)
     for copy in outs:
         copy.wait()
@@ -249,16 +254,14 @@
     unpack_all(copies, held_ref, grads_ref, unpack_second)
     table_copy.wait()
     outs = []
-    states = to_columns(accum_ref)
     for b in range(8):
         here = pl.ds(128 * b, 128)
         hit = one_hot(iota((128, SLOTS), 0) + 128 * b == flat_ref[step : step + 1, :])
         total = to_narrow(jnp.concatenate([sums_ref[here, :], dot(hit, grads_ref[...])], axis=1))
-        new, states = adagrad(b, total, rows_ref[here, :], states)
+        new = apply_rows(b, total, accum_ref, new_accum_ref, rows_ref)
         turned_ref[b] = jnp.transpose(new)
         outs.append(pltpu.make_async_copy(turned_ref.at[b], new_table_ref.at[0, :, here], out_sems.at[b]))
         outs[-1].start()
-    new_accum_ref[...] = jnp.transpose(states)[:8]
     for copy in outs:
         copy.wait()
 
@@ -309,7 +312,6 @@
     for g in range(parts):
         here = slice(part * g, part * g + part)
         hit = one_hot(slots_column == iota((2 * edges, part), 1) + part * g)
-        weights_ref[2 * edges :, here] = hit
         fetched = fetched + dot(hit, rows_ref[here, :])
     fetched = to_narrow(fetched)
     head, tail = fetched[:edges], fetched[edges:]
@@ -326,7 +328,7 @@
         scores = dot(queries, rows_ref[here, :], ((1,), (1,)))
         weights = jax.nn.sigmoid(scores) * (negative_ref[step : step + 1, here] / 1024)
         weights = weights.astype(BF16)
-        weights_ref[: 2 * edges, here] = weights
+        weights_ref[:, here] = weights
         pull = pull + dot(weights, rows_ref[here, :])
     pull = to_narrow(pull)
     positive_weight = -jax.nn.sigmoid(-positive)
@@ -337,11 +339,12 @@
         push_re * rel_re - push_im * rel_im, push_re * rel_im + push_im * rel_re
     )
     edge_grads = to_wide(jnp.concatenate([grad_head, grad_tail], axis=0)).astype(BF16)
-    edge_grads = jnp.concatenate([queries, edge_grads], axis=0)
     outs = []
     for g in range(parts):
         here = slice(part * g, part * g + part)
-        grads = dot(weights_ref[:, here], edge_grads, ((0,), (0,)))
+        grads = dot(weights_ref[:, here], queries, ((0,), (0,)))
+        hit = one_hot(iota((part, 2 * edges), 0) + part * g == slots)
+        grads = grads + dot(hit, edge_grads)
         for j in range(per):
             sent_ref[per * g + j] = pack(grads[CAP * j : CAP * j + CAP]).astype(BF16)
         blocks = pl.ds(per * g, per)
@@ -404,11 +407,15 @@
     out_ref[...] = total.astype(BF16)
 
 
+def add_pair(own_ref, other_ref, out_ref):
+    out_ref[...] = (own_ref[...].astype(F32) + other_ref[...].astype(F32)).astype(BF16)
+
+
 def sum_z(at_ref, *refs):
     *parts, out_ref, all_ref = refs
     n = len(parts)
     for d in range(n):
-        all_ref[lax.rem(at_ref[2] + n - d, n)] = parts[d][...].astype(F32)
+        all_ref[lax.rem(at_ref[2] + 8 - d, n)] = parts[d][...].astype(F32)
     total = all_ref[0]
     for z in range(1, n):
         total = total + all_ref[z]
@@ -441,7 +448,12 @@
         mine, other = mine_ref[here, :], other_ref[here, :]
         dense = jnp.where(at_ref[3] == b // (count // 2), mine, other).astype(F32)
         total = jnp.concatenate([unpack_relations(dense[:200]), unpack_relations(dense[200:])], axis=0)
-        new_table_ref[rows, :], states = adagrad(b, total, table_ref[rows, :], states)
+        new, states = adagrad(b, total, table_ref[rows, :], states)
+        if new_table_ref.shape[0] == REL:
+            new_table_ref[rows, :] = new
+        else:
+            end = min(128 * b + 128, new_table_ref.shape[1])
+            new_table_ref[:, 128 * b : end] = jnp.transpose(new)[:, : end - 128 * b]
     new_state_ref[...] = jnp.transpose(states)[:8]
 
 
@@ -496,7 +508,7 @@
     return lax.ppermute(x, "edge", edge_pairs(d if axis == 1 else 0, d if axis == 2 else 0))
 
 
-def relation_scatter(at, keep, give):
+def relation_scatter(at, keep, give, last):
     shape = jax.ShapeDtypeStruct
     arrived = [lax.ppermute(give, "edge", edge_pairs(0, 0, 1))]
     own = keep
@@ -510,8 +522,12 @@
         )(at, own, *arrived)
         arrived = [move(part, axis, d + 1) for d, part in enumerate(parts)]
     own = kernel(sum_y, "vvvv", [shape(own.shape, BF16)], "v")(own, *arrived)[0]
-    arrived = [move(own, 2, d) for d in range(1, 8)]
-    own = kernel(sum_z, "s" + "v" * 8, [shape(own.shape, F32)], "v", [pltpu.VMEM((8, *own.shape), F32)])(
+    n = 8
+    if last:
+        own = kernel(add_pair, "vv", [shape(own.shape, BF16)], "v")(own, move(own, 2, 4))[0]
+        n = 4
+    arrived = [move(own, 2, d) for d in range(1, n)]
+    own = kernel(sum_z, "s" + "v" * n, [shape(own.shape, F32)], "v", [pltpu.VMEM((n, *own.shape), F32)])(
         at, own, *arrived
     )[0]
     return own, arrived
@@ -567,14 +583,14 @@
             wires + [dense, dense],
             "h" * len(wires) + "hh",
             [
-                pltpu.VMEM((SLOTS, 512), BF16), pltpu.VMEM((512, SLOTS), BF16), held, copies(WIRE_PARTS), held,
+                pltpu.VMEM((SLOTS, 512), BF16), pltpu.VMEM((256, SLOTS), BF16), held, copies(WIRE_PARTS), held,
                 pltpu.SemaphoreType.DMA((2, 4)), pltpu.VMEM((2, DENSE // 2, 128), F32),
                 pltpu.SemaphoreType.DMA((2, REL // 128)),
             ],
             4 << 30,
         )(at, rows, slots, negative, relation, rel_ids)
         grads[0] = exchange(grads[0])
-        own, arrived = relation_scatter(at, keep, give)
+        own, arrived = relation_scatter(at, keep, give, last)
         scratch = [copies(WIRE_PARTS), pltpu.SemaphoreType.DMA, copies(8)]
         outs = [shape(table.shape, F32), shape((8, 128), F32)]
         if last:
@@ -611,9 +627,12 @@
         own = relation_gather_y(at, own)
         mine, other = relation_gather_x(at, own)
         rel_table, rel_state = kernel(
-            relation_update, "svvvv", [shape((REL, WIDTH), F32), shape((8, 128), F32)], "vv"
+            relation_update,
+            "svvvv",
+            [shape((WIDTH, rel_count) if last else (REL, WIDTH), F32), shape((8, 128), F32)],
+            "vv",
         )(at, mine, other, rel_table, rel_state)
-    return table, accum.reshape(1, 1024), rel_table[:rel_count], rel_state.reshape(REL)[:rel_count]
+    return table, accum.reshape(1, 1024), rel_table.T, rel_state.reshape(REL)[:rel_count]
 
 
 def solution(mesh):

time: 336 us -> 339 us (level)
  waiting for transfers between devices: 133 us -> 144 us
  starting transfers between devices: 125 us -> 117 us
    ppermute x26 -> x23, waiting for transfers between devices: 38 us -> 48.3 us  [move(): lax.ppermute(x, 'edge', edge_pairs(d if axis == 1 else 0, d if axis == 2...]
    ppermute x26 -> x23, starting transfers between devices: 49.9 us -> 42.5 us  [move(): lax.ppermute(x, 'edge', edge_pairs(d if axis == 1 else 0, d if axis == 2...]
    unnamed x23 -> x22, local copies, waits for them, and re-layouts: 7.87 us -> 6.1 us
    pallas_call x25 -> x26, Pallas kernels: 60.2 us -> 61.8 us  [kernel(): call(*[pltpu.with_memory_space_constraint(x, pltpu.HBM) if k == 'h' else...]
  transfers between devices with their start and end apart: 48 -> 45, of which waited for: 29 -> 31; matrix products, arithmetic and copies ran while one was open for 3% -> 2% of each run, Pallas kernels for 6% -> 6%
where the time goes in v7:
time: 339 us; the launch traced here: 333 us
  waiting for transfers between devices  144 us (42%)
  starting transfers between devices  117 us (35%)
  Pallas kernels  61.8 us (18%)
  local copies, waits for them, and re-layouts  8.42 us (2%)
    all_to_all x6, waiting for transfers between devices, exchange(): return lax.all_to_all(x, 'edge', split_axis=0, concat_axis=0, tiled=True)  74.1 us
    pallas_call x26, Pallas kernels, kernel(): call(*[pltpu.with_memory_space_constraint(x, pltpu.HBM) if k == 'h' else...  61.8 us
    all_to_all x6, starting transfers between devices, exchange(): return lax.all_to_all(x, 'edge', split_axis=0, concat_axis=0, tiled=True)  50.6 us
    ppermute x23, waiting for transfers between devices, move(): lax.ppermute(x, 'edge', edge_pairs(d if axis == 1 else 0, d if axis == 2...  48.3 us
    ppermute x23, starting transfers between devices, move(): lax.ppermute(x, 'edge', edge_pairs(d if axis == 1 else 0, d if axis == 2...  42.5 us
    ppermute x12, starting transfers between devices, move(): return lax.ppermute(x, 'rep', [(k, (k + d) % 4) for k in range(4)])  19.6 us
    ppermute x12, waiting for transfers between devices, move(): return lax.ppermute(x, 'rep', [(k, (k + d) % 4) for k in range(4)])  14.8 us
  transfers between devices with their start and end apart: 45, of which 31 were waited for; matrix products, arithmetic and copies ran while one was open for 2% of the time, Pallas kernels for 6%

profile of v7, /device:TPU:1, one launch (start us, length us, event | category | flops | bytes accessed | tf_op | source)
XLA Modules:
  0.0 333.0 jit_solution(5830662428365648107)
XLA Ops:
  3.1 13.2 %all-to-all-start = ((s32[64,1,128]{2,1,0:T(1,128)}), s32[64,1,128]{2,1,0:T(1,128)S(1)}, u32[]{:S(2)}, u32[]{:S(2)}) async-start(s32[64,1,128]{2,1,0:T(1,128)} %bitcast.20), calls=%async_computation | async-start | bytes 65536 | tf_op jit(solution)/shard_map/all_to_all | solution.py:489
  18.6 6.8 %all-to-all-done = s32[64,1,128]{2,1,0:T(1,128)S(1)} async-done(((s32[64,1,128]{2,1,0:T(1,128)}), s32[64,1,128]{2,1,0:T(1,128)S(1)}, u32[]{:S(2)}, u32[]{:S(2)}) %all-to-all-start) | async-done | bytes 32800 | tf_op jit(solution)/shard_map/all_to_all | solution.py:489
  25.5 3.9 %shard_map.113 = bf16[64,128,128]{2,1,0:T(8,128)(2,1)} custom-call(bf16[1024,512]{1,0:T(8,128)(2,1)S(1)} %shard_map.111.wide_ref, s32[64,128]{1,0:T(8,128)S(1)} %bitcast.16), custom_call_target="tpu_custom_call" | custom-call | flops 3221225472 | bytes 1048576 | tf_op jit(solution)/shard_map/pallas_call | solution.py:479
  29.4 6.0 %all-to-all-start.1 = ((bf16[64,128,128]{2,1,0:T(8,128)(2,1)}), bf16[64,128,128]{2,1,0:T(8,128)(2,1)}, u32[]{:S(2)}, u32[]{:S(2)}) async-start(bf16[64,128,128]{2,1,0:T(8,128)(2,1)} %shard_map.113), calls=%async_computation.1 | async-start | bytes 4194304 | tf_op jit(solution)/shard_map/all_to_all | solution.py:489
  35.7 2.9 copy.21
  41.3 45.1 %all-to-all-done.1.refs_1_ = bf16[64,128,128]{2,1,0:T(8,128)(2,1)} async-done(((bf16[64,128,128]{2,1,0:T(8,128)(2,1)}), bf16[64,128,128]{2,1,0:T(8,128)(2,1)}, u32[]{:S(2)}, u32[]{:S(2)}) %all-to-all-start.1) | async-done | bytes 2097184 | tf_op jit(solution)/shard_map/all_to_all | solution.py:489
  86.5 9.6 %shard_map.115 = (bf16[64,128,128]{2,1,0:T(8,128)(2,1)}, f32[1600,128]{1,0:T(8,128)}, f32[1600,128]{1,0:T(8,128)}) custom-call(s32[4]{0:T(128)S(1)} %pad_add_fusion.1.refs_0_.at_ref, bf16[64,128,128]{2,1,0:T(8,128)(2,1)} %all-to-all-done.1.refs_1_, s32[2,256]{1,0:T(2,128)S(1)} %get-tuple-element.40.refs_2_, f32[2,2560]{1,0:T(2,128)S(1)} %pad_maximum_fusion.refs_3_, ...), custom_call_target="tpu_custom_call" | custom-call | flops 4294967296 | bytes 1048576 | tf_op jit(solution)/shard_map/pallas_call | solution.py:479
  96.1 6.2 %all-to-all-start.2 = ((bf16[64,128,128]{2,1,0:T(8,128)(2,1)}), bf16[64,128,128]{2,1,0:T(8,128)(2,1)}, u32[]{:S(2)}, u32[]{:S(2)}) async-start(bf16[64,128,128]{2,1,0:T(8,128)(2,1)} %get-tuple-element.42), calls=%async_computation.2 | async-start | bytes 4194304 | tf_op jit(solution)/shard_map/all_to_all | solution.py:489
  111.3 3.2 collective-permute-done.2.refs_3_
  125.0 3.2 collective-permute-start.8
  135.0 15.0 %collective-permute-done.7.refs_5_.refs_1_ = bf16[112,128]{1,0:T(8,128)(2,1)S(1)} collective-permute-done((bf16[112,128]{1,0:T(8,128)(2,1)S(1)}, bf16[112,128]{1,0:T(8,128)(2,1)S(1)}, u32[]{:S(2)}, u32[]{:S(2)}) %collective-permute-start.7) | collective-permute-done | bytes 28704 | tf_op jit(solution)/shard_map/ppermute | solution.py:508
  154.7 3.5 %collective-permute-done.10.refs_8_.refs_4_ = bf16[112,128]{1,0:T(8,128)(2,1)S(1)} collective-permute-done((bf16[112,128]{1,0:T(8,128)(2,1)S(1)}, bf16[112,128]{1,0:T(8,128)(2,1)S(1)}, u32[]{:S(2)}, u32[]{:S(2)}) %collective-permute-start.10) | collective-permute-done | bytes 28704 | tf_op jit(solution)/shard_map/ppermute | solution.py:508
  158.2 9.4 %shard_map.119 = (f32[1,1024,400]{2,1,0:T(8,128)}, f32[8,128]{1,0:T(8,128)S(1)}, bf16[64,128,128]{2,1,0:T(8,128)(2,1)}) custom-call(bf16[64,128,128]{2,1,0:T(8,128)(2,1)} %all-to-all-done.2.refs_0_, s32[2,2560]{1,0:T(2,128)S(1)} %pad_add_fusion.refs_1_, f32[1,1024,400]{2,1,0:T(8,128)} %copy-done, f32[8,128]{1,0:T(8,128)S(1)} %bitcast.19, ...), custom_call_target="tpu_custom_call" | custom-call | flops 5368709120 | bytes 1048576 | tf_op jit(solution)/shard_map/pallas_call | solution.py:479
  167.6 7.8 %all-to-all-start.3 = ((bf16[64,128,128]{2,1,0:T(8,128)(2,1)}), bf16[64,128,128]{2,1,0:T(8,128)(2,1)}, u32[]{:S(2)}, u32[]{:S(2)}) async-start(bf16[64,128,128]{2,1,0:T(8,128)(2,1)} %get-tuple-element.53), calls=%async_computation.3 | async-start | bytes 4194304 | tf_op jit(solution)/shard_map/all_to_all | solution.py:489
  177.5 2.6 collective-permute-start.15
  183.3 3.1 collective-permute-done.15.refs_2_
  192.2 3.2 collective-permute-done.18.refs_2_
  198.8 3.5 %shard_map.123 = (f32[1024,400]{1,0:T(8,128)S(1)}, f32[8,128]{1,0:T(8,128)S(1)}) custom-call(s32[4]{0:T(128)S(1)} %pad_add_fusion.1.refs_0_.at_ref, bf16[1600,128]{1,0:T(8,128)(2,1)S(1)} %shard_map.122.mine_ref, bf16[1600,128]{1,0:T(8,128)(2,1)S(1)} %collective-permute-done.20.other_ref, f32[1024,400]{1,0:T(8,128)S(1)} %pad.8.refs_0_.table_ref, ...), custom_call_target="tpu_custom_call" | custom-call | bytes 1048576 | tf_op jit(solution)/shard_map/pallas_call | solution.py:479
  204.5 22.1 %all-to-all-done.3.refs_1_ = bf16[64,128,128]{2,1,0:T(8,128)(2,1)} async-done(((bf16[64,128,128]{2,1,0:T(8,128)(2,1)}), bf16[64,128,128]{2,1,0:T(8,128)(2,1)}, u32[]{:S(2)}, u32[]{:S(2)}) %all-to-all-start.3) | async-done | bytes 2097184 | tf_op jit(solution)/shard_map/all_to_all | solution.py:489
  226.6 9.7 %shard_map.125 = (bf16[64,80,128]{2,1,0:T(8,128)(2,1)}, bf16[64,48,128]{2,1,0:T(8,128)(2,1)}, f32[1600,128]{1,0:T(8,128)}, f32[1600,128]{1,0:T(8,128)}) custom-call(s32[4]{0:T(128)S(1)} %pad_add_fusion.1.refs_0_.at_ref, bf16[64,128,128]{2,1,0:T(8,128)(2,1)} %all-to-all-done.3.refs_1_, s32[2,256]{1,0:T(2,128)S(1)} %get-tuple-element.40.refs_2_, ...), custom_call_target="tpu_custom_call" | custom-call | flops 4294967296 | bytes 1048576 | tf_op jit(solution)/shard_map/pallas_call | solution.py:479
  236.3 6.0 %all-to-all-start.5 = ((bf16[64,80,128]{2,1,0:T(8,128)(2,1)}), bf16[64,80,128]{2,1,0:T(8,128)(2,1)S(1)}, u32[]{:S(2)}, u32[]{:S(2)}) async-start(bf16[64,80,128]{2,1,0:T(8,128)(2,1)} %get-tuple-element.66), calls=%async_computation.5 | async-start | bytes 2621440 | tf_op jit(solution)/shard_map/all_to_all | solution.py:489
  250.8 3.2 collective-permute-done.23.refs_3_
  256.0 2.8 collective-permute-start.26
  259.9 5.3 %collective-permute-done.26.refs_1_ = f32[112,128]{1,0:T(8,128)S(1)} collective-permute-done((f32[112,128]{1,0:T(8,128)S(1)}, f32[112,128]{1,0:T(8,128)S(1)}, u32[]{:S(2)}, u32[]{:S(2)}) %collective-permute-start.26) | collective-permute-done | bytes 57376 | tf_op jit(solution)/shard_map/ppermute | solution.py:508
  265.3 4.1 %collective-permute-start.28 = (bf16[112,128]{1,0:T(8,128)(2,1)S(1)}, bf16[112,128]{1,0:T(8,128)(2,1)S(1)}, u32[]{:S(2)}, u32[]{:S(2)}) collective-permute-start(bf16[112,128]{1,0:T(8,128)(2,1)S(1)} %shard_map.128.own_ref), channel_id=1, source_target_pairs={{0,32},{4,36},{8,40},{12,44},{16,48},{20,52},{24,56},{28,60},{32,0... | collective-permute-start | bytes 86024 | tf_op jit(solution)/shard_map/ppermute | solution.py:508
  269.4 8.4 %collective-permute-done.28.other_ref = bf16[112,128]{1,0:T(8,128)(2,1)S(1)} collective-permute-done((bf16[112,128]{1,0:T(8,128)(2,1)S(1)}, bf16[112,128]{1,0:T(8,128)(2,1)S(1)}, u32[]{:S(2)}, u32[]{:S(2)}) %collective-permute-start.28) | collective-permute-done | bytes 28704 | tf_op jit(solution)/shard_map/ppermute | solution.py:508
  284.9 11.5 %all-to-all-start.4 = ((bf16[64,48,128]{2,1,0:T(8,128)(2,1)}), bf16[64,48,128]{2,1,0:T(8,128)(2,1)}, u32[]{:S(2)}, u32[]{:S(2)}) async-start(bf16[64,48,128]{2,1,0:T(8,128)(2,1)} %shard_map.131), calls=%async_computation.4 | async-start | bytes 1572864 | tf_op jit(solution)/shard_map/all_to_all | solution.py:489
  297.9 2.6 collective-permute-start.33
  310.3 2.6 collective-permute-done.36.refs_2_
  317.5 5.6 %shard_map.136 = (f32[400,1000]{1,0:T(8,128)}, f32[8,128]{1,0:T(8,128)}) custom-call(s32[4]{0:T(128)S(1)} %pad_add_fusion.1.refs_0_.at_ref, bf16[1600,128]{1,0:T(8,128)(2,1)S(1)} %shard_map.135.mine_ref, bf16[1600,128]{1,0:T(8,128)(2,1)S(1)} %collective-permute-done.38.other_ref, f32[1024,400]{1,0:T(8,128)S(1)} %copy-done.2, ...), custom_call_target="tpu_custom_call" | custom-call | bytes 1048576 | tf_op jit(solution)/shard_map/pallas_call | solution.py:479
  323.1 2.9 shard_map.132.refs_2_
  326.0 6.6 %shard_map.133 = (f32[1,400,1024]{2,1,0:T(8,128)}, f32[8,128]{1,0:T(8,128)}) custom-call(bf16[64,48,128]{2,1,0:T(8,128)(2,1)} %all-to-all-done.4.refs_0_, s32[2,2560]{1,0:T(2,128)S(1)} %pad_add_fusion.refs_1_, f32[1024,256]{1,0:T(8,128)S(1)} %shard_map.132.refs_2_, f32[1,1024,400]{2,1,0:T(8,128)} %get-tuple-element.67.refs_3_, ...), custom_call_target="tpu_custom_call" | custom-call | flops 2147483648 | bytes 1048576 | tf_op jit(solution)/shard_map/pallas_call | solution.py:479
  (117 shorter events, 90.0 us)
Async XLA Ops:
  3.1 22.4 %all-to-all-start = ((s32[64,1,128]{2,1,0:T(1,128)}), s32[64,1,128]{2,1,0:T(1,128)S(1)}, u32[]{:S(2)}, u32[]{:S(2)}) async-start(s32[64,1,128]{2,1,0:T(1,128)} %bitcast.20), calls=%async_computation | async-start | bytes 65536 | tf_op jit(solution)/shard_map/all_to_all | solution.py:489
  29.4 57.1 %all-to-all-start.1 = ((bf16[64,128,128]{2,1,0:T(8,128)(2,1)}), bf16[64,128,128]{2,1,0:T(8,128)(2,1)}, u32[]{:S(2)}, u32[]{:S(2)}) async-start(bf16[64,128,128]{2,1,0:T(8,128)(2,1)} %shard_map.113), calls=%async_computation.1 | async-start | bytes 4194304 | tf_op jit(solution)/shard_map/all_to_all | solution.py:489
  96.1 62.1 %all-to-all-start.2 = ((bf16[64,128,128]{2,1,0:T(8,128)(2,1)}), bf16[64,128,128]{2,1,0:T(8,128)(2,1)}, u32[]{:S(2)}, u32[]{:S(2)}) async-start(bf16[64,128,128]{2,1,0:T(8,128)(2,1)} %get-tuple-element.42), calls=%async_computation.2 | async-start | bytes 4194304 | tf_op jit(solution)/shard_map/all_to_all | solution.py:489
  105.8 5.5 %collective-permute-start.1 = (bf16[400,128]{1,0:T(8,128)(2,1)S(1)}, bf16[400,128]{1,0:T(8,128)(2,1)S(1)}, u32[]{:S(2)}, u32[]{:S(2)}) collective-permute-start(bf16[400,128]{1,0:T(8,128)(2,1)S(1)} %get-tuple-element.46), channel_id=1, source_target_pairs={{0,1},{1,2},{2,3},{3,0},{4,5},{5,6},{6,7},{7,4},{8,9},{9,10},{10,1... | collective-permute-start | bytes 307208 | tf_op jit(solution)/shard_map/ppermute | solution.py:507
  107.1 7.4 %collective-permute-start.2 = (bf16[400,128]{1,0:T(8,128)(2,1)S(1)}, bf16[400,128]{1,0:T(8,128)(2,1)S(1)}, u32[]{:S(2)}, u32[]{:S(2)}) collective-permute-start(bf16[400,128]{1,0:T(8,128)(2,1)S(1)} %get-tuple-element.47), channel_id=1, source_target_pairs={{0,2},{1,3},{2,0},{3,1},{4,6},{5,7},{6,4},{7,5},{8,10},{9,11},{10,... | collective-permute-start | bytes 307208 | tf_op jit(solution)/shard_map/ppermute | solution.py:507
  115.1 5.4 %collective-permute-start.4 = (f32[112,128]{1,0:T(8,128)S(1)}, f32[112,128]{1,0:T(8,128)S(1)}, u32[]{:S(2)}, u32[]{:S(2)}) collective-permute-start(f32[112,128]{1,0:T(8,128)S(1)} %get-tuple-element.50), channel_id=1, source_target_pairs={{0,64},{4,68},{8,72},{12,76},{16,80},{20,84},{24,88},{28,92},{32,9... | collective-permute-start | bytes 172040 | tf_op jit(solution)/shard_map/ppermute | solution.py:508
  116.4 5.3 %collective-permute-start.5 = (f32[112,128]{1,0:T(8,128)S(1)}, f32[112,128]{1,0:T(8,128)S(1)}, u32[]{:S(2)}, u32[]{:S(2)}) collective-permute-start(f32[112,128]{1,0:T(8,128)S(1)} %get-tuple-element.51), channel_id=1, source_target_pairs={{0,128},{4,132},{8,136},{12,140},{16,144},{20,148},{24,152},{28,15... | collective-permute-start | bytes 172040 | tf_op jit(solution)/shard_map/ppermute | solution.py:508
  123.4 26.7 %collective-permute-start.7 = (bf16[112,128]{1,0:T(8,128)(2,1)S(1)}, bf16[112,128]{1,0:T(8,128)(2,1)S(1)}, u32[]{:S(2)}, u32[]{:S(2)}) collective-permute-start(bf16[112,128]{1,0:T(8,128)(2,1)S(1)} %shard_map.118.refs_0_), channel_id=1, source_target_pairs={{0,8},{4,12},{8,16},{12,20},{16,24},{20,28},{24,32},{28,36},{32,40... | collective-permute-start | bytes 86024 | tf_op jit(solution)/shard_map/ppermute | solution.py:508
  125.0 27.5 %collective-permute-start.8 = (bf16[112,128]{1,0:T(8,128)(2,1)S(1)}, bf16[112,128]{1,0:T(8,128)(2,1)S(1)}, u32[]{:S(2)}, u32[]{:S(2)}) collective-permute-start(bf16[112,128]{1,0:T(8,128)(2,1)S(1)} %shard_map.118.refs_0_), channel_id=1, source_target_pairs={{0,16},{4,20},{8,24},{12,28},{16,32},{20,36},{24,40},{28,44},{32,4... | collective-permute-start | bytes 86024 | tf_op jit(solution)/shard_map/ppermute | solution.py:508
  128.5 26.2 %collective-permute-start.9 = (bf16[112,128]{1,0:T(8,128)(2,1)S(1)}, bf16[112,128]{1,0:T(8,128)(2,1)S(1)}, u32[]{:S(2)}, u32[]{:S(2)}) collective-permute-start(bf16[112,128]{1,0:T(8,128)(2,1)S(1)} %shard_map.118.refs_0_), channel_id=1, source_target_pairs={{0,24},{4,28},{8,32},{12,36},{16,40},{20,44},{24,48},{28,52},{32,5... | collective-permute-start | bytes 86024 | tf_op jit(solution)/shard_map/ppermute | solution.py:508
  130.5 27.7 %collective-permute-start.10 = (bf16[112,128]{1,0:T(8,128)(2,1)S(1)}, bf16[112,128]{1,0:T(8,128)(2,1)S(1)}, u32[]{:S(2)}, u32[]{:S(2)}) collective-permute-start(bf16[112,128]{1,0:T(8,128)(2,1)S(1)} %shard_map.118.refs_0_), channel_id=1, source_target_pairs={{0,32},{4,36},{8,40},{12,44},{16,48},{20,52},{24,56},{28,60},{32,0... | collective-permute-start | bytes 86024 | tf_op jit(solution)/shard_map/ppermute | solution.py:508
  132.8 25.4 %collective-permute-start.11 = (bf16[112,128]{1,0:T(8,128)(2,1)S(1)}, bf16[112,128]{1,0:T(8,128)(2,1)S(1)}, u32[]{:S(2)}, u32[]{:S(2)}) collective-permute-start(bf16[112,128]{1,0:T(8,128)(2,1)S(1)} %shard_map.118.refs_0_), channel_id=1, source_target_pairs={{0,40},{4,44},{8,48},{12,52},{16,56},{20,60},{24,0},{28,4},{32,8},... | collective-permute-start | bytes 86024 | tf_op jit(solution)/shard_map/ppermute | solution.py:508
  150.1 8.1 %collective-permute-start.12 = (bf16[112,128]{1,0:T(8,128)(2,1)S(1)}, bf16[112,128]{1,0:T(8,128)(2,1)S(1)}, u32[]{:S(2)}, u32[]{:S(2)}) collective-permute-start(bf16[112,128]{1,0:T(8,128)(2,1)S(1)} %shard_map.118.refs_0_), channel_id=1, source_target_pairs={{0,48},{4,52},{8,56},{12,60},{16,0},{20,4},{24,8},{28,12},{32,16},... | collective-permute-start | bytes 86024 | tf_op jit(solution)/shard_map/ppermute | solution.py:508
  152.5 5.7 %collective-permute-start.13 = (bf16[112,128]{1,0:T(8,128)(2,1)S(1)}, bf16[112,128]{1,0:T(8,128)(2,1)S(1)}, u32[]{:S(2)}, u32[]{:S(2)}) collective-permute-start(bf16[112,128]{1,0:T(8,128)(2,1)S(1)} %shard_map.118.refs_0_), channel_id=1, source_target_pairs={{0,56},{4,60},{8,0},{12,4},{16,8},{20,12},{24,16},{28,20},{32,24},... | collective-permute-start | bytes 86024 | tf_op jit(solution)/shard_map/ppermute | solution.py:508
  167.6 59.0 %all-to-all-start.3 = ((bf16[64,128,128]{2,1,0:T(8,128)(2,1)}), bf16[64,128,128]{2,1,0:T(8,128)(2,1)}, u32[]{:S(2)}, u32[]{:S(2)}) async-start(bf16[64,128,128]{2,1,0:T(8,128)(2,1)} %get-tuple-element.53), calls=%async_computation.3 | async-start | bytes 4194304 | tf_op jit(solution)/shard_map/all_to_all | solution.py:489
  176.1 7.3 %collective-permute-start.14 = (f32[112,128]{1,0:T(8,128)S(1)}, f32[112,128]{1,0:T(8,128)S(1)}, u32[]{:S(2)}, u32[]{:S(2)}) collective-permute-start(f32[112,128]{1,0:T(8,128)S(1)} %shard_map.120.refs_0_), channel_id=1, source_target_pairs={{0,64},{4,68},{8,72},{12,76},{16,80},{20,84},{24,88},{28,92},{32,9... | collective-permute-start | bytes 172040 | tf_op jit(solution)/shard_map/ppermute | solution.py:508
  177.5 8.9 %collective-permute-start.15 = (f32[112,128]{1,0:T(8,128)S(1)}, f32[112,128]{1,0:T(8,128)S(1)}, u32[]{:S(2)}, u32[]{:S(2)}) collective-permute-start(f32[112,128]{1,0:T(8,128)S(1)} %shard_map.120.refs_0_), channel_id=1, source_target_pairs={{0,128},{4,132},{8,136},{12,140},{16,144},{20,148},{24,152},{28,15... | collective-permute-start | bytes 172040 | tf_op jit(solution)/shard_map/ppermute | solution.py:508
  180.1 6.3 %collective-permute-start.16 = (f32[112,128]{1,0:T(8,128)S(1)}, f32[112,128]{1,0:T(8,128)S(1)}, u32[]{:S(2)}, u32[]{:S(2)}) collective-permute-start(f32[112,128]{1,0:T(8,128)S(1)} %shard_map.120.refs_0_), channel_id=1, source_target_pairs={{0,192},{4,196},{8,200},{12,204},{16,208},{20,212},{24,216},{28,22... | collective-permute-start | bytes 172040 | tf_op jit(solution)/shard_map/ppermute | solution.py:508
  187.0 5.2 %collective-permute-start.17 = (bf16[400,128]{1,0:T(8,128)(2,1)S(1)}, bf16[400,128]{1,0:T(8,128)(2,1)S(1)}, u32[]{:S(2)}, u32[]{:S(2)}) collective-permute-start(bf16[400,128]{1,0:T(8,128)(2,1)S(1)} %shard_map.121.refs_0_), channel_id=1, source_target_pairs={{0,1},{1,2},{2,3},{3,0},{4,5},{5,6},{6,7},{7,4},{8,9},{9,10},{10,1... | collective-permute-start | bytes 307208 | tf_op jit(solution)/shard_map/ppermute | solution.py:507
  188.3 7.1 %collective-permute-start.18 = (bf16[400,128]{1,0:T(8,128)(2,1)S(1)}, bf16[400,128]{1,0:T(8,128)(2,1)S(1)}, u32[]{:S(2)}, u32[]{:S(2)}) collective-permute-start(bf16[400,128]{1,0:T(8,128)(2,1)S(1)} %shard_map.121.refs_0_), channel_id=1, source_target_pairs={{0,2},{1,3},{2,0},{3,1},{4,6},{5,7},{6,4},{7,5},{8,10},{9,11},{10,... | collective-permute-start | bytes 307208 | tf_op jit(solution)/shard_map/ppermute | solution.py:507
  236.3 48.6 %all-to-all-start.5 = ((bf16[64,80,128]{2,1,0:T(8,128)(2,1)}), bf16[64,80,128]{2,1,0:T(8,128)(2,1)S(1)}, u32[]{:S(2)}, u32[]{:S(2)}) async-start(bf16[64,80,128]{2,1,0:T(8,128)(2,1)} %get-tuple-element.66), calls=%async_computation.5 | async-start | bytes 2621440 | tf_op jit(solution)/shard_map/all_to_all | solution.py:489
  245.4 5.4 %collective-permute-start.22 = (bf16[400,128]{1,0:T(8,128)(2,1)S(1)}, bf16[400,128]{1,0:T(8,128)(2,1)S(1)}, u32[]{:S(2)}, u32[]{:S(2)}) collective-permute-start(bf16[400,128]{1,0:T(8,128)(2,1)S(1)} %get-tuple-element.59), channel_id=1, source_target_pairs={{0,1},{1,2},{2,3},{3,0},{4,5},{5,6},{6,7},{7,4},{8,9},{9,10},{10,1... | collective-permute-start | bytes 307208 | tf_op jit(solution)/shard_map/ppermute | solution.py:507
  246.7 7.3 %collective-permute-start.23 = (bf16[400,128]{1,0:T(8,128)(2,1)S(1)}, bf16[400,128]{1,0:T(8,128)(2,1)S(1)}, u32[]{:S(2)}, u32[]{:S(2)}) collective-permute-start(bf16[400,128]{1,0:T(8,128)(2,1)S(1)} %get-tuple-element.60), channel_id=1, source_target_pairs={{0,2},{1,3},{2,0},{3,1},{4,6},{5,7},{6,4},{7,5},{8,10},{9,11},{10,... | collective-permute-start | bytes 307208 | tf_op jit(solution)/shard_map/ppermute | solution.py:507
  254.6 5.3 %collective-permute-start.25 = (f32[112,128]{1,0:T(8,128)S(1)}, f32[112,128]{1,0:T(8,128)S(1)}, u32[]{:S(2)}, u32[]{:S(2)}) collective-permute-start(f32[112,128]{1,0:T(8,128)S(1)} %get-tuple-element.63), channel_id=1, source_target_pairs={{0,64},{4,68},{8,72},{12,76},{16,80},{20,84},{24,88},{28,92},{32,9... | collective-permute-start | bytes 172040 | tf_op jit(solution)/shard_map/ppermute | solution.py:508
  256.0 9.2 %collective-permute-start.26 = (f32[112,128]{1,0:T(8,128)S(1)}, f32[112,128]{1,0:T(8,128)S(1)}, u32[]{:S(2)}, u32[]{:S(2)}) collective-permute-start(f32[112,128]{1,0:T(8,128)S(1)} %get-tuple-element.64), channel_id=1, source_target_pairs={{0,128},{4,132},{8,136},{12,140},{16,144},{20,148},{24,152},{28,15... | collective-permute-start | bytes 172040 | tf_op jit(solution)/shard_map/ppermute | solution.py:508
  258.8 6.4 %collective-permute-start.27 = (f32[112,128]{1,0:T(8,128)S(1)}, f32[112,128]{1,0:T(8,128)S(1)}, u32[]{:S(2)}, u32[]{:S(2)}) collective-permute-start(f32[112,128]{1,0:T(8,128)S(1)} %get-tuple-element.65), channel_id=1, source_target_pairs={{0,192},{4,196},{8,200},{12,204},{16,208},{20,212},{24,216},{28,22... | collective-permute-start | bytes 172040 | tf_op jit(solution)/shard_map/ppermute | solution.py:508
  265.3 12.6 %collective-permute-start.28 = (bf16[112,128]{1,0:T(8,128)(2,1)S(1)}, bf16[112,128]{1,0:T(8,128)(2,1)S(1)}, u32[]{:S(2)}, u32[]{:S(2)}) collective-permute-start(bf16[112,128]{1,0:T(8,128)(2,1)S(1)} %shard_map.128.own_ref), channel_id=1, source_target_pairs={{0,32},{4,36},{8,40},{12,44},{16,48},{20,52},{24,56},{28,60},{32,0... | collective-permute-start | bytes 86024 | tf_op jit(solution)/shard_map/ppermute | solution.py:508
  278.0 6.2 %collective-permute-start.31 = (bf16[112,128]{1,0:T(8,128)(2,1)S(1)}, bf16[112,128]{1,0:T(8,128)(2,1)S(1)}, u32[]{:S(2)}, u32[]{:S(2)}) collective-permute-start(bf16[112,128]{1,0:T(8,128)(2,1)S(1)} %shard_map.129.refs_0_), channel_id=1, source_target_pairs={{0,24},{4,28},{8,32},{12,36},{16,40},{20,44},{24,48},{28,52},{32,5... | collective-permute-start | bytes 86024 | tf_op jit(solution)/shard_map/ppermute | solution.py:508
  284.9 41.1 %all-to-all-start.4 = ((bf16[64,48,128]{2,1,0:T(8,128)(2,1)}), bf16[64,48,128]{2,1,0:T(8,128)(2,1)}, u32[]{:S(2)}, u32[]{:S(2)}) async-start(bf16[64,48,128]{2,1,0:T(8,128)(2,1)} %shard_map.131), calls=%async_computation.4 | async-start | bytes 1572864 | tf_op jit(solution)/shard_map/all_to_all | solution.py:489
  296.4 5.8 %collective-permute-start.32 = (f32[112,128]{1,0:T(8,128)S(1)}, f32[112,128]{1,0:T(8,128)S(1)}, u32[]{:S(2)}, u32[]{:S(2)}) collective-permute-start(f32[112,128]{1,0:T(8,128)S(1)} %shard_map.130.after_ref.refs_0_), channel_id=1, source_target_pairs={{0,64},{4,68},{8,72},{12,76},{16,80},{20,84},{24,88},{28,92},{32,9... | collective-permute-start | bytes 172040 | tf_op jit(solution)/shard_map/ppermute | solution.py:508
  297.9 5.6 %collective-permute-start.33 = (f32[112,128]{1,0:T(8,128)S(1)}, f32[112,128]{1,0:T(8,128)S(1)}, u32[]{:S(2)}, u32[]{:S(2)}) collective-permute-start(f32[112,128]{1,0:T(8,128)S(1)} %shard_map.130.after_ref.refs_0_), channel_id=1, source_target_pairs={{0,128},{4,132},{8,136},{12,140},{16,144},{20,148},{24,152},{28,15... | collective-permute-start | bytes 172040 | tf_op jit(solution)/shard_map/ppermute | solution.py:508
  306.4 6.5 %collective-permute-start.36 = (bf16[400,128]{1,0:T(8,128)(2,1)S(1)}, bf16[400,128]{1,0:T(8,128)(2,1)S(1)}, u32[]{:S(2)}, u32[]{:S(2)}) collective-permute-start(bf16[400,128]{1,0:T(8,128)(2,1)S(1)} %shard_map.134.refs_0_), channel_id=1, source_target_pairs={{0,2},{1,3},{2,0},{3,1},{4,6},{5,7},{6,4},{7,5},{8,10},{9,11},{10,... | collective-permute-start | bytes 307208 | tf_op jit(solution)/shard_map/ppermute | solution.py:507
  (23 other events, 247.9 us)

commit v8 on v7

--- a/solution.py
+++ b/solution.py
@@ -232,42 +232,33 @@
         copy.wait()
 
 
-def first_sums(step, wire_in_ref, flat_ref, sums_ref, in_sems, held_ref, grads_ref):
-    copies = wire_copies(wire_in_ref, held_ref, in_sems)
-    for copy in copies:
-        copy.start()
-    unpack_all(copies, held_ref, grads_ref, unpack_first)
-    for b in range(8):
-        hit = one_hot(iota((128, SLOTS), 0) + 128 * b == flat_ref[step : step + 1, :])
-        sums_ref[128 * b : 128 * b + 128, :] = dot(hit, grads_ref[...])
-
-
 def last_update(
-    step, wire_in_ref, flat_ref, sums_ref, table_ref, accum_ref, new_table_ref, new_accum_ref,
-    in_sems, table_sem, out_sems, held_ref, rows_ref, grads_ref, turned_ref,
+    step, first_ref, second_ref, flat_ref, table_ref, accum_ref, new_table_ref, new_accum_ref,
+    first_sems, second_sems, table_sem, out_sems, first_held_ref, second_held_ref, rows_ref, grads_ref, turned_ref,
 ):
-    copies = wire_copies(wire_in_ref, held_ref, in_sems)
-    for copy in copies:
+    firsts = wire_copies(first_ref, first_held_ref, first_sems)
+    seconds = wire_copies(second_ref, second_held_ref, second_sems)
+    for copy in firsts + seconds:
         copy.start()
     table_copy = pltpu.make_async_copy(table_ref.at[0], rows_ref, table_sem)
     table_copy.start()
-    unpack_all(copies, held_ref, grads_ref, unpack_second)
+    unpack_all(firsts, first_held_ref, grads_ref.at[:, pl.ds(0, 256)], unpack_first)
+    unpack_all(seconds, second_held_ref, grads_ref.at[:, pl.ds(256, 256)], unpack_second)
     table_copy.wait()
     outs = []
     for b in range(8):
         here = pl.ds(128 * b, 128)
         hit = one_hot(iota((128, SLOTS), 0) + 128 * b == flat_ref[step : step + 1, :])
-        total = to_narrow(jnp.concatenate([sums_ref[here, :], dot(hit, grads_ref[...])], axis=1))
-        new = apply_rows(b, total, accum_ref, new_accum_ref, rows_ref)
-        turned_ref[b] = jnp.transpose(new)
+        total = to_narrow(dot(hit, grads_ref[...]))
+        turned_ref[b] = jnp.transpose(apply_rows(b, total, accum_ref, new_accum_ref, rows_ref))
         outs.append(pltpu.make_async_copy(turned_ref.at[b], new_table_ref.at[0, :, here], out_sems.at[b]))
         outs[-1].start()
     for copy in outs:
         copy.wait()
 
 
-def pass_on(ref, after_ref, out_ref):
-    del ref, after_ref, out_ref
+def pass_on(ref, *rest):
+    del ref, rest
 
 
 def complex_parts(x):
@@ -407,10 +398,6 @@
     out_ref[...] = total.astype(BF16)
 
 
-def add_pair(own_ref, other_ref, out_ref):
-    out_ref[...] = (own_ref[...].astype(F32) + other_ref[...].astype(F32)).astype(BF16)
-
-
 def sum_z(at_ref, *refs):
     *parts, out_ref, all_ref = refs
     n = len(parts)
@@ -508,7 +495,7 @@
     return lax.ppermute(x, "edge", edge_pairs(d if axis == 1 else 0, d if axis == 2 else 0))
 
 
-def relation_scatter(at, keep, give, last):
+def relation_scatter(at, keep, give):
     shape = jax.ShapeDtypeStruct
     arrived = [lax.ppermute(give, "edge", edge_pairs(0, 0, 1))]
     own = keep
@@ -523,9 +510,6 @@
         arrived = [move(part, axis, d + 1) for d, part in enumerate(parts)]
     own = kernel(sum_y, "vvvv", [shape(own.shape, BF16)], "v")(own, *arrived)[0]
     n = 8
-    if last:
-        own = kernel(add_pair, "vv", [shape(own.shape, BF16)], "v")(own, move(own, 2, 4))[0]
-        n = 4
     arrived = [move(own, 2, d) for d in range(1, n)]
     own = kernel(sum_z, "s" + "v" * n, [shape(own.shape, F32)], "v", [pltpu.VMEM((n, *own.shape), F32)])(
         at, own, *arrived
@@ -590,29 +574,24 @@
             4 << 30,
         )(at, rows, slots, negative, relation, rel_ids)
         grads[0] = exchange(grads[0])
-        own, arrived = relation_scatter(at, keep, give, last)
+        own, arrived = relation_scatter(at, keep, give)
         scratch = [copies(WIRE_PARTS), pltpu.SemaphoreType.DMA, copies(8)]
         outs = [shape(table.shape, F32), shape((8, 128), F32)]
         if last:
-            second = kernel(pass_on, "ha", [wires[1]], "h", aliases={0: 0})(grads[1], own)[0]
+            second = kernel(pass_on, "haa", [wires[1]], "h", aliases={0: 0})(grads[1], own, grads[0])[0]
             second = exchange(second)
-            sums = kernel(
-                lambda *refs, s=s: first_sums(s, *refs),
-                "hv",
-                [shape((1024, 256), F32)],
-                "v",
-                [copies(WIRE_PARTS), pltpu.VMEM((OWN, FIRST_ROWS, 128), BF16), pltpu.VMEM((SLOTS, 256), BF16)],
-                2 << 30,
-            )(grads[0], flat)[0]
-            scratch += [pltpu.VMEM((OWN, 128 - FIRST_ROWS, 128), BF16), pltpu.VMEM((1024, WIDTH), F32)]
             table, accum = kernel(
                 lambda *refs, s=s: last_update(s, *refs),
-                "hvvhv",
+                "hhvhv",
                 [shape((1, WIDTH, 1024), F32), outs[1]],
                 "hv",
-                scratch + [pltpu.VMEM((SLOTS, 256), BF16), pltpu.VMEM((8, WIDTH, 128), F32)],
-                2 << 30,
-            )(second, flat, sums, table, accum)
+                [
+                    copies(WIRE_PARTS), *scratch,
+                    pltpu.VMEM((OWN, FIRST_ROWS, 128), BF16), pltpu.VMEM((OWN, 128 - FIRST_ROWS, 128), BF16),
+                    pltpu.VMEM((1024, WIDTH), F32), pltpu.VMEM((SLOTS, 512), BF16), pltpu.VMEM((8, WIDTH, 128), F32),
+                ],
+                4 << 30,
+            )(grads[0], second, flat, table, accum)
             table = jnp.swapaxes(table, 1, 2)
         else:
             scratch += [held, pltpu.VMEM((1024, WIDTH), F32), pltpu.VMEM((SLOTS, 512), BF16)]

time: 339 us -> 334 us (0.985)
  waiting for transfers between devices: 144 us -> 133 us
  starting transfers between devices: 117 us -> 125 us
    ppermute x23 -> x26, waiting for transfers between devices: 48.3 us -> 38 us  [move(): lax.ppermute(x, 'edge', edge_pairs(d if axis == 1 else 0, d if axis == 2...]
    ppermute x23 -> x26, starting transfers between devices: 42.5 us -> 49.9 us  [move(): lax.ppermute(x, 'edge', edge_pairs(d if axis == 1 else 0, d if axis == 2...]
    pallas_call x26 -> x24, Pallas kernels: 61.8 us -> 59.8 us  [kernel(): call(*[pltpu.with_memory_space_constraint(x, pltpu.HBM) if k == 'h' else...]
  transfers between devices with their start and end apart: 45 -> 48, of which waited for: 31 -> 29; matrix products, arithmetic and copies ran while one was open for 2% -> 2% of each run, Pallas kernels for 6% -> 5%
where the time goes in v8:
time: 334 us; the launch traced here: 329 us
  waiting for transfers between devices  133 us (40%)
  starting transfers between devices  125 us (37%)
  Pallas kernels  59.8 us (18%)
  local copies, waits for them, and re-layouts  9.48 us (3%)
    all_to_all x6, waiting for transfers between devices, exchange(): return lax.all_to_all(x, 'edge', split_axis=0, concat_axis=0, tiled=True)  74.1 us
    pallas_call x24, Pallas kernels, kernel(): call(*[pltpu.with_memory_space_constraint(x, pltpu.HBM) if k == 'h' else...  59.8 us
    all_to_all x6, starting transfers between devices, exchange(): return lax.all_to_all(x, 'edge', split_axis=0, concat_axis=0, tiled=True)  50.8 us
    ppermute x26, starting transfers between devices, move(): lax.ppermute(x, 'edge', edge_pairs(d if axis == 1 else 0, d if axis == 2...  49.9 us
    ppermute x26, waiting for transfers between devices, move(): lax.ppermute(x, 'edge', edge_pairs(d if axis == 1 else 0, d if axis == 2...  38 us
    ppermute x12, starting transfers between devices, move(): return lax.ppermute(x, 'rep', [(k, (k + d) % 4) for k in range(4)])  18.7 us
    ppermute x12, waiting for transfers between devices, move(): return lax.ppermute(x, 'rep', [(k, (k + d) % 4) for k in range(4)])  14 us
    unnamed x22, local copies, waits for them, and re-layouts  7.16 us
  transfers between devices with their start and end apart: 48, of which 29 were waited for; matrix products, arithmetic and copies ran while one was open for 2% of the time, Pallas kernels for 5%

profile of v8, /device:TPU:1, one launch (start us, length us, event | category | flops | bytes accessed | tf_op | source)
XLA Modules:
  0.0 328.6 jit_solution(8344021966506938822)
XLA Ops:
  3.1 13.2 %all-to-all-start = ((s32[64,1,128]{2,1,0:T(1,128)}), s32[64,1,128]{2,1,0:T(1,128)S(1)}, u32[]{:S(2)}, u32[]{:S(2)}) async-start(s32[64,1,128]{2,1,0:T(1,128)} %bitcast.20), calls=%async_computation | async-start | bytes 65536 | tf_op jit(solution)/shard_map/all_to_all | solution.py:476
  18.6 6.8 %all-to-all-done = s32[64,1,128]{2,1,0:T(1,128)S(1)} async-done(((s32[64,1,128]{2,1,0:T(1,128)}), s32[64,1,128]{2,1,0:T(1,128)S(1)}, u32[]{:S(2)}, u32[]{:S(2)}) %all-to-all-start) | async-done | bytes 32800 | tf_op jit(solution)/shard_map/all_to_all | solution.py:476
  25.5 3.9 %shard_map.113 = bf16[64,128,128]{2,1,0:T(8,128)(2,1)} custom-call(bf16[1024,512]{1,0:T(8,128)(2,1)S(1)} %shard_map.111.wide_ref, s32[64,128]{1,0:T(8,128)S(1)} %bitcast.16), custom_call_target="tpu_custom_call" | custom-call | flops 3221225472 | bytes 1048576 | tf_op jit(solution)/shard_map/pallas_call | solution.py:466
  29.4 6.0 %all-to-all-start.1 = ((bf16[64,128,128]{2,1,0:T(8,128)(2,1)}), bf16[64,128,128]{2,1,0:T(8,128)(2,1)}, u32[]{:S(2)}, u32[]{:S(2)}) async-start(bf16[64,128,128]{2,1,0:T(8,128)(2,1)} %shard_map.113), calls=%async_computation.1 | async-start | bytes 4194304 | tf_op jit(solution)/shard_map/all_to_all | solution.py:476
  35.7 2.9 copy.21
  41.4 45.1 %all-to-all-done.1.refs_1_ = bf16[64,128,128]{2,1,0:T(8,128)(2,1)} async-done(((bf16[64,128,128]{2,1,0:T(8,128)(2,1)}), bf16[64,128,128]{2,1,0:T(8,128)(2,1)}, u32[]{:S(2)}, u32[]{:S(2)}) %all-to-all-start.1) | async-done | bytes 2097184 | tf_op jit(solution)/shard_map/all_to_all | solution.py:476
  86.5 9.6 %shard_map.115 = (bf16[64,128,128]{2,1,0:T(8,128)(2,1)}, f32[1600,128]{1,0:T(8,128)}, f32[1600,128]{1,0:T(8,128)}) custom-call(s32[4]{0:T(128)S(1)} %pad_add_fusion.1.refs_0_.at_ref, bf16[64,128,128]{2,1,0:T(8,128)(2,1)} %all-to-all-done.1.refs_1_, s32[2,256]{1,0:T(2,128)S(1)} %get-tuple-element.40.refs_2_, f32[2,2560]{1,0:T(2,128)S(1)} %pad_maximum_fusion.refs_3_, ...), custom_call_target="tpu_custom_call" | custom-call | flops 4294967296 | bytes 1048576 | tf_op jit(solution)/shard_map/pallas_call | solution.py:466
  96.1 6.2 %all-to-all-start.2 = ((bf16[64,128,128]{2,1,0:T(8,128)(2,1)}), bf16[64,128,128]{2,1,0:T(8,128)(2,1)}, u32[]{:S(2)}, u32[]{:S(2)}) async-start(bf16[64,128,128]{2,1,0:T(8,128)(2,1)} %get-tuple-element.42), calls=%async_computation.2 | async-start | bytes 4194304 | tf_op jit(solution)/shard_map/all_to_all | solution.py:476
  111.3 3.2 collective-permute-done.2.refs_3_
  125.0 3.2 collective-permute-start.8
  135.0 15.0 %collective-permute-done.7.refs_5_.refs_1_ = bf16[112,128]{1,0:T(8,128)(2,1)S(1)} collective-permute-done((bf16[112,128]{1,0:T(8,128)(2,1)S(1)}, bf16[112,128]{1,0:T(8,128)(2,1)S(1)}, u32[]{:S(2)}, u32[]{:S(2)}) %collective-permute-start.7) | collective-permute-done | bytes 28704 | tf_op jit(solution)/shard_map/ppermute | solution.py:495
  154.7 3.5 %collective-permute-done.10.refs_8_.refs_4_ = bf16[112,128]{1,0:T(8,128)(2,1)S(1)} collective-permute-done((bf16[112,128]{1,0:T(8,128)(2,1)S(1)}, bf16[112,128]{1,0:T(8,128)(2,1)S(1)}, u32[]{:S(2)}, u32[]{:S(2)}) %collective-permute-start.10) | collective-permute-done | bytes 28704 | tf_op jit(solution)/shard_map/ppermute | solution.py:495
  158.2 9.3 %shard_map.119 = (f32[1,1024,400]{2,1,0:T(8,128)}, f32[8,128]{1,0:T(8,128)S(1)}, bf16[64,128,128]{2,1,0:T(8,128)(2,1)}) custom-call(bf16[64,128,128]{2,1,0:T(8,128)(2,1)} %all-to-all-done.2.refs_0_, s32[2,2560]{1,0:T(2,128)S(1)} %pad_add_fusion.refs_1_.refs_2_, f32[1,1024,400]{2,1,0:T(8,128)} %copy-done, f32[8,128]{1,0:T(8,128)S(1)} %bitcast.19, ...), custom_call_target="tpu_custom_call" | custom-call | flops 5368709120 | bytes 1048576 | tf_op jit(solution)/shard_map/pallas_call | solution.py:466
  167.6 7.9 %all-to-all-start.3 = ((bf16[64,128,128]{2,1,0:T(8,128)(2,1)}), bf16[64,128,128]{2,1,0:T(8,128)(2,1)}, u32[]{:S(2)}, u32[]{:S(2)}) async-start(bf16[64,128,128]{2,1,0:T(8,128)(2,1)} %get-tuple-element.53), calls=%async_computation.3 | async-start | bytes 4194304 | tf_op jit(solution)/shard_map/all_to_all | solution.py:476
  177.5 2.6 collective-permute-start.15
  183.3 3.1 collective-permute-done.15.refs_2_
  192.2 3.2 collective-permute-done.18.refs_2_
  198.8 3.5 %shard_map.123 = (f32[1024,400]{1,0:T(8,128)S(1)}, f32[8,128]{1,0:T(8,128)S(1)}) custom-call(s32[4]{0:T(128)S(1)} %pad_add_fusion.1.refs_0_.at_ref, bf16[1600,128]{1,0:T(8,128)(2,1)S(1)} %shard_map.122.mine_ref, bf16[1600,128]{1,0:T(8,128)(2,1)S(1)} %collective-permute-done.20.other_ref, f32[1024,400]{1,0:T(8,128)S(1)} %pad.8.refs_0_.table_ref, ...), custom_call_target="tpu_custom_call" | custom-call | bytes 1048576 | tf_op jit(solution)/shard_map/pallas_call | solution.py:466
  204.5 22.1 %all-to-all-done.3.refs_1_ = bf16[64,128,128]{2,1,0:T(8,128)(2,1)} async-done(((bf16[64,128,128]{2,1,0:T(8,128)(2,1)}), bf16[64,128,128]{2,1,0:T(8,128)(2,1)}, u32[]{:S(2)}, u32[]{:S(2)}) %all-to-all-start.3) | async-done | bytes 2097184 | tf_op jit(solution)/shard_map/all_to_all | solution.py:476
  226.6 9.6 %shard_map.125 = (bf16[64,80,128]{2,1,0:T(8,128)(2,1)}, bf16[64,48,128]{2,1,0:T(8,128)(2,1)}, f32[1600,128]{1,0:T(8,128)}, f32[1600,128]{1,0:T(8,128)}) custom-call(s32[4]{0:T(128)S(1)} %pad_add_fusion.1.refs_0_.at_ref, bf16[64,128,128]{2,1,0:T(8,128)(2,1)} %all-to-all-done.3.refs_1_, s32[2,256]{1,0:T(2,128)S(1)} %get-tuple-element.40.refs_2_, ...), custom_call_target="tpu_custom_call" | custom-call | flops 4294967296 | bytes 1048576 | tf_op jit(solution)/shard_map/pallas_call | solution.py:466
  236.3 6.0 %all-to-all-start.4 = ((bf16[64,80,128]{2,1,0:T(8,128)(2,1)}), bf16[64,80,128]{2,1,0:T(8,128)(2,1)S(1)}, u32[]{:S(2)}, u32[]{:S(2)}) async-start(bf16[64,80,128]{2,1,0:T(8,128)(2,1)} %get-tuple-element.55), calls=%async_computation.4 | async-start | bytes 2621440 | tf_op jit(solution)/shard_map/all_to_all | solution.py:476
  250.8 3.2 collective-permute-done.23.refs_3_
  256.0 2.8 collective-permute-start.26
  259.9 5.3 %collective-permute-done.26.refs_1_ = f32[112,128]{1,0:T(8,128)S(1)} collective-permute-done((f32[112,128]{1,0:T(8,128)S(1)}, f32[112,128]{1,0:T(8,128)S(1)}, u32[]{:S(2)}, u32[]{:S(2)}) %collective-permute-start.26) | collective-permute-done | bytes 57376 | tf_op jit(solution)/shard_map/ppermute | solution.py:495
  267.1 3.2 collective-permute-start.30
  271.2 3.3 %collective-permute-start.32 = (bf16[112,128]{1,0:T(8,128)(2,1)S(1)}, bf16[112,128]{1,0:T(8,128)(2,1)S(1)}, u32[]{:S(2)}, u32[]{:S(2)}) collective-permute-start(bf16[112,128]{1,0:T(8,128)(2,1)S(1)} %shard_map.128.refs_0_), channel_id=1, source_target_pairs={{0,40},{4,44},{8,48},{12,52},{16,56},{20,60},{24,0},{28,4},{32,8},... | collective-permute-start | bytes 86024 | tf_op jit(solution)/shard_map/ppermute | solution.py:495
  274.6 3.2 collective-permute-start.33
  283.0 11.7 %all-to-all-start.5 = ((bf16[64,48,128]{2,1,0:T(8,128)(2,1)}), bf16[64,48,128]{2,1,0:T(8,128)(2,1)}, u32[]{:S(2)}, u32[]{:S(2)}) async-start(bf16[64,48,128]{2,1,0:T(8,128)(2,1)} %shard_map.130), calls=%async_computation.5 | async-start | bytes 1572864 | tf_op jit(solution)/shard_map/all_to_all | solution.py:476
  296.1 2.6 collective-permute-start.36
  311.0 2.6 collective-permute-start.41
  315.0 5.6 %shard_map.134 = (f32[400,1000]{1,0:T(8,128)}, f32[8,128]{1,0:T(8,128)}) custom-call(s32[4]{0:T(128)S(1)} %pad_add_fusion.1.refs_0_.at_ref, bf16[1600,128]{1,0:T(8,128)(2,1)S(1)} %shard_map.133.mine_ref, bf16[1600,128]{1,0:T(8,128)(2,1)S(1)} %collective-permute-done.41.other_ref, f32[1024,400]{1,0:T(8,128)S(1)} %copy-done.2, ...), custom_call_target="tpu_custom_call" | custom-call | bytes 1048576 | tf_op jit(solution)/shard_map/pallas_call | solution.py:466
  320.6 7.6 %shard_map.131 = (f32[1,400,1024]{2,1,0:T(8,128)}, f32[8,128]{1,0:T(8,128)}) custom-call(bf16[64,80,128]{2,1,0:T(8,128)(2,1)} %copy-done.3, bf16[64,48,128]{2,1,0:T(8,128)(2,1)} %all-to-all-done.5.refs_1_, s32[2,2560]{1,0:T(2,128)S(1)} %pad_add_fusion.refs_1_.refs_2_, f32[1,1024,400]{2,1,0:T(8,128)} %get-tuple-element.67.refs_3_, ...), custom_call_target="tpu_custom_call" | custom-call | flops 4294967296 | bytes 1048576 | tf_op jit(solution)/shard_map/pallas_call | solution.py:466
  (121 shorter events, 90.1 us)
Async XLA Ops:
  3.1 22.4 %all-to-all-start = ((s32[64,1,128]{2,1,0:T(1,128)}), s32[64,1,128]{2,1,0:T(1,128)S(1)}, u32[]{:S(2)}, u32[]{:S(2)}) async-start(s32[64,1,128]{2,1,0:T(1,128)} %bitcast.20), calls=%async_computation | async-start | bytes 65536 | tf_op jit(solution)/shard_map/all_to_all | solution.py:476
  29.4 57.1 %all-to-all-start.1 = ((bf16[64,128,128]{2,1,0:T(8,128)(2,1)}), bf16[64,128,128]{2,1,0:T(8,128)(2,1)}, u32[]{:S(2)}, u32[]{:S(2)}) async-start(bf16[64,128,128]{2,1,0:T(8,128)(2,1)} %shard_map.113), calls=%async_computation.1 | async-start | bytes 4194304 | tf_op jit(solution)/shard_map/all_to_all | solution.py:476
  96.1 62.1 %all-to-all-start.2 = ((bf16[64,128,128]{2,1,0:T(8,128)(2,1)}), bf16[64,128,128]{2,1,0:T(8,128)(2,1)}, u32[]{:S(2)}, u32[]{:S(2)}) async-start(bf16[64,128,128]{2,1,0:T(8,128)(2,1)} %get-tuple-element.42), calls=%async_computation.2 | async-start | bytes 4194304 | tf_op jit(solution)/shard_map/all_to_all | solution.py:476
  105.8 5.5 %collective-permute-start.1 = (bf16[400,128]{1,0:T(8,128)(2,1)S(1)}, bf16[400,128]{1,0:T(8,128)(2,1)S(1)}, u32[]{:S(2)}, u32[]{:S(2)}) collective-permute-start(bf16[400,128]{1,0:T(8,128)(2,1)S(1)} %get-tuple-element.46), channel_id=1, source_target_pairs={{0,1},{1,2},{2,3},{3,0},{4,5},{5,6},{6,7},{7,4},{8,9},{9,10},{10,1... | collective-permute-start | bytes 307208 | tf_op jit(solution)/shard_map/ppermute | solution.py:494
  107.1 7.4 %collective-permute-start.2 = (bf16[400,128]{1,0:T(8,128)(2,1)S(1)}, bf16[400,128]{1,0:T(8,128)(2,1)S(1)}, u32[]{:S(2)}, u32[]{:S(2)}) collective-permute-start(bf16[400,128]{1,0:T(8,128)(2,1)S(1)} %get-tuple-element.47), channel_id=1, source_target_pairs={{0,2},{1,3},{2,0},{3,1},{4,6},{5,7},{6,4},{7,5},{8,10},{9,11},{10,... | collective-permute-start | bytes 307208 | tf_op jit(solution)/shard_map/ppermute | solution.py:494
  115.1 5.4 %collective-permute-start.4 = (f32[112,128]{1,0:T(8,128)S(1)}, f32[112,128]{1,0:T(8,128)S(1)}, u32[]{:S(2)}, u32[]{:S(2)}) collective-permute-start(f32[112,128]{1,0:T(8,128)S(1)} %get-tuple-element.50), channel_id=1, source_target_pairs={{0,64},{4,68},{8,72},{12,76},{16,80},{20,84},{24,88},{28,92},{32,9... | collective-permute-start | bytes 172040 | tf_op jit(solution)/shard_map/ppermute | solution.py:495
  123.4 26.7 %collective-permute-start.7 = (bf16[112,128]{1,0:T(8,128)(2,1)S(1)}, bf16[112,128]{1,0:T(8,128)(2,1)S(1)}, u32[]{:S(2)}, u32[]{:S(2)}) collective-permute-start(bf16[112,128]{1,0:T(8,128)(2,1)S(1)} %shard_map.118.refs_0_), channel_id=1, source_target_pairs={{0,8},{4,12},{8,16},{12,20},{16,24},{20,28},{24,32},{28,36},{32,40... | collective-permute-start | bytes 86024 | tf_op jit(solution)/shard_map/ppermute | solution.py:495
  125.0 27.5 %collective-permute-start.8 = (bf16[112,128]{1,0:T(8,128)(2,1)S(1)}, bf16[112,128]{1,0:T(8,128)(2,1)S(1)}, u32[]{:S(2)}, u32[]{:S(2)}) collective-permute-start(bf16[112,128]{1,0:T(8,128)(2,1)S(1)} %shard_map.118.refs_0_), channel_id=1, source_target_pairs={{0,16},{4,20},{8,24},{12,28},{16,32},{20,36},{24,40},{28,44},{32,4... | collective-permute-start | bytes 86024 | tf_op jit(solution)/shard_map/ppermute | solution.py:495
  128.5 26.2 %collective-permute-start.9 = (bf16[112,128]{1,0:T(8,128)(2,1)S(1)}, bf16[112,128]{1,0:T(8,128)(2,1)S(1)}, u32[]{:S(2)}, u32[]{:S(2)}) collective-permute-start(bf16[112,128]{1,0:T(8,128)(2,1)S(1)} %shard_map.118.refs_0_), channel_id=1, source_target_pairs={{0,24},{4,28},{8,32},{12,36},{16,40},{20,44},{24,48},{28,52},{32,5... | collective-permute-start | bytes 86024 | tf_op jit(solution)/shard_map/ppermute | solution.py:495
  130.5 27.7 %collective-permute-start.10 = (bf16[112,128]{1,0:T(8,128)(2,1)S(1)}, bf16[112,128]{1,0:T(8,128)(2,1)S(1)}, u32[]{:S(2)}, u32[]{:S(2)}) collective-permute-start(bf16[112,128]{1,0:T(8,128)(2,1)S(1)} %shard_map.118.refs_0_), channel_id=1, source_target_pairs={{0,32},{4,36},{8,40},{12,44},{16,48},{20,52},{24,56},{28,60},{32,0... | collective-permute-start | bytes 86024 | tf_op jit(solution)/shard_map/ppermute | solution.py:495
  132.8 25.4 %collective-permute-start.11 = (bf16[112,128]{1,0:T(8,128)(2,1)S(1)}, bf16[112,128]{1,0:T(8,128)(2,1)S(1)}, u32[]{:S(2)}, u32[]{:S(2)}) collective-permute-start(bf16[112,128]{1,0:T(8,128)(2,1)S(1)} %shard_map.118.refs_0_), channel_id=1, source_target_pairs={{0,40},{4,44},{8,48},{12,52},{16,56},{20,60},{24,0},{28,4},{32,8},... | collective-permute-start | bytes 86024 | tf_op jit(solution)/shard_map/ppermute | solution.py:495
  150.1 8.1 %collective-permute-start.12 = (bf16[112,128]{1,0:T(8,128)(2,1)S(1)}, bf16[112,128]{1,0:T(8,128)(2,1)S(1)}, u32[]{:S(2)}, u32[]{:S(2)}) collective-permute-start(bf16[112,128]{1,0:T(8,128)(2,1)S(1)} %shard_map.118.refs_0_), channel_id=1, source_target_pairs={{0,48},{4,52},{8,56},{12,60},{16,0},{20,4},{24,8},{28,12},{32,16},... | collective-permute-start | bytes 86024 | tf_op jit(solution)/shard_map/ppermute | solution.py:495
  152.5 5.7 %collective-permute-start.13 = (bf16[112,128]{1,0:T(8,128)(2,1)S(1)}, bf16[112,128]{1,0:T(8,128)(2,1)S(1)}, u32[]{:S(2)}, u32[]{:S(2)}) collective-permute-start(bf16[112,128]{1,0:T(8,128)(2,1)S(1)} %shard_map.118.refs_0_), channel_id=1, source_target_pairs={{0,56},{4,60},{8,0},{12,4},{16,8},{20,12},{24,16},{28,20},{32,24},... | collective-permute-start | bytes 86024 | tf_op jit(solution)/shard_map/ppermute | solution.py:495
  167.6 59.0 %all-to-all-start.3 = ((bf16[64,128,128]{2,1,0:T(8,128)(2,1)}), bf16[64,128,128]{2,1,0:T(8,128)(2,1)}, u32[]{:S(2)}, u32[]{:S(2)}) async-start(bf16[64,128,128]{2,1,0:T(8,128)(2,1)} %get-tuple-element.53), calls=%async_computation.3 | async-start | bytes 4194304 | tf_op jit(solution)/shard_map/all_to_all | solution.py:476
  176.1 7.3 %collective-permute-start.14 = (f32[112,128]{1,0:T(8,128)S(1)}, f32[112,128]{1,0:T(8,128)S(1)}, u32[]{:S(2)}, u32[]{:S(2)}) collective-permute-start(f32[112,128]{1,0:T(8,128)S(1)} %shard_map.120.refs_0_), channel_id=1, source_target_pairs={{0,64},{4,68},{8,72},{12,76},{16,80},{20,84},{24,88},{28,92},{32,9... | collective-permute-start | bytes 172040 | tf_op jit(solution)/shard_map/ppermute | solution.py:495
  177.5 8.9 %collective-permute-start.15 = (f32[112,128]{1,0:T(8,128)S(1)}, f32[112,128]{1,0:T(8,128)S(1)}, u32[]{:S(2)}, u32[]{:S(2)}) collective-permute-start(f32[112,128]{1,0:T(8,128)S(1)} %shard_map.120.refs_0_), channel_id=1, source_target_pairs={{0,128},{4,132},{8,136},{12,140},{16,144},{20,148},{24,152},{28,15... | collective-permute-start | bytes 172040 | tf_op jit(solution)/shard_map/ppermute | solution.py:495
  180.1 6.3 %collective-permute-start.16 = (f32[112,128]{1,0:T(8,128)S(1)}, f32[112,128]{1,0:T(8,128)S(1)}, u32[]{:S(2)}, u32[]{:S(2)}) collective-permute-start(f32[112,128]{1,0:T(8,128)S(1)} %shard_map.120.refs_0_), channel_id=1, source_target_pairs={{0,192},{4,196},{8,200},{12,204},{16,208},{20,212},{24,216},{28,22... | collective-permute-start | bytes 172040 | tf_op jit(solution)/shard_map/ppermute | solution.py:495
  188.3 7.1 %collective-permute-start.18 = (bf16[400,128]{1,0:T(8,128)(2,1)S(1)}, bf16[400,128]{1,0:T(8,128)(2,1)S(1)}, u32[]{:S(2)}, u32[]{:S(2)}) collective-permute-start(bf16[400,128]{1,0:T(8,128)(2,1)S(1)} %shard_map.121.refs_0_), channel_id=1, source_target_pairs={{0,2},{1,3},{2,0},{3,1},{4,6},{5,7},{6,4},{7,5},{8,10},{9,11},{10,... | collective-permute-start | bytes 307208 | tf_op jit(solution)/shard_map/ppermute | solution.py:494
  236.3 45.7 %all-to-all-start.4 = ((bf16[64,80,128]{2,1,0:T(8,128)(2,1)}), bf16[64,80,128]{2,1,0:T(8,128)(2,1)S(1)}, u32[]{:S(2)}, u32[]{:S(2)}) async-start(bf16[64,80,128]{2,1,0:T(8,128)(2,1)} %get-tuple-element.55), calls=%async_computation.4 | async-start | bytes 2621440 | tf_op jit(solution)/shard_map/all_to_all | solution.py:476
  246.7 7.3 %collective-permute-start.23 = (bf16[400,128]{1,0:T(8,128)(2,1)S(1)}, bf16[400,128]{1,0:T(8,128)(2,1)S(1)}, u32[]{:S(2)}, u32[]{:S(2)}) collective-permute-start(bf16[400,128]{1,0:T(8,128)(2,1)S(1)} %get-tuple-element.61), channel_id=1, source_target_pairs={{0,2},{1,3},{2,0},{3,1},{4,6},{5,7},{6,4},{7,5},{8,10},{9,11},{10,... | collective-permute-start | bytes 307208 | tf_op jit(solution)/shard_map/ppermute | solution.py:494
  256.0 9.2 %collective-permute-start.26 = (f32[112,128]{1,0:T(8,128)S(1)}, f32[112,128]{1,0:T(8,128)S(1)}, u32[]{:S(2)}, u32[]{:S(2)}) collective-permute-start(f32[112,128]{1,0:T(8,128)S(1)} %get-tuple-element.65), channel_id=1, source_target_pairs={{0,128},{4,132},{8,136},{12,140},{16,144},{20,148},{24,152},{28,15... | collective-permute-start | bytes 172040 | tf_op jit(solution)/shard_map/ppermute | solution.py:495
  258.8 6.4 %collective-permute-start.27 = (f32[112,128]{1,0:T(8,128)S(1)}, f32[112,128]{1,0:T(8,128)S(1)}, u32[]{:S(2)}, u32[]{:S(2)}) collective-permute-start(f32[112,128]{1,0:T(8,128)S(1)} %get-tuple-element.66), channel_id=1, source_target_pairs={{0,192},{4,196},{8,200},{12,204},{16,208},{20,212},{24,216},{28,22... | collective-permute-start | bytes 172040 | tf_op jit(solution)/shard_map/ppermute | solution.py:495
  265.2 9.3 %collective-permute-start.28 = (bf16[112,128]{1,0:T(8,128)(2,1)S(1)}, bf16[112,128]{1,0:T(8,128)(2,1)S(1)}, u32[]{:S(2)}, u32[]{:S(2)}) collective-permute-start(bf16[112,128]{1,0:T(8,128)(2,1)S(1)} %shard_map.128.refs_0_), channel_id=1, source_target_pairs={{0,8},{4,12},{8,16},{12,20},{16,24},{20,28},{24,32},{28,36},{32,40... | collective-permute-start | bytes 86024 | tf_op jit(solution)/shard_map/ppermute | solution.py:495
  265.3 12.4 %collective-permute-start.29 = (bf16[112,128]{1,0:T(8,128)(2,1)S(1)}, bf16[112,128]{1,0:T(8,128)(2,1)S(1)}, u32[]{:S(2)}, u32[]{:S(2)}) collective-permute-start(bf16[112,128]{1,0:T(8,128)(2,1)S(1)} %shard_map.128.refs_0_), channel_id=1, source_target_pairs={{0,16},{4,20},{8,24},{12,28},{16,32},{20,36},{24,40},{28,44},{32,4... | collective-permute-start | bytes 86024 | tf_op jit(solution)/shard_map/ppermute | solution.py:495
  267.1 11.8 %collective-permute-start.30 = (bf16[112,128]{1,0:T(8,128)(2,1)S(1)}, bf16[112,128]{1,0:T(8,128)(2,1)S(1)}, u32[]{:S(2)}, u32[]{:S(2)}) collective-permute-start(bf16[112,128]{1,0:T(8,128)(2,1)S(1)} %shard_map.128.refs_0_), channel_id=1, source_target_pairs={{0,24},{4,28},{8,32},{12,36},{16,40},{20,44},{24,48},{28,52},{32,5... | collective-permute-start | bytes 86024 | tf_op jit(solution)/shard_map/ppermute | solution.py:495
  270.3 10.9 %collective-permute-start.31 = (bf16[112,128]{1,0:T(8,128)(2,1)S(1)}, bf16[112,128]{1,0:T(8,128)(2,1)S(1)}, u32[]{:S(2)}, u32[]{:S(2)}) collective-permute-start(bf16[112,128]{1,0:T(8,128)(2,1)S(1)} %shard_map.128.refs_0_), channel_id=1, source_target_pairs={{0,32},{4,36},{8,40},{12,44},{16,48},{20,52},{24,56},{28,60},{32,0... | collective-permute-start | bytes 86024 | tf_op jit(solution)/shard_map/ppermute | solution.py:495
  271.2 10.0 %collective-permute-start.32 = (bf16[112,128]{1,0:T(8,128)(2,1)S(1)}, bf16[112,128]{1,0:T(8,128)(2,1)S(1)}, u32[]{:S(2)}, u32[]{:S(2)}) collective-permute-start(bf16[112,128]{1,0:T(8,128)(2,1)S(1)} %shard_map.128.refs_0_), channel_id=1, source_target_pairs={{0,40},{4,44},{8,48},{12,52},{16,56},{20,60},{24,0},{28,4},{32,8},... | collective-permute-start | bytes 86024 | tf_op jit(solution)/shard_map/ppermute | solution.py:495
  274.6 6.6 %collective-permute-start.33 = (bf16[112,128]{1,0:T(8,128)(2,1)S(1)}, bf16[112,128]{1,0:T(8,128)(2,1)S(1)}, u32[]{:S(2)}, u32[]{:S(2)}) collective-permute-start(bf16[112,128]{1,0:T(8,128)(2,1)S(1)} %shard_map.128.refs_0_), channel_id=1, source_target_pairs={{0,48},{4,52},{8,56},{12,60},{16,0},{20,4},{24,8},{28,12},{32,16},... | collective-permute-start | bytes 86024 | tf_op jit(solution)/shard_map/ppermute | solution.py:495
  283.0 37.6 %all-to-all-start.5 = ((bf16[64,48,128]{2,1,0:T(8,128)(2,1)}), bf16[64,48,128]{2,1,0:T(8,128)(2,1)}, u32[]{:S(2)}, u32[]{:S(2)}) async-start(bf16[64,48,128]{2,1,0:T(8,128)(2,1)} %shard_map.130), calls=%async_computation.5 | async-start | bytes 1572864 | tf_op jit(solution)/shard_map/all_to_all | solution.py:476
  294.7 5.8 %collective-permute-start.35 = (f32[112,128]{1,0:T(8,128)S(1)}, f32[112,128]{1,0:T(8,128)S(1)}, u32[]{:S(2)}, u32[]{:S(2)}) collective-permute-start(f32[112,128]{1,0:T(8,128)S(1)} %shard_map.129.rest_0_.refs_0_), channel_id=1, source_target_pairs={{0,64},{4,68},{8,72},{12,76},{16,80},{20,84},{24,88},{28,92},{32,9... | collective-permute-start | bytes 172040 | tf_op jit(solution)/shard_map/ppermute | solution.py:495
  296.1 5.6 %collective-permute-start.36 = (f32[112,128]{1,0:T(8,128)S(1)}, f32[112,128]{1,0:T(8,128)S(1)}, u32[]{:S(2)}, u32[]{:S(2)}) collective-permute-start(f32[112,128]{1,0:T(8,128)S(1)} %shard_map.129.rest_0_.refs_0_), channel_id=1, source_target_pairs={{0,128},{4,132},{8,136},{12,140},{16,144},{20,148},{24,152},{28,15... | collective-permute-start | bytes 172040 | tf_op jit(solution)/shard_map/ppermute | solution.py:495
  303.9 6.2 %collective-permute-start.39 = (bf16[400,128]{1,0:T(8,128)(2,1)S(1)}, bf16[400,128]{1,0:T(8,128)(2,1)S(1)}, u32[]{:S(2)}, u32[]{:S(2)}) collective-permute-start(bf16[400,128]{1,0:T(8,128)(2,1)S(1)} %shard_map.132.refs_0_), channel_id=1, source_target_pairs={{0,2},{1,3},{2,0},{3,1},{4,6},{5,7},{6,4},{7,5},{8,10},{9,11},{10,... | collective-permute-start | bytes 307208 | tf_op jit(solution)/shard_map/ppermute | solution.py:494
  (26 other events, 227.2 us)
